TPU v7x, 1024 devices: a whole 4x4x32 slice. The times are simulated.
1024 devices in a mesh: grp: 128 (over x, z), dev: 8 (over y, core).
Axes of the slice: x: 4, y: 4, z: 32, core: 2. Of those that a mesh axis runs over, the one named last changes fastest.
Arguments:
- features: bfloat16 [262144, 256], P(('grp', 'dev')), may hold values from -6 to 6
- tiles: bfloat16 [8192, 128, 128], P(('grp', 'dev')), may hold values from -0.375 to 0.375
- tile_dst: int32 [8192], P(('grp', 'dev')), may hold values from 0 to 1
- tile_src: int32 [8192], P(('grp', 'dev')), may hold values from 0 to 31
- tile_count: int32 [1024], P(('grp', 'dev')), may hold values from 1 to 8, as said below
- send_rows: int32 [1024, 128, 2], P(('grp', 'dev')), may hold values from 0 to 255, as said below
- send_count: int32 [1024, 128], P(('grp', 'dev')), may hold values from 0 to 2, as said below
- weight: bfloat16 [256, 256], replicated, may hold values from -0.375 to 0.375
- cotangent: bfloat16 [262144, 256], P(('grp', 'dev')), may hold values from -6 to 6
Outputs:
- output: bfloat16 [262144, 256], P(('grp', 'dev'))
- grad_features: float32 [262144, 256], P(('grp', 'dev'))
- grad_weight: float32 [256, 256], replicated
Inputs may be any that keep to these rules, and one draw needn't show every extreme that they name: The first tile_count entries of a device's tile lists are used, the others ignored; some device has 8. `send_rows`: local row numbers of the sending device, distinct within each list of one device for one peer group. The first send_count entries of a list are live; some group receives 2 live rows from every device.
All inputs are finite; a program needn't handle non-finite values.
Results may differ from a plain program's by a relative error of at most 0.013.
Values may be sent and summed in bfloat16 or wider, within the bound.
No kernel may reach another device: no remote copies, remote signals or barrier semaphores. Data moves between devices by JAX's collectives and lax.ppermute only.
A program may use at most 32 MiB of HBM per device.

v0:
```python
import jax
import jax.numpy as jnp
from jax import lax
from jax.sharding import PartitionSpec as P


def take_slots(tiles, tile_dst, tile_src, first_slot, live_tiles):
    keep_mask = first_slot + jnp.arange(8, dtype=jnp.int32) < live_tiles
    return (tiles, tile_src, tile_dst, keep_mask)


def send_back(mine_bound, group_count, send_slots, feature_width):
    going_back = mine_bound.reshape(group_count, send_slots, feature_width).astype(jnp.bfloat16)
    return lax.all_to_all(going_back, "grp", split_axis=0, concat_axis=0, tiled=True)


def per_device(
    features, tiles, tile_dst, tile_src, tile_count, send_rows, send_count, weight, cotangent
):
    own_count, feature_width = features.shape
    tile_size = tiles.shape[1]
    send_slots = send_rows.shape[2]
    member_count = lax.axis_size("dev")
    group_count = lax.axis_size("grp")
    dest_tiles = own_count // tile_size
    bound_rows = member_count * group_count * send_slots
    group_rows = member_count * own_count
    source_total = (group_rows + bound_rows + tile_size - 1) // tile_size * tile_size
    picked = features[send_rows[0]]
    live_slots = jnp.arange(send_slots, dtype=jnp.int32)[None, :] < send_count[0][:, None]
    outgoing = jnp.where(live_slots[..., None], picked, jnp.zeros_like(picked))
    arrived = lax.all_to_all(outgoing, "grp", split_axis=0, concat_axis=0, tiled=True)
    gathered_rows, gathered_bound = (
        lax.all_gather(features, "dev", axis=0, tiled=True),
        lax.all_gather(arrived, "dev", axis=0, tiled=True),
    )
    source = jnp.concatenate(
        [
            gathered_rows,
            gathered_bound.reshape(bound_rows, feature_width),
            jnp.zeros((source_total - group_rows - bound_rows, feature_width), jnp.bfloat16),
        ],
        axis=0,
    )
    source_blocks = source.reshape(-1, tile_size, feature_width)
    live_tiles = tile_count[0]
    block_count = (live_tiles + 7) // 8
    dest_range = jnp.arange(dest_tiles, dtype=jnp.int32)

    def forward_block(block_index, running):
        tile_block, source_ids, dest_ids, keep_mask = take_slots(
            tiles, tile_dst, tile_src, block_index * 8, live_tiles
        )
        products = jnp.einsum(
            "kij,kjf->kif",
            tile_block,
            source_blocks[source_ids],
            preferred_element_type=jnp.float32,
        )
        selector = (dest_ids[None, :] == dest_range[:, None]) & keep_mask[None, :]
        return running + jnp.sum(
            jnp.where(selector[:, :, None, None], products[None], jnp.float32(0.0)), axis=1
        )

    summed = lax.fori_loop(
        0,
        block_count,
        forward_block,
        jnp.zeros((dest_tiles, tile_size, feature_width), jnp.float32),
    )
    aggregated = summed.reshape(own_count, feature_width).astype(jnp.bfloat16)
    output = jnp.dot(aggregated, weight, preferred_element_type=jnp.float32).astype(jnp.bfloat16)
    weight_terms = lax.dot_general(
        aggregated, cotangent, (((0,), (0,)), ((), ())), preferred_element_type=jnp.float32
    )
    grad_weight = lax.psum(weight_terms, ("grp", "dev"))
    upstream = lax.dot_general(
        cotangent, weight, (((1,), (1,)), ((), ())), preferred_element_type=jnp.float32
    ).astype(jnp.bfloat16)
    up_blocks = upstream.reshape(dest_tiles, tile_size, feature_width)

    def backward_block(block_index, running):
        tile_block, source_ids, dest_ids, keep_mask = take_slots(
            tiles, tile_dst, tile_src, block_index * 8, live_tiles
        )
        contrib = jnp.einsum(
            "kji,kjf->kif", tile_block, up_blocks[dest_ids], preferred_element_type=jnp.float32
        )
        contrib = jnp.where(keep_mask[:, None, None], contrib, jnp.float32(0.0))
        return running.at[source_ids].add(contrib)

    partial_terms = lax.fori_loop(
        0,
        block_count,
        backward_block,
        jnp.zeros((source_total // tile_size, tile_size, feature_width), jnp.float32),
    )
    partial_terms = (
        partial_terms.reshape(source_total, feature_width).astype(jnp.bfloat16).astype(jnp.float32)
    )
    local_terms = partial_terms[:group_rows]
    bound_terms = partial_terms[group_rows : group_rows + bound_rows]
    mine_local, mine_bound = (
        lax.psum_scatter(
            local_terms.astype(jnp.bfloat16), "dev", scatter_dimension=0, tiled=True
        ).astype(jnp.float32),
        lax.psum_scatter(
            bound_terms.astype(jnp.bfloat16), "dev", scatter_dimension=0, tiled=True
        ).astype(jnp.float32),
    )
    came_back = send_back(mine_bound, group_count, send_slots, feature_width)
    values = jnp.where(live_slots[..., None], came_back.astype(jnp.float32), jnp.float32(0.0))
    added = (
        jnp.zeros((own_count, feature_width), jnp.float32)
        .at[send_rows[0].reshape(-1)]
        .add(values.reshape(-1, feature_width))
    )
    grad_features = mine_local + added
    return (output, grad_features, grad_weight)


def solution(mesh):
    placed = (
        P(("grp", "dev"), None),
        P(("grp", "dev"), None, None),
        P(("grp", "dev")),
        P(("grp", "dev")),
        P(("grp", "dev")),
        P(("grp", "dev"), None, None),
        P(("grp", "dev"), None),
        P(),
        P(("grp", "dev"), None),
    )
    return jax.shard_map(
        per_device,
        mesh=mesh,
        in_specs=placed,
        out_specs=(P(("grp", "dev"), None), P(("grp", "dev"), None), P()),
        check_vma=False,
    )
```

profile of v0, /device:TPU:1, one launch (start us, length us, event | category | flops | bytes accessed | tf_op | source)
XLA Modules:
  0.0 1102.1 jit_solution(3557415600545316867)
XLA Ops:
  8.1 1.1 convolution_convert_fusion
  9.2 2.4 broadcast_in_dim.84
  11.7 5.3 while.23
  13.6 3.3 scatter_fusion
  17.0 2.5 convert_element_type.41
  19.5 1.4 fusion.5
  21.0 0.7 reduce-scatter.3.cloned.1.call-update
  22.0 1.2 gather_fusion.1
  23.6 63.9 %all_to_all.10 = bf16[128,2,256]{2,1,0:T(2,128)(2,1)} all-to-all(bf16[128,2,256]{2,1,0:T(2,128)(2,1)S(1)} %broadcast_select_fusion), channel_id=1, replica_groups=mesh['grp'=128,'dev'=8] {'grp'}, dimensions={0} | all-to-all | bytes 262144 | tf_op jit(solution)/shard_map/all_to_all | solution.py:32
  88.4 1.6 convert_element_type.45
  90.1 15.6 %all-to-all-start.1 = ((bf16[128,2,256]{2,1,0:T(2,128)(2,1)}), bf16[128,2,256]{2,1,0:T(2,128)(2,1)S(1)}, u32[]{:S(2)}, u32[]{:S(2)}) async-start(bf16[128,2,256]{2,1,0:T(2,128)(2,1)} %convert_element_type.45), calls=%async_computation.3 | async-start | bytes 262144 | tf_op jit(solution)/shard_map/all_to_all | solution.py:14
  105.7 26.6 %reduce-scatter.3.cloned.1.call-done = bf16[256,256]{1,0:T(8,128)(2,1)} async-done(((bf16[2048,256]{1,0:T(8,128)(2,1)}), bf16[256,256]{1,0:T(8,128)(2,1)}) %reduce-scatter.3.cloned.1.call-update) | async-done | bytes 131088 | tf_op jit(solution)/shard_map/reduce_scatter | solution.py:104
  132.3 0.9 convert_element_type.43
  133.2 42.7 %all-gather.5.cloned.1.call-done = bf16[1024,2,256]{2,1,0:T(2,128)(2,1)} async-done(((bf16[128,2,256]{2,1,0:T(2,128)(2,1)}), bf16[1024,2,256]{2,1,0:T(2,128)(2,1)}) %all-gather.5.cloned.1.call-update) | async-done | bytes 1048592 | tf_op jit(solution)/shard_map/all_gather | solution.py:35
  175.9 1.5 reshape.197
  177.4 42.5 %all-gather.3.cloned.1.call-done = bf16[2048,256]{1,0:T(8,128)(2,1)} async-done(((bf16[256,256]{1,0:T(8,128)(2,1)}), bf16[2048,256]{1,0:T(8,128)(2,1)}) %all-gather.3.cloned.1.call-update) | async-done | bytes 1048592 | tf_op jit(solution)/shard_map/all_gather | solution.py:34
  219.9 2.7 pad_maximum_fusion
  222.6 2.2 gather_fusion.2
  225.1 1.0 while.24
  226.1 0.9 fusion.6
  227.1 0.8 convolution_convert_fusion.1
  228.3 2.1 scatter_fusion.1
  230.4 863.4 %all-reduce.2.cloned.1.call-done = f32[256,256]{1,0:T(8,128)} async-done(((f32[256,256]{1,0:T(8,128)}), f32[256,256]{1,0:T(8,128)}) %all-reduce.2.cloned.1.call-update) | async-done | bytes 262160 | tf_op jit(solution)/shard_map/psum | solution.py:76
  1093.9 1.7 copy.55
  (56 shorter events, 5.4 us)
Async XLA Ops:
  7.2 0.9 copy-start
  7.2 4.5 copy-start.3
  7.2 4.5 copy-start.6
  7.2 4.4 copy-start.5
  7.2 81.2 %reduce-scatter.5.cloned.1.call-start = ((), (), s32[]{:S(2)}) async-start(), calls=%async_computation.7 | async-start | bytes 1179648 | tf_op jit(solution)/shard_map/reduce_scatter | solution.py:107
  19.4 2.3 copy-start.7
  19.5 2.6 copy-start.2
  19.5 3.8 copy-start.8
  20.9 111.3 %reduce-scatter.3.cloned.1.call-start = ((), (), s32[]{:S(2)}) async-start(), calls=%async_computation.6 | async-start | bytes 1179648 | tf_op jit(solution)/shard_map/reduce_scatter | solution.py:104
  21.7 154.2 %all-gather.5.cloned.1.call-start = ((), (), s32[]{:S(2)}) async-start(), calls=%async_computation.5 | async-start | bytes 1179648 | tf_op jit(solution)/shard_map/all_gather | solution.py:35
  87.5 132.3 %all-gather.3.cloned.1.call-start = ((), (), s32[]{:S(2)}) async-start(), calls=%async_computation.4 | async-start | bytes 1179648 | tf_op jit(solution)/shard_map/all_gather | solution.py:34
  90.1 137.9 %all-to-all-start.1 = ((bf16[128,2,256]{2,1,0:T(2,128)(2,1)}), bf16[128,2,256]{2,1,0:T(2,128)(2,1)S(1)}, u32[]{:S(2)}, u32[]{:S(2)}) async-start(bf16[128,2,256]{2,1,0:T(2,128)(2,1)} %convert_element_type.45), calls=%async_computation.3 | async-start | bytes 262144 | tf_op jit(solution)/shard_map/all_to_all | solution.py:14
  105.6 988.2 %all-reduce.2.cloned.1.call-start = ((), (), s32[]{:S(2)}) async-start(), calls=%async_computation.8 | async-start | bytes 524288 | tf_op jit(solution)/shard_map/psum | solution.py:76
  225.1 2.0 copy-start.4
  230.4 865.1 %copy-start.1 = (f32[256,256]{1,0:T(8,128)}, f32[256,256]{1,0:T(8,128)S(1)}, u32[]{:S(2)}) copy-start(f32[256,256]{1,0:T(8,128)S(1)} %scatter_fusion.1) | copy-start | bytes 786436
Sparse Core Ops, SparseCore 0:
  21.1 58.3 reduce-scatter.4
  82.9 49.3 reduce-scatter.2
  135.0 40.8 all-gather.4
  178.5 41.3 all-gather.2
  227.2 866.6 all-reduce.1
where the time goes:
time: 1100 us
  waiting for transfers between devices  977 us (89%)
  blocking collectives  63.9 us (6%)
  starting transfers between devices  15.8 us (1%)
  between operations  14.8 us (1%)
  local copies, waits for them, and re-layouts  13.8 us (1%)
  other arithmetic  13.7 us (1%)
    psum x1, waiting for transfers between devices, per_device(): grad_weight = lax.psum(weight_terms, ('grp', 'dev'))  863 us
    all_to_all x1, blocking collectives, per_device(): lax.all_to_all(outgoing, 'grp', split_axis=0, concat_axis=0, tiled=True)  63.9 us
    all_gather x1, waiting for transfers between devices, per_device(): lax.all_gather(arrived, 'dev', axis=0, tiled=True)  42.7 us
    all_gather x1, waiting for transfers between devices, per_device(): lax.all_gather(features, 'dev', axis=0, tiled=True)  42.5 us
    reduce_scatter x1, waiting for transfers between devices, per_device(): lax.psum_scatter(local_terms.astype(jnp.bfloat16), 'dev', scatter_dimensi...  26.6 us
  transfers between devices with their start and end apart: 6, of which 4 were waited for; matrix products, arithmetic and copies ran while one was open for 1% of the time, Pallas kernels for 0%

commit v1 on v0

v1 whole, which is shorter than its diff:
```python
import jax
import jax.numpy as jnp
from jax import lax
from jax.experimental import pallas as pl
from jax.experimental.pallas import tpu as pltpu
from jax.sharding import Mesh, PartitionSpec as P

AXES = ("x", "zh", "zl", "y", "core")
SIZES = (4, 16, 2, 4, 2)
GRP = ("x", "zh", "zl")
DEV = ("y", "core")
NEAR = ("x", "zl", "y", "core")
FAR = "zh"
MEMBERS = 8
NEAR_SIZE = 64
FAR_SIZE = 16
TILE = 128
NT = 8

F32 = jnp.float32
BF16 = jnp.bfloat16
SMEM = pl.BlockSpec(memory_space=pltpu.SMEM)
VMEM = pl.BlockSpec(memory_space=pltpu.VMEM)


def swap(x, axes):
    return lax.all_to_all(x, axes, split_axis=0, concat_axis=0, tiled=True)


def dot(a, b, da=1, db=0):
    return lax.dot_general(a, b, (((da,), (db,)), ((), ())), preferred_element_type=F32)


def halves(x):
    high = x.astype(BF16)
    return high, (x - high.astype(F32)).astype(BF16)


def params():
    return pltpu.CompilerParams(vmem_limit_bytes=24 * 1024 * 1024)


def one_hot(idx_ref, rows):
    slots = idx_ref.shape[1]
    places = lax.broadcasted_iota(jnp.int32, (rows, slots), 0)
    return (places == idx_ref[...]).astype(F32).astype(BF16)


def pick_kernel(idx_ref, features_ref, out_ref):
    picks = one_hot(idx_ref, features_ref.shape[0])
    out_ref[...] = dot(picks, features_ref[...], 0, 0).astype(BF16)


def terms_kernel(count_ref, src_ref, dst_ref, tiles_ref, cot_ref, out_ref, acc_ref):
    live = count_ref[0]
    out_ref[...] = jnp.zeros(out_ref.shape, BF16)
    for k in range(NT):
        @pl.when(k < live)
        def _():
            acc_ref[src_ref[k]] = jnp.zeros(acc_ref.shape[1:], F32)
    for k in range(NT):
        @pl.when(k < live)
        def _():
            acc_ref[src_ref[k]] += dot(tiles_ref[k], cot_ref[dst_ref[k]], 0, 0)
    for k in range(NT):
        @pl.when(k < live)
        def _():
            block = src_ref[k]
            member = (block % 16) // 2
            part = block % 2 + 2 * (block // 16)
            out_ref[member, part] = acc_ref[block].astype(BF16)


def mid_kernel(terms_ref, features_ref, arrived_ref, own_ref, bound_ref, gw_ref):
    own = terms_ref[0, 0].astype(F32)
    bound = terms_ref[0, 1].astype(F32)
    for m in range(1, MEMBERS):
        own += terms_ref[m, 0].astype(F32)
        bound += terms_ref[m, 1].astype(F32)
    own_ref[...] = own
    bound_ref[...] = bound.astype(BF16)
    own_high, own_low = halves(own)
    bound_high, bound_low = halves(bound)
    features = features_ref[...]
    arrived = arrived_ref[...]
    gw_ref[...] = (dot(features, own_high, 0, 0) + dot(features, own_low, 0, 0)
                   + dot(arrived, bound_high, 0, 0) + dot(arrived, bound_low, 0, 0))


def forward_kernel(count_ref, src_ref, dst_ref, tiles_ref, own_ref, bound_ref, weight_ref, out_ref, acc_ref):
    live = count_ref[0]
    acc_ref[...] = jnp.zeros(acc_ref.shape, F32)
    for k in range(NT):
        block = src_ref[k]

        @pl.when((k < live) & (block < 16))
        def _():
            acc_ref[dst_ref[k]] += dot(tiles_ref[k], own_ref[block])

        @pl.when((k < live) & (block >= 16))
        def _():
            acc_ref[dst_ref[k]] += dot(tiles_ref[k], bound_ref[block - 16])
    for t in range(2):
        out_ref[t] = dot(acc_ref[t].astype(BF16), weight_ref[...]).astype(BF16)


def back_kernel(idx_ref, own_ref, back_ref, weight_ref, out_ref):
    picks = one_hot(idx_ref, own_ref.shape[0])
    total = own_ref[...] + dot(picks, back_ref[...])
    high, low = halves(total)
    weight = weight_ref[...]
    out_ref[...] = dot(high, weight, 1, 1) + dot(low, weight, 1, 1)


def per_device(
    features, tiles, tile_dst, tile_src, tile_count, send_rows, send_count, weight, cotangent
):
    rows, width = features.shape
    groups, slots = send_rows.shape[1:]
    shape = jax.ShapeDtypeStruct
    live = jnp.arange(slots, dtype=jnp.int32)[None, :] < send_count[0][:, None]
    idx = jnp.where(live, send_rows[0], -1).reshape(1, groups * slots)

    outgoing = pl.pallas_call(
        pick_kernel, out_shape=shape((groups * slots, width), BF16),
        in_specs=[VMEM, VMEM], out_specs=VMEM, compiler_params=params(), name="pick",
    )(idx, features)
    arrived = swap(outgoing.reshape(groups, slots, width), GRP).reshape(groups * slots, width)

    terms = pl.pallas_call(
        terms_kernel, out_shape=shape((MEMBERS, 4, TILE, width), BF16),
        in_specs=[SMEM, SMEM, SMEM, VMEM, VMEM], out_specs=VMEM,
        scratch_shapes=[pltpu.VMEM((32, TILE, width), F32)],
        compiler_params=params(), name="terms",
    )(tile_count, tile_src, tile_dst, tiles, cotangent.reshape(2, TILE, width))
    terms = swap(terms, DEV).reshape(MEMBERS, 2, rows, width)

    own, bound, gw = pl.pallas_call(
        mid_kernel,
        out_shape=(shape((rows, width), F32), shape((rows, width), BF16), shape((width, width), F32)),
        in_specs=[VMEM] * 3, out_specs=(VMEM,) * 3, compiler_params=params(), name="mid",
    )(terms, features, arrived)

    near = swap(gw.reshape(NEAR_SIZE, width // NEAR_SIZE, width), NEAR).sum(axis=0)
    far = swap(jnp.broadcast_to(near[None], (FAR_SIZE,) + near.shape), FAR).sum(axis=0)
    grad_weight = swap(jnp.broadcast_to(far[None], (NEAR_SIZE,) + far.shape), NEAR).reshape(width, width)

    back = swap(bound.reshape(groups, slots, width), GRP).reshape(groups * slots, width)
    grad_features = pl.pallas_call(
        back_kernel, out_shape=shape((rows, width), F32),
        in_specs=[VMEM] * 4, out_specs=VMEM, compiler_params=params(), name="back",
    )(idx, own, back, weight)

    all_own = lax.all_gather(features, DEV, axis=0, tiled=True)
    all_bound = lax.all_gather(arrived, DEV, axis=0, tiled=True)
    output = pl.pallas_call(
        forward_kernel, out_shape=shape((2, TILE, width), BF16),
        in_specs=[SMEM, SMEM, SMEM, VMEM, VMEM, VMEM, VMEM], out_specs=VMEM,
        scratch_shapes=[pltpu.VMEM((2, TILE, width), F32)],
        compiler_params=params(), name="forward",
    )(tile_count, tile_src, tile_dst, tiles, all_own.reshape(16, TILE, width),
      all_bound.reshape(16, TILE, width), weight).reshape(rows, width)
    return output, grad_features, grad_weight


def solution(mesh):
    fine = Mesh(mesh.devices.reshape(SIZES), AXES)
    placed = (
        P(AXES, None),
        P(AXES, None, None),
        P(AXES),
        P(AXES),
        P(AXES),
        P(AXES, None, None),
        P(AXES, None),
        P(),
        P(AXES, None),
    )
    return jax.shard_map(
        per_device,
        mesh=fine,
        in_specs=placed,
        out_specs=(P(AXES, None), P(AXES, None), P()),
        check_vma=False,
    )
```

time: 1100 us -> 240 us (0.22)
  waiting for transfers between devices: 977 us -> 137 us
  blocking collectives: 63.9 us -> 0 us
  starting transfers between devices: 15.8 us -> 66.5 us
  other arithmetic: 13.7 us -> 0.87 us
    psum x1 -> x0, waiting for transfers between devices: 863 us -> none  [per_device(): grad_weight = lax.psum(weight_terms, ('grp', 'dev'))]
    all_to_all x1 -> x6, waiting for transfers between devices: 0.01 us -> 109 us  [swap(): return lax.all_to_all(x, axes, split_axis=0, concat_axis=0, tiled=True)]
    all_to_all x1 -> x0, blocking collectives: 63.9 us -> none  [per_device(): lax.all_to_all(outgoing, 'grp', split_axis=0, concat_axis=0, tiled=True)]
    all_gather x2, waiting for transfers between devices: 85.2 us -> 26.1 us  [the longest x1 26.1 us: per_device(): all_bound = lax.all_gather(arrived, DEV, axis=0, tiled=True)]
    all_to_all x1 -> x6, starting transfers between devices: 15.6 us -> 66.4 us  [swap(): return lax.all_to_all(x, axes, split_axis=0, concat_axis=0, tiled=True)]
    reduce_scatter x2 -> x0, waiting for transfers between devices: 26.6 us -> none  [the longest x1 26.6 us: per_device(): lax.psum_scatter(local_terms.astype(jnp.bfloat16), 'dev', scatter_dimensi...]
  transfers between devices with their start and end apart: 6 -> 8, of which waited for: 4 -> 6; matrix products, arithmetic and copies ran while one was open for 1% -> 1% of each run, Pallas kernels for 0% -> 3%
where the time goes in v1:
time: 240 us; the launch traced here: 239 us
  waiting for transfers between devices  137 us (57%)
  starting transfers between devices  66.5 us (28%)
  between operations  14.9 us (6%)
  local copies, waits for them, and re-layouts  13.4 us (6%)
  Pallas kernels  7.06 us (3%)
    all_to_all x6, waiting for transfers between devices, swap(): return lax.all_to_all(x, axes, split_axis=0, concat_axis=0, tiled=True)  109 us
    all_to_all x6, starting transfers between devices, swap(): return lax.all_to_all(x, axes, split_axis=0, concat_axis=0, tiled=True)  66.4 us
    all_gather x1, waiting for transfers between devices, per_device(): all_bound = lax.all_gather(arrived, DEV, axis=0, tiled=True)  26.1 us
    unnamed x29, local copies, waits for them, and re-layouts  8.65 us
  transfers between devices with their start and end apart: 8, of which 6 were waited for; matrix products, arithmetic and copies ran while one was open for 1% of the time, Pallas kernels for 3%

profile of v1, /device:TPU:1, one launch (start us, length us, event | category | flops | bytes accessed | tf_op | source)
XLA Modules:
  0.0 239.3 jit_solution(18223145170671853672)
XLA Ops:
  7.2 0.8 copy.15
  9.0 0.9 copy-done.1
  10.9 33.6 %all-to-all-start = ((bf16[128,2,256]{2,1,0:T(2,128)(2,1)}), bf16[128,2,256]{2,1,0:T(2,128)(2,1)S(1)}, u32[]{:S(2)}, u32[]{:S(2)}) async-start(bf16[128,2,256]{2,1,0:T(2,128)(2,1)} %reshape.76), calls=%async_computation | async-start | bytes 262144 | tf_op jit(solution)/shard_map/all_to_all | solution.py:27
  45.1 0.9 copy-done.6
  46.0 0.9 copy-done.9
  48.3 2.5 %terms.1 = bf16[8,4,128,256]{3,2,1,0:T(8,128)(2,1)S(1)} custom-call(s32[1]{0:T(128)S(6)} %copy.18.count_ref, s32[8]{0:T(128)S(1)} %copy-done.10, s32[8]{0:T(128)S(1)} %copy-done.12, bf16[8,128,128]{2,1,0:T(8,128)(2,1)S(1)} %copy-done.6, bf16[2,128,256]{2,1,0:T(8,128)(2,1)S(1)} %bitcast.9), custom_call_target="tpu_custom_call" | custom-call | tf_op jit(solution)/shard_map/terms/pallas_call | solution.py:130
  50.8 1.3 copy-done
  52.1 22.5 %all-to-all-done = bf16[128,2,256]{2,1,0:T(2,128)(2,1)S(1)} async-done(((bf16[128,2,256]{2,1,0:T(2,128)(2,1)}), bf16[128,2,256]{2,1,0:T(2,128)(2,1)S(1)}, u32[]{:S(2)}, u32[]{:S(2)}) %all-to-all-start) | async-done | bytes 131104 | tf_op jit(solution)/shard_map/all_to_all | solution.py:27
  74.7 7.7 %all-to-all-start.1 = ((bf16[8,4,128,256]{3,2,1,0:T(8,128)(2,1)}), bf16[8,4,128,256]{3,2,1,0:T(8,128)(2,1)S(1)}, u32[]{:S(2)}, u32[]{:S(2)}) async-start(bf16[8,4,128,256]{3,2,1,0:T(8,128)(2,1)} %copy-done), calls=%async_computation.1 | async-start | bytes 4194304 | tf_op jit(solution)/shard_map/all_to_all | solution.py:27
  82.4 26.3 %all-to-all-done.1 = bf16[8,4,128,256]{3,2,1,0:T(8,128)(2,1)S(1)} async-done(((bf16[8,4,128,256]{3,2,1,0:T(8,128)(2,1)}), bf16[8,4,128,256]{3,2,1,0:T(8,128)(2,1)S(1)}, u32[]{:S(2)}, u32[]{:S(2)}) %all-to-all-start.1) | async-done | bytes 2097184 | tf_op jit(solution)/shard_map/all_to_all | solution.py:27
  109.3 0.8 reshape.84
  110.1 5.2 %all-to-all-start.3 = ((f32[64,4,256]{2,1,0:T(4,128)}), f32[64,4,256]{2,1,0:T(4,128)S(1)}, u32[]{:S(2)}, u32[]{:S(2)}) async-start(f32[64,4,256]{2,1,0:T(4,128)} %reshape.84), calls=%async_computation.3 | async-start | bytes 524288 | tf_op jit(solution)/shard_map/all_to_all | solution.py:27
  116.0 9.1 %all-to-all-done.3 = f32[64,4,256]{2,1,0:T(4,128)S(1)} async-done(((f32[64,4,256]{2,1,0:T(4,128)}), f32[64,4,256]{2,1,0:T(4,128)S(1)}, u32[]{:S(2)}, u32[]{:S(2)}) %all-to-all-start.3) | async-done | bytes 262176 | tf_op jit(solution)/shard_map/all_to_all | solution.py:27
  125.8 3.5 %all-to-all-start.4 = ((f32[16,4,256]{2,1,0:T(4,128)}), f32[16,4,256]{2,1,0:T(4,128)S(1)}, u32[]{:S(2)}, u32[]{:S(2)}) async-start(f32[16,4,256]{2,1,0:T(4,128)} %broadcast_in_dim.9), calls=%async_computation.4 | async-start | bytes 131072 | tf_op jit(solution)/shard_map/all_to_all | solution.py:27
  130.1 20.7 %all-to-all-done.4 = f32[16,4,256]{2,1,0:T(4,128)S(1)} async-done(((f32[16,4,256]{2,1,0:T(4,128)}), f32[16,4,256]{2,1,0:T(4,128)S(1)}, u32[]{:S(2)}, u32[]{:S(2)}) %all-to-all-start.4) | async-done | bytes 65568 | tf_op jit(solution)/shard_map/all_to_all | solution.py:27
  150.8 9.3 %all-to-all-start.2 = ((bf16[128,2,256]{2,1,0:T(2,128)(2,1)}), bf16[128,2,256]{2,1,0:T(2,128)(2,1)S(1)}, u32[]{:S(2)}, u32[]{:S(2)}) async-start(bf16[128,2,256]{2,1,0:T(2,128)(2,1)} %reshape.82), calls=%async_computation.2 | async-start | bytes 262144 | tf_op jit(solution)/shard_map/all_to_all | solution.py:27
  160.1 30.6 %all-to-all-done.2 = bf16[128,2,256]{2,1,0:T(2,128)(2,1)S(1)} async-done(((bf16[128,2,256]{2,1,0:T(2,128)(2,1)}), bf16[128,2,256]{2,1,0:T(2,128)(2,1)S(1)}, u32[]{:S(2)}, u32[]{:S(2)}) %all-to-all-start.2) | async-done | bytes 131104 | tf_op jit(solution)/shard_map/all_to_all | solution.py:27
  191.4 7.1 %all-to-all-start.5 = ((f32[64,4,256]{2,1,0:T(4,128)}), f32[64,4,256]{2,1,0:T(4,128)S(1)}, u32[]{:S(2)}, u32[]{:S(2)}) async-start(f32[64,4,256]{2,1,0:T(4,128)} %broadcast_in_dim.10), calls=%async_computation.5 | async-start | bytes 524288 | tf_op jit(solution)/shard_map/all_to_all | solution.py:27
  199.4 1.1 back.1
  200.4 26.1 %all-gather.5.cloned.1.call-done = bf16[2048,256]{1,0:T(8,128)(2,1)} async-done(((bf16[256,256]{1,0:T(8,128)(2,1)}), bf16[2048,256]{1,0:T(8,128)(2,1)}) %all-gather.5.cloned.1.call-update) | async-done | bytes 1048592 | tf_op jit(solution)/shard_map/all_gather | solution.py:155
  226.6 1.2 copy-done.4
  227.8 1.2 copy-done.5
  229.0 2.6 %forward.1 = bf16[2,128,256]{2,1,0:T(8,128)(2,1)} custom-call(s32[1]{0:T(128)S(6)} %copy.18.count_ref, s32[8]{0:T(128)S(1)} %copy-done.11, s32[8]{0:T(128)S(1)} %copy-done.13, bf16[8,128,128]{2,1,0:T(8,128)(2,1)S(1)} %copy-done.7, bf16[16,128,256]{2,1,0:T(8,128)(2,1)S(1)} %bitcast.7, bf16[16,128,256]{2,1,0:T(8,128)(2,1)S(1)} %bitcast.8, ...), custom_call_target="tpu_custom_call" | custom-call | tf_op jit(solution)/shard_map/forward/pallas_call | solution.py:156
  231.7 0.8 reshape.85
  (42 shorter events, 7.7 us)
Async XLA Ops:
  9.0 0.9 copy-start.1
  10.9 63.8 %all-to-all-start = ((bf16[128,2,256]{2,1,0:T(2,128)(2,1)}), bf16[128,2,256]{2,1,0:T(2,128)(2,1)S(1)}, u32[]{:S(2)}, u32[]{:S(2)}) async-start(bf16[128,2,256]{2,1,0:T(2,128)(2,1)} %reshape.76), calls=%async_computation | async-start | bytes 262144 | tf_op jit(solution)/shard_map/all_to_all | solution.py:27
  45.1 1.0 copy-start.6
  46.0 0.9 copy-start.9
  46.9 0.7 copy-start.10
  47.6 0.7 copy-start.12
  50.8 1.3 copy-start
  52.1 56.6 %copy-start.2 = (bf16[256,256]{1,0:T(8,128)(2,1)S(1)}, bf16[256,256]{1,0:T(8,128)(2,1)}, u32[]{:S(2)}) copy-start(bf16[256,256]{1,0:T(8,128)(2,1)} %features_ref.3) | copy-start | bytes 393220
  74.7 34.0 %all-to-all-start.1 = ((bf16[8,4,128,256]{3,2,1,0:T(8,128)(2,1)}), bf16[8,4,128,256]{3,2,1,0:T(8,128)(2,1)S(1)}, u32[]{:S(2)}, u32[]{:S(2)}) async-start(bf16[8,4,128,256]{3,2,1,0:T(8,128)(2,1)} %copy-done), calls=%async_computation.1 | async-start | bytes 4194304 | tf_op jit(solution)/shard_map/all_to_all | solution.py:27
  82.4 47.7 %copy-start.3 = (bf16[256,256]{1,0:T(8,128)(2,1)}, bf16[256,256]{1,0:T(8,128)(2,1)S(1)}, u32[]{:S(2)}) copy-start(bf16[256,256]{1,0:T(8,128)(2,1)S(1)} %reshape.77.arrived_ref) | copy-start | bytes 393220
  109.3 90.1 %copy-start.8 = (bf16[256,256]{1,0:T(8,128)(2,1)S(1)}, bf16[256,256]{1,0:T(8,128)(2,1)}, u32[]{:S(2)}) copy-start(bf16[256,256]{1,0:T(8,128)(2,1)} %weight_ref.3) | copy-start | bytes 393220
  109.3 117.3 %copy-start.7 = (bf16[8,128,128]{2,1,0:T(8,128)(2,1)S(1)}, bf16[8,128,128]{2,1,0:T(8,128)(2,1)}, u32[]{:S(2)}) copy-start(bf16[8,128,128]{2,1,0:T(8,128)(2,1)} %tiles_ref.3) | copy-start | bytes 786436
  109.3 117.3 %copy-start.11 = (s32[8]{0:T(128)S(1)}, s32[8]{0:T(128)}, u32[]{:S(2)}) copy-start(s32[8]{0:T(128)} %src_ref.3) | copy-start | bytes 100
  109.3 117.2 %copy-start.13 = (s32[8]{0:T(128)S(1)}, s32[8]{0:T(128)}, u32[]{:S(2)}) copy-start(s32[8]{0:T(128)} %dst_ref.3) | copy-start | bytes 100
  110.1 15.0 %all-to-all-start.3 = ((f32[64,4,256]{2,1,0:T(4,128)}), f32[64,4,256]{2,1,0:T(4,128)S(1)}, u32[]{:S(2)}, u32[]{:S(2)}) async-start(f32[64,4,256]{2,1,0:T(4,128)} %reshape.84), calls=%async_computation.3 | async-start | bytes 524288 | tf_op jit(solution)/shard_map/all_to_all | solution.py:27
  115.3 85.1 %all-gather.3.cloned.1.call-start = ((), (), s32[]{:S(2)}) async-start(), calls=%async_computation.6 | async-start | bytes 1179648 | tf_op jit(solution)/shard_map/all_gather | solution.py:154
  125.8 24.9 %all-to-all-start.4 = ((f32[16,4,256]{2,1,0:T(4,128)}), f32[16,4,256]{2,1,0:T(4,128)S(1)}, u32[]{:S(2)}, u32[]{:S(2)}) async-start(f32[16,4,256]{2,1,0:T(4,128)} %broadcast_in_dim.9), calls=%async_computation.4 | async-start | bytes 131072 | tf_op jit(solution)/shard_map/all_to_all | solution.py:27
  150.8 39.9 %all-to-all-start.2 = ((bf16[128,2,256]{2,1,0:T(2,128)(2,1)}), bf16[128,2,256]{2,1,0:T(2,128)(2,1)S(1)}, u32[]{:S(2)}, u32[]{:S(2)}) async-start(bf16[128,2,256]{2,1,0:T(2,128)(2,1)} %reshape.82), calls=%async_computation.2 | async-start | bytes 262144 | tf_op jit(solution)/shard_map/all_to_all | solution.py:27
  191.4 40.3 %all-to-all-start.5 = ((f32[64,4,256]{2,1,0:T(4,128)}), f32[64,4,256]{2,1,0:T(4,128)S(1)}, u32[]{:S(2)}, u32[]{:S(2)}) async-start(f32[64,4,256]{2,1,0:T(4,128)} %broadcast_in_dim.10), calls=%async_computation.5 | async-start | bytes 524288 | tf_op jit(solution)/shard_map/all_to_all | solution.py:27
  198.5 28.0 %all-gather.5.cloned.1.call-start = ((), (), s32[]{:S(2)}) async-start(), calls=%async_computation.7 | async-start | bytes 1179648 | tf_op jit(solution)/shard_map/all_gather | solution.py:155
  226.6 1.2 copy-start.4
  227.8 1.2 copy-start.5
Sparse Core Ops, SparseCore 0:
  118.9 23.7 all-gather.2
  202.7 23.8 all-gather.4

commit v2 on v1

v2 whole, which is shorter than its diff:
```python
import jax
import jax.numpy as jnp
from jax import lax
from jax.experimental import pallas as pl
from jax.experimental.pallas import tpu as pltpu
from jax.sharding import Mesh, PartitionSpec as P

AXES = ("x", "zh", "zl", "y", "core")
SIZES = (4, 16, 2, 4, 2)
SLOTS = 2
X, ZH, ZL, Y, CORE = SIZES
GRP = ("x", "zh", "zl")
DEV = ("y", "core")
SIDE = ("x", "zl")
NEAR = ("x", "zl", "y", "core")
FAR = "zh"
TILE = 128
NT = 8
CHUNKS = 64

F32 = jnp.float32
BF16 = jnp.bfloat16
SMEM = pl.BlockSpec(memory_space=pltpu.SMEM)
ANY = pl.BlockSpec(memory_space=pl.ANY)
VMEM = pl.BlockSpec(memory_space=pltpu.VMEM)


def swap(x, axes):
    return lax.all_to_all(x, axes, split_axis=0, concat_axis=0, tiled=True)


def shift(x, axis, step, size):
    return lax.ppermute(x, axis, [(i, (i + step) % size) for i in range(size)])


def dot(a, b, da=1, db=0):
    return lax.dot_general(a, b, (((da,), (db,)), ((), ())), preferred_element_type=F32)


def halves(x):
    high = x.astype(BF16)
    return high, (x - high.astype(F32)).astype(BF16)


def call(kernel, out_shape, in_specs, name, scratch=()):
    out_specs = (VMEM,) * len(out_shape) if isinstance(out_shape, tuple) else VMEM
    return pl.pallas_call(
        kernel, out_shape=out_shape, in_specs=in_specs, out_specs=out_specs,
        scratch_shapes=scratch, name=name,
        compiler_params=pltpu.CompilerParams(vmem_limit_bytes=24 * 1024 * 1024),
    )


def one_hot(idx_ref, rows):
    places = lax.broadcasted_iota(jnp.int32, (rows, idx_ref.shape[1]), 0)
    return (places == idx_ref[...]).astype(F32).astype(BF16)


def digits(count, dim, sizes):
    left = lax.broadcasted_iota(jnp.int32, (count, count), dim)
    found = []
    for size in reversed(sizes):
        found.append(lax.rem(left, size))
        left = lax.div(left, size)
    return found[::-1]


def boundary_row(x, zh, zl, s):
    return ((x * ZH + zh) * ZL + zl) * SLOTS + s


def permutation(match):
    return match.astype(F32).astype(BF16)


def pick_kernel(idx_ref, features_ref, out_ref):
    picks = one_hot(idx_ref, features_ref.shape[0])
    out_ref[...] = dot(picks, features_ref[...], 0, 0).astype(BF16)


def terms_kernel(place_ref, count_ref, src_ref, dst_ref, tiles_ref, cot_ref, mine_ref, other_ref, acc_ref):
    live = count_ref[0]
    core = place_ref[1]
    mine_ref[...] = jnp.zeros(mine_ref.shape, BF16)
    other_ref[...] = jnp.zeros(other_ref.shape, BF16)
    for k in range(NT):
        @pl.when(k < live)
        def _():
            acc_ref[src_ref[k]] = jnp.zeros(acc_ref.shape[1:], F32)
    for k in range(NT):
        @pl.when(k < live)
        def _():
            acc_ref[src_ref[k]] += dot(tiles_ref[k], cot_ref[dst_ref[k]], 0, 0)
    for k in range(NT):
        block = src_ref[k]
        member = lax.div(lax.rem(block, 16), 2)
        y = lax.div(member, 2)
        part = lax.rem(block, 2) + 2 * lax.div(block, 16)
        same = lax.rem(member, 2) == core

        @pl.when((k < live) & same)
        def _():
            mine_ref[y, part] = acc_ref[block].astype(BF16)

        @pl.when((k < live) & jnp.logical_not(same))
        def _():
            other_ref[y, part] = acc_ref[block].astype(BF16)


def pair_kernel(place_ref, mine_ref, came_ref, keep_ref, *out_refs):
    y = place_ref[0]
    keep_ref[...] = mine_ref[y].astype(F32) + came_ref[y].astype(F32)
    for step, out_ref in enumerate(out_refs, 1):
        to = lax.rem(y + step, Y)
        out_ref[...] = (mine_ref[to].astype(F32) + came_ref[to].astype(F32)).astype(BF16)


def mid_kernel(keep_ref, came1_ref, came2_ref, came3_ref, features_ref, arrived_ref, own_ref, bound_ref, gw_ref):
    terms = keep_ref[...]
    for came_ref in (came1_ref, came2_ref, came3_ref):
        terms += came_ref[...].astype(F32)
    own = terms[:2].reshape(2 * TILE, -1)
    bound = terms[2:].reshape(2 * TILE, -1)
    own_ref[...] = own
    own_high, own_low = halves(own)
    bound_high, bound_low = halves(bound)
    features = features_ref[...]
    arrived = arrived_ref[...]
    gw = (dot(features, own_high, 0, 0) + dot(features, own_low, 0, 0)
          + dot(arrived, bound_high, 0, 0) + dot(arrived, bound_low, 0, 0))
    for c in range(CHUNKS):
        row, col = c // 2 * 8, c % 2 * 128
        gw_ref[c] = gw[row:row + 8, col:col + 128]
    rows = bound.shape[0]
    x, zl, zh, s = digits(rows, 0, (X, ZL, ZH, SLOTS))
    order = permutation(boundary_row(x, zh, zl, s) == lax.broadcasted_iota(jnp.int32, (rows, rows), 1))
    bound_ref[...] = dot(order, bound_high).astype(BF16)


def pack_kernel(side_ref, near_ref, out_ref):
    rows = side_ref.shape[0]
    zh, x, zl, s = digits(rows, 0, (ZH, X, ZL, SLOTS))
    order = permutation(((x * ZL + zl) * ZH + zh) * SLOTS + s == lax.broadcasted_iota(jnp.int32, (rows, rows), 1))
    lines = rows // ZH
    out_ref[:, :lines, :] = dot(order, side_ref[...]).astype(BF16).reshape(ZH, lines, -1)
    high, low = halves(jnp.sum(near_ref[...], axis=0))
    both = jnp.concatenate([high, low], axis=1)
    for z in range(ZH):
        out_ref[z, lines:, :] = both


def far_kernel(far_ref, done_ref, out_ref):
    del done_ref
    lines = far_ref.shape[1] - 8
    both = jnp.sum(far_ref[:, lines:, :].astype(F32), axis=0)
    out_ref[...] = jnp.broadcast_to((both[:, :128] + both[:, 128:])[None], out_ref.shape)


def back_kernel(idx_ref, own_ref, far_ref, weight_ref, out_ref):
    rows = own_ref.shape[0]
    count = idx_ref.shape[1]
    lines = far_ref.shape[1] - 8
    picks = one_hot(idx_ref, rows)
    zh, x, zl, s = digits(count, 1, (ZH, X, ZL, SLOTS))
    order = permutation(boundary_row(x, zh, zl, s) == lax.broadcasted_iota(jnp.int32, (count, count), 0))
    back = far_ref[:, :lines, :].reshape(count, -1)
    total = own_ref[...] + dot(dot(picks, order).astype(BF16), back)
    high, low = halves(total)
    weight = weight_ref[...]
    out_ref[...] = dot(high, weight, 1, 1) + dot(low, weight, 1, 1)


def forward_kernel(place_ref, count_ref, src_ref, dst_ref, tiles_ref, own_ref, same_ref, twin_ref, weight_ref,
                   out_ref, acc_ref):
    live = count_ref[0]
    acc_ref[...] = jnp.zeros(acc_ref.shape, F32)
    for k in range(NT):
        block = src_ref[k]
        member = lax.div(lax.rem(block, 16), 2)
        away = lax.rem(place_ref[0] - lax.div(member, 2) + Y, Y)
        half = lax.rem(block, 2)
        same = lax.rem(member, 2) == place_ref[1]

        def add(tile, source):
            acc_ref[dst_ref[k]] += dot(tile, source)

        @pl.when((k < live) & (block < 16))
        def _():
            add(tiles_ref[k], own_ref[block])

        @pl.when((k < live) & (block >= 16) & same)
        def _():
            add(tiles_ref[k], same_ref[away, half])

        @pl.when((k < live) & (block >= 16) & jnp.logical_not(same))
        def _():
            add(tiles_ref[k], twin_ref[away, half])
    for t in range(2):
        out_ref[t] = dot(acc_ref[t].astype(BF16), weight_ref[...]).astype(BF16)


def per_device(
    features, tiles, tile_dst, tile_src, tile_count, send_rows, send_count, weight, cotangent
):
    rows, width = features.shape
    groups, slots = send_rows.shape[1:]
    shape = jax.ShapeDtypeStruct
    place = jnp.stack([lax.axis_index("y"), lax.axis_index("core")])
    live = jnp.arange(slots, dtype=jnp.int32)[None, :] < send_count[0][:, None]
    idx = jnp.where(live, send_rows[0], -1).reshape(1, groups * slots)

    outgoing = call(pick_kernel, shape((groups * slots, width), BF16), [VMEM] * 2, "pick")(idx, features)
    arrived = swap(outgoing.reshape(groups, slots, width), GRP).reshape(groups * slots, width)

    part = shape((4, TILE, width), BF16)
    half = shape((Y, 4, TILE, width), BF16)
    mine, other = call(
        terms_kernel, (half, half), [SMEM] * 4 + [VMEM] * 2, "terms", [pltpu.VMEM((32, TILE, width), F32)],
    )(place, tile_count, tile_src, tile_dst, tiles, cotangent.reshape(2, TILE, width))
    came = shift(other, "core", 1, CORE)
    keep, *sent = call(
        pair_kernel, (shape((4, TILE, width), F32), part, part, part), [SMEM] + [VMEM] * 2, "pair",
    )(place, mine, came)
    came = [shift(block, "y", step, Y) for step, block in enumerate(sent, 1)]

    own, bound, gw = call(
        mid_kernel,
        (shape((rows, width), F32), shape((rows, width), BF16), shape((CHUNKS, 8, 128), F32)),
        [VMEM] * 6, "mid",
    )(keep, *came, features, arrived)

    side = swap(bound.reshape(X * ZL, ZH * slots, width), SIDE).reshape(rows, width)
    near = swap(gw, NEAR)
    packed = call(pack_kernel, shape((ZH, rows // ZH + 8, width), BF16), [VMEM] * 2, "pack")(side, near)
    far = swap(packed, FAR)
    all_own = lax.all_gather(features, DEV, axis=0, tiled=True).reshape(16, TILE, width)
    block = arrived.reshape(1, 2, TILE, width)
    same = jnp.concatenate([block] + [shift(block, "y", step, Y) for step in (1, 2, 3)], axis=0)
    twin = shift(same, "core", 1, CORE)
    output = call(
        forward_kernel, shape((2, TILE, width), BF16), [SMEM] * 4 + [VMEM] * 5, "forward",
        [pltpu.VMEM((2, TILE, width), F32)],
    )(place, tile_count, tile_src, tile_dst, tiles, all_own, same, twin, weight)

    spread = call(far_kernel, shape((CHUNKS, 8, 128), F32), [VMEM, ANY], "far")(far, output)
    grad_weight = swap(spread, NEAR).reshape(width // 8, 2, 8, 128).transpose(0, 2, 1, 3).reshape(width, width)
    grad_features = call(back_kernel, shape((rows, width), F32), [VMEM] * 4, "back")(idx, own, far, weight)
    output = output.reshape(rows, width)
    return output, grad_features, grad_weight


def solution(mesh):
    fine = Mesh(mesh.devices.reshape(SIZES), AXES)
    split = [P(AXES)] * 7
    return jax.shard_map(
        per_device,
        mesh=fine,
        in_specs=(*split, P(), P(AXES)),
        out_specs=(P(AXES), P(AXES), P()),
        check_vma=False,
    )
```

time: 240 us -> 179 us (0.75)
  waiting for transfers between devices: 137 us -> 45.2 us
  starting transfers between devices: 66.5 us -> 89.7 us
  blocking collectives: 0 us -> 9.32 us
  local copies, waits for them, and re-layouts: 13.4 us -> 8.45 us
  Pallas kernels: 7.06 us -> 9.83 us
    all_to_all x6 -> x4, waiting for transfers between devices: 109 us -> 37.2 us  [swap(): return lax.all_to_all(x, axes, split_axis=0, concat_axis=0, tiled=True)]
    ppermute x0 -> x8, starting transfers between devices: none -> 39.4 us  [shift(): return lax.ppermute(x, axis, [(i, (i + step) % size) for i in range(size)])]
    all_gather x2 -> x1, waiting for transfers between devices: 26.1 us -> 0.01 us  [per_device(): lax.all_gather(features, DEV, axis=0, tiled=True).reshape(16, TILE, width)]
    all_to_all x6 -> x4, starting transfers between devices: 66.4 us -> 50.2 us  [swap(): return lax.all_to_all(x, axes, split_axis=0, concat_axis=0, tiled=True)]
    all_to_all x0 -> x1, blocking collectives: none -> 9.32 us  [swap(): return lax.all_to_all(x, axes, split_axis=0, concat_axis=0, tiled=True)]
    ppermute x0 -> x8, waiting for transfers between devices: none -> 7.24 us  [shift(): return lax.ppermute(x, axis, [(i, (i + step) % size) for i in range(size)])]
    unnamed x29 -> x27, local copies, waits for them, and re-layouts: 8.65 us -> 5.52 us
    pallas_call x5 -> x8, Pallas kernels: 7.06 us -> 9.83 us  [the longest x1 2.32 us: per_device(): call(terms_kernel, (half, half), [SMEM] * 4 + [VMEM] * 2, 'terms', [pltpu...]
  transfers between devices with their start and end apart: 8 -> 13, of which waited for: 6 -> 8; matrix products, arithmetic and copies ran while one was open for 1% -> 2% of each run, Pallas kernels for 3% -> 3%
where the time goes in v2:
time: 179 us; the launch traced here: 177 us
  starting transfers between devices  89.7 us (50%)
  waiting for transfers between devices  45.2 us (25%)
  between operations  14.9 us (8%)
  Pallas kernels  9.83 us (5%)
  blocking collectives  9.32 us (5%)
  local copies, waits for them, and re-layouts  8.45 us (5%)
    all_to_all x4, starting transfers between devices, swap(): return lax.all_to_all(x, axes, split_axis=0, concat_axis=0, tiled=True)  50.2 us
    ppermute x8, starting transfers between devices, shift(): return lax.ppermute(x, axis, [(i, (i + step) % size) for i in range(size)])  39.4 us
    all_to_all x4, waiting for transfers between devices, swap(): return lax.all_to_all(x, axes, split_axis=0, concat_axis=0, tiled=True)  37.2 us
    all_to_all x1, blocking collectives, swap(): return lax.all_to_all(x, axes, split_axis=0, concat_axis=0, tiled=True)  9.32 us
    ppermute x8, waiting for transfers between devices, shift(): return lax.ppermute(x, axis, [(i, (i + step) % size) for i in range(size)])  7.24 us
    unnamed x27, local copies, waits for them, and re-layouts  5.52 us
  transfers between devices with their start and end apart: 13, of which 8 were waited for; matrix products, arithmetic and copies ran while one was open for 2% of the time, Pallas kernels for 3%

profile of v2, /device:TPU:1, one launch (start us, length us, event | category | flops | bytes accessed | tf_op | source)
XLA Modules:
  0.0 177.5 jit_solution(7392360382630887068)
XLA Ops:
  10.4 2.3 %terms.1 = (bf16[4,4,128,256]{3,2,1,0:T(8,128)(2,1)S(1)}, bf16[4,4,128,256]{3,2,1,0:T(8,128)(2,1)}) custom-call(s32[2]{0:T(128)S(1)} %pad_add_fusion.place_ref, s32[1]{0:T(128)S(6)} %copy.18.count_ref, s32[8]{0:T(128)S(1)} %copy-done.7, s32[8]{0:T(128)S(1)} %copy-done.8, bf16[8,128,128]{2,1,0:T(8,128)(2,1)S(1)} %copy-done.1, bf16[2,128,256]{2,1,0:T(8,128)(2,1)S(1)} %bitcast.16), custom_call_target="tpu_custom_call" | custom-call | tf_op jit(solution)/shard_map/terms/pallas_call | solution.py:217
  12.7 17.4 %collective-permute-start.4 = (bf16[4,4,128,256]{3,2,1,0:T(8,128)(2,1)}, bf16[4,4,128,256]{3,2,1,0:T(8,128)(2,1)S(1)}, u32[]{:S(2)}, u32[]{:S(2)}) collective-permute-start(bf16[4,4,128,256]{3,2,1,0:T(8,128)(2,1)} %get-tuple-element.13), channel_id=1, source_target_pairs={{0,1},{1,0},{2,3},{3,2},{4,5},{5,4},{6,7},{7,6},{8,9},{9,8},{10,11... | collective-permute-start | bytes 3145736 | tf_op jit(solution)/shard_map/ppermute | solution.py:33
  31.7 20.0 %all-to-all-start = ((bf16[128,2,256]{2,1,0:T(2,128)(2,1)}), bf16[128,2,256]{2,1,0:T(2,128)(2,1)}, u32[]{:S(2)}, u32[]{:S(2)}) async-start(bf16[128,2,256]{2,1,0:T(2,128)(2,1)} %reshape.68), calls=%async_computation | async-start | bytes 262144 | tf_op jit(solution)/shard_map/all_to_all | solution.py:29
  51.7 1.4 pair.1
  53.1 3.1 %collective-permute-start.5 = (bf16[4,128,256]{2,1,0:T(8,128)(2,1)}, bf16[4,128,256]{2,1,0:T(8,128)(2,1)S(1)}, u32[]{:S(2)}, u32[]{:S(2)}) collective-permute-start(bf16[4,128,256]{2,1,0:T(8,128)(2,1)} %get-tuple-element.15), channel_id=1, source_target_pairs={{0,2},{2,4},{4,6},{6,0},{1,3},{3,5},{5,7},{7,1},{8,10},{10,12},{12... | collective-permute-start | bytes 786440 | tf_op jit(solution)/shard_map/ppermute | solution.py:33
  56.2 5.2 %collective-permute-start.6 = (bf16[4,128,256]{2,1,0:T(8,128)(2,1)S(1)}, bf16[4,128,256]{2,1,0:T(8,128)(2,1)S(1)}, u32[]{:S(2)}, u32[]{:S(2)}) collective-permute-start(bf16[4,128,256]{2,1,0:T(8,128)(2,1)S(1)} %get-tuple-element.16), channel_id=1, source_target_pairs={{0,4},{2,6},{4,0},{6,2},{1,5},{3,7},{5,1},{7,3},{8,12},{10,14},{12... | collective-permute-start | bytes 786440 | tf_op jit(solution)/shard_map/ppermute | solution.py:33
  61.5 2.1 %collective-permute-start.7 = (bf16[4,128,256]{2,1,0:T(8,128)(2,1)S(1)}, bf16[4,128,256]{2,1,0:T(8,128)(2,1)S(1)}, u32[]{:S(2)}, u32[]{:S(2)}) collective-permute-start(bf16[4,128,256]{2,1,0:T(8,128)(2,1)S(1)} %get-tuple-element.17), channel_id=1, source_target_pairs={{0,6},{2,0},{4,2},{6,4},{1,7},{3,1},{5,3},{7,5},{8,14},{10,8},{12,... | collective-permute-start | bytes 786440 | tf_op jit(solution)/shard_map/ppermute | solution.py:33
  63.6 18.2 %all-to-all-done = bf16[128,2,256]{2,1,0:T(2,128)(2,1)} async-done(((bf16[128,2,256]{2,1,0:T(2,128)(2,1)}), bf16[128,2,256]{2,1,0:T(2,128)(2,1)}, u32[]{:S(2)}, u32[]{:S(2)}) %all-to-all-start) | async-done | bytes 131104 | tf_op jit(solution)/shard_map/all_to_all | solution.py:29
  83.9 9.3 %all_to_all.25 = bf16[8,32,256]{2,1,0:T(8,128)(2,1)S(1)} all-to-all(bf16[8,32,256]{2,1,0:T(8,128)(2,1)S(1)} %bitcast.17), channel_id=1, replica_groups=mesh['x'=4,'zh'=16,'zl'=2,'y'=4,'core'=2] {'x','zl'}, dimensions={0} | all-to-all | bytes 262144 | tf_op jit(solution)/shard_map/all_to_all | solution.py:29
  93.2 9.5 %all-to-all-start.2 = ((f32[64,8,128]{2,1,0:T(8,128)}), f32[64,8,128]{2,1,0:T(8,128)S(1)}, u32[]{:S(2)}, u32[]{:S(2)}) async-start(f32[64,8,128]{2,1,0:T(8,128)} %get-tuple-element.20), calls=%async_computation.2 | async-start | bytes 524288 | tf_op jit(solution)/shard_map/all_to_all | solution.py:29
  103.5 9.1 %all-to-all-done.2.near_ref = f32[64,8,128]{2,1,0:T(8,128)S(1)} async-done(((f32[64,8,128]{2,1,0:T(8,128)}), f32[64,8,128]{2,1,0:T(8,128)S(1)}, u32[]{:S(2)}, u32[]{:S(2)}) %all-to-all-start.2) | async-done | bytes 262176 | tf_op jit(solution)/shard_map/all_to_all | solution.py:29
  113.4 8.8 %all-to-all-start.3 = ((bf16[16,24,256]{2,1,0:T(8,128)(2,1)}), bf16[16,24,256]{2,1,0:T(8,128)(2,1)S(1)}, u32[]{:S(2)}, u32[]{:S(2)}) async-start(bf16[16,24,256]{2,1,0:T(8,128)(2,1)} %pack.1), calls=%async_computation.3 | async-start | bytes 393216 | tf_op jit(solution)/shard_map/all_to_all | solution.py:29
  123.2 2.2 %collective-permute-start = (bf16[1,2,128,256]{3,2,1,0:T(8,128)(2,1)S(1)}, bf16[1,2,128,256]{3,2,1,0:T(8,128)(2,1)S(1)}, u32[]{:S(2)}, u32[]{:S(2)}) collective-permute-start(bf16[1,2,128,256]{3,2,1,0:T(8,128)(2,1)S(1)} %reshape_reshape.3), channel_id=1, source_target_pairs={{0,2},{2,4},{4,6},{6,0},{1,3},{3,5},{5,7},{7,1},{8,10},{10,12},{12... | collective-permute-start | bytes 393224 | tf_op jit(solution)/shard_map/ppermute | solution.py:33
  125.4 3.7 %collective-permute-start.1 = (bf16[1,2,128,256]{3,2,1,0:T(8,128)(2,1)S(1)}, bf16[1,2,128,256]{3,2,1,0:T(8,128)(2,1)S(1)}, u32[]{:S(2)}, u32[]{:S(2)}) collective-permute-start(bf16[1,2,128,256]{3,2,1,0:T(8,128)(2,1)S(1)} %reshape_reshape.3), channel_id=1, source_target_pairs={{0,4},{2,6},{4,0},{6,2},{1,5},{3,7},{5,1},{7,3},{8,12},{10,14},{12... | collective-permute-start | bytes 393224 | tf_op jit(solution)/shard_map/ppermute | solution.py:33
  129.1 2.5 %collective-permute-start.2 = (bf16[1,2,128,256]{3,2,1,0:T(8,128)(2,1)S(1)}, bf16[1,2,128,256]{3,2,1,0:T(8,128)(2,1)S(1)}, u32[]{:S(2)}, u32[]{:S(2)}) collective-permute-start(bf16[1,2,128,256]{3,2,1,0:T(8,128)(2,1)S(1)} %reshape_reshape.3), channel_id=1, source_target_pairs={{0,6},{2,0},{4,2},{6,4},{1,7},{3,1},{5,3},{7,5},{8,14},{10,8},{12,... | collective-permute-start | bytes 393224 | tf_op jit(solution)/shard_map/ppermute | solution.py:33
  132.0 3.8 %collective-permute-done.1 = bf16[1,2,128,256]{3,2,1,0:T(8,128)(2,1)S(1)} collective-permute-done((bf16[1,2,128,256]{3,2,1,0:T(8,128)(2,1)S(1)}, bf16[1,2,128,256]{3,2,1,0:T(8,128)(2,1)S(1)}, u32[]{:S(2)}, u32[]{:S(2)}) %collective-permute-start.1) | collective-permute-done | bytes 131104 | tf_op jit(solution)/shard_map/ppermute | solution.py:33
  135.9 1.5 collective-permute-done.2
  137.4 3.1 %collective-permute-start.3 = (bf16[4,2,128,256]{3,2,1,0:T(8,128)(2,1)S(1)}, bf16[4,2,128,256]{3,2,1,0:T(8,128)(2,1)S(1)}, u32[]{:S(2)}, u32[]{:S(2)}) collective-permute-start(bf16[4,2,128,256]{3,2,1,0:T(8,128)(2,1)S(1)} %constant_dynamic-update-slice_fusion.same_ref), channel_id=1, source_target_pairs={{0,1},{1,0},{2,3},{3,2},{4,5},{5,4},{6,7},{7,6},{8,9},{9,8},{10,11... | collective-permute-start | bytes 1572872 | tf_op jit(solution)/shard_map/ppermute | solution.py:33
  140.5 1.5 collective-permute-done.3.twin_ref
  142.0 1.2 copy-done.3
  143.2 1.9 %forward.1.done_ref = bf16[2,128,256]{2,1,0:T(8,128)(2,1)} custom-call(s32[2]{0:T(128)S(1)} %pad_add_fusion.place_ref, s32[1]{0:T(128)S(6)} %copy.18.count_ref, s32[8]{0:T(128)S(1)} %copy-done.7, s32[8]{0:T(128)S(1)} %copy-done.8, bf16[8,128,128]{2,1,0:T(8,128)(2,1)S(1)} %copy-done.2, bf16[16,128,256]{2,1,0:T(8,128)(2,1)S(1)} %bitcast.13, ...), custom_call_target="tpu_custom_call" | custom-call | tf_op jit(solution)/shard_map/forward/pallas_call | solution.py:240
  145.1 1.4 all-to-all-done.3.far_ref
  148.2 12.0 %all-to-all-start.4 = ((f32[64,8,128]{2,1,0:T(8,128)}), f32[64,8,128]{2,1,0:T(8,128)S(1)}, u32[]{:S(2)}, u32[]{:S(2)}) async-start(f32[64,8,128]{2,1,0:T(8,128)} %far.1), calls=%async_computation.4 | async-start | bytes 524288 | tf_op jit(solution)/shard_map/all_to_all | solution.py:29
  161.3 8.6 %all-to-all-done.4 = f32[64,8,128]{2,1,0:T(8,128)S(1)} async-done(((f32[64,8,128]{2,1,0:T(8,128)}), f32[64,8,128]{2,1,0:T(8,128)S(1)}, u32[]{:S(2)}, u32[]{:S(2)}) %all-to-all-start.4) | async-done | bytes 262176 | tf_op jit(solution)/shard_map/all_to_all | solution.py:29
  (48 shorter events, 12.7 us)
Async XLA Ops:
  7.9 0.7 copy-start.7
  7.9 0.7 copy-start.8
  8.6 0.9 copy-start.1
  9.5 0.9 copy-start.6
  10.4 19.8 %copy-start.10 = (s32[1,128]{1,0:T(1,128)S(1)}, s32[1,128]{1,0:T(1,128)}, u32[]{:S(2)}) copy-start(s32[1,128]{1,0:T(1,128)} %param.15) | copy-start | bytes 1540
  10.4 19.9 %copy-start.9 = (s32[1,128,2]{1,2,0:T(2,128)S(1)}, s32[1,128,2]{1,2,0:T(2,128)}, u32[]{:S(2)}) copy-start(s32[1,128,2]{1,2,0:T(2,128)} %param.14) | copy-start | bytes 3076
  12.7 18.0 %copy-start = (bf16[256,256]{1,0:T(8,128)(2,1)S(1)}, bf16[256,256]{1,0:T(8,128)(2,1)}, u32[]{:S(2)}) copy-start(bf16[256,256]{1,0:T(8,128)(2,1)} %features_ref.3) | copy-start | bytes 393220
  12.7 38.9 %collective-permute-start.4 = (bf16[4,4,128,256]{3,2,1,0:T(8,128)(2,1)}, bf16[4,4,128,256]{3,2,1,0:T(8,128)(2,1)S(1)}, u32[]{:S(2)}, u32[]{:S(2)}) collective-permute-start(bf16[4,4,128,256]{3,2,1,0:T(8,128)(2,1)} %get-tuple-element.13), channel_id=1, source_target_pairs={{0,1},{1,0},{2,3},{3,2},{4,5},{5,4},{6,7},{7,6},{8,9},{9,8},{10,11... | collective-permute-start | bytes 3145736 | tf_op jit(solution)/shard_map/ppermute | solution.py:33
  31.7 50.1 %all-to-all-start = ((bf16[128,2,256]{2,1,0:T(2,128)(2,1)}), bf16[128,2,256]{2,1,0:T(2,128)(2,1)}, u32[]{:S(2)}, u32[]{:S(2)}) async-start(bf16[128,2,256]{2,1,0:T(2,128)(2,1)} %reshape.68), calls=%async_computation | async-start | bytes 262144 | tf_op jit(solution)/shard_map/all_to_all | solution.py:29
  53.1 29.7 %collective-permute-start.5 = (bf16[4,128,256]{2,1,0:T(8,128)(2,1)}, bf16[4,128,256]{2,1,0:T(8,128)(2,1)S(1)}, u32[]{:S(2)}, u32[]{:S(2)}) collective-permute-start(bf16[4,128,256]{2,1,0:T(8,128)(2,1)} %get-tuple-element.15), channel_id=1, source_target_pairs={{0,2},{2,4},{4,6},{6,0},{1,3},{3,5},{5,7},{7,1},{8,10},{10,12},{12... | collective-permute-start | bytes 786440 | tf_op jit(solution)/shard_map/ppermute | solution.py:33
  56.2 26.6 %collective-permute-start.6 = (bf16[4,128,256]{2,1,0:T(8,128)(2,1)S(1)}, bf16[4,128,256]{2,1,0:T(8,128)(2,1)S(1)}, u32[]{:S(2)}, u32[]{:S(2)}) collective-permute-start(bf16[4,128,256]{2,1,0:T(8,128)(2,1)S(1)} %get-tuple-element.16), channel_id=1, source_target_pairs={{0,4},{2,6},{4,0},{6,2},{1,5},{3,7},{5,1},{7,3},{8,12},{10,14},{12... | collective-permute-start | bytes 786440 | tf_op jit(solution)/shard_map/ppermute | solution.py:33
  61.5 21.3 %collective-permute-start.7 = (bf16[4,128,256]{2,1,0:T(8,128)(2,1)S(1)}, bf16[4,128,256]{2,1,0:T(8,128)(2,1)S(1)}, u32[]{:S(2)}, u32[]{:S(2)}) collective-permute-start(bf16[4,128,256]{2,1,0:T(8,128)(2,1)S(1)} %get-tuple-element.17), channel_id=1, source_target_pairs={{0,6},{2,0},{4,2},{6,4},{1,7},{3,1},{5,3},{7,5},{8,14},{10,8},{12,... | collective-permute-start | bytes 786440 | tf_op jit(solution)/shard_map/ppermute | solution.py:33
  93.2 19.3 %all-to-all-start.2 = ((f32[64,8,128]{2,1,0:T(8,128)}), f32[64,8,128]{2,1,0:T(8,128)S(1)}, u32[]{:S(2)}, u32[]{:S(2)}) async-start(f32[64,8,128]{2,1,0:T(8,128)} %get-tuple-element.20), calls=%async_computation.2 | async-start | bytes 524288 | tf_op jit(solution)/shard_map/all_to_all | solution.py:29
  102.7 39.3 %all-gather.2.cloned.1.call-start = ((), (), s32[]{:S(2)}) async-start(), calls=%async_computation.5 | async-start | bytes 1179648 | tf_op jit(solution)/shard_map/all_gather | solution.py:236
  113.4 33.1 %all-to-all-start.3 = ((bf16[16,24,256]{2,1,0:T(8,128)(2,1)}), bf16[16,24,256]{2,1,0:T(8,128)(2,1)S(1)}, u32[]{:S(2)}, u32[]{:S(2)}) async-start(bf16[16,24,256]{2,1,0:T(8,128)(2,1)} %pack.1), calls=%async_computation.3 | async-start | bytes 393216 | tf_op jit(solution)/shard_map/all_to_all | solution.py:29
  123.2 8.8 %collective-permute-start = (bf16[1,2,128,256]{3,2,1,0:T(8,128)(2,1)S(1)}, bf16[1,2,128,256]{3,2,1,0:T(8,128)(2,1)S(1)}, u32[]{:S(2)}, u32[]{:S(2)}) collective-permute-start(bf16[1,2,128,256]{3,2,1,0:T(8,128)(2,1)S(1)} %reshape_reshape.3), channel_id=1, source_target_pairs={{0,2},{2,4},{4,6},{6,0},{1,3},{3,5},{5,7},{7,1},{8,10},{10,12},{12... | collective-permute-start | bytes 393224 | tf_op jit(solution)/shard_map/ppermute | solution.py:33
  125.4 10.5 %collective-permute-start.1 = (bf16[1,2,128,256]{3,2,1,0:T(8,128)(2,1)S(1)}, bf16[1,2,128,256]{3,2,1,0:T(8,128)(2,1)S(1)}, u32[]{:S(2)}, u32[]{:S(2)}) collective-permute-start(bf16[1,2,128,256]{3,2,1,0:T(8,128)(2,1)S(1)} %reshape_reshape.3), channel_id=1, source_target_pairs={{0,4},{2,6},{4,0},{6,2},{1,5},{3,7},{5,1},{7,3},{8,12},{10,14},{12... | collective-permute-start | bytes 393224 | tf_op jit(solution)/shard_map/ppermute | solution.py:33
  129.1 8.3 %collective-permute-start.2 = (bf16[1,2,128,256]{3,2,1,0:T(8,128)(2,1)S(1)}, bf16[1,2,128,256]{3,2,1,0:T(8,128)(2,1)S(1)}, u32[]{:S(2)}, u32[]{:S(2)}) collective-permute-start(bf16[1,2,128,256]{3,2,1,0:T(8,128)(2,1)S(1)} %reshape_reshape.3), channel_id=1, source_target_pairs={{0,6},{2,0},{4,2},{6,4},{1,7},{3,1},{5,3},{7,5},{8,14},{10,8},{12,... | collective-permute-start | bytes 393224 | tf_op jit(solution)/shard_map/ppermute | solution.py:33
  132.0 10.0 %copy-start.2 = (bf16[8,128,128]{2,1,0:T(8,128)(2,1)S(1)}, bf16[8,128,128]{2,1,0:T(8,128)(2,1)}, u32[]{:S(2)}) copy-start(bf16[8,128,128]{2,1,0:T(8,128)(2,1)} %tiles_ref.3) | copy-start | bytes 786436
  135.9 6.2 %copy-start.4 = (bf16[256,256]{1,0:T(8,128)(2,1)S(1)}, bf16[256,256]{1,0:T(8,128)(2,1)}, u32[]{:S(2)}) copy-start(bf16[256,256]{1,0:T(8,128)(2,1)} %weight_ref.3) | copy-start | bytes 393220
  137.4 4.6 %collective-permute-start.3 = (bf16[4,2,128,256]{3,2,1,0:T(8,128)(2,1)S(1)}, bf16[4,2,128,256]{3,2,1,0:T(8,128)(2,1)S(1)}, u32[]{:S(2)}, u32[]{:S(2)}) collective-permute-start(bf16[4,2,128,256]{3,2,1,0:T(8,128)(2,1)S(1)} %constant_dynamic-update-slice_fusion.same_ref), channel_id=1, source_target_pairs={{0,1},{1,0},{2,3},{3,2},{4,5},{5,4},{6,7},{7,6},{8,9},{9,8},{10,11... | collective-permute-start | bytes 1572872 | tf_op jit(solution)/shard_map/ppermute | solution.py:33
  142.0 1.2 copy-start.3
  146.5 0.9 copy-start.5
  148.2 21.8 %all-to-all-start.4 = ((f32[64,8,128]{2,1,0:T(8,128)}), f32[64,8,128]{2,1,0:T(8,128)S(1)}, u32[]{:S(2)}, u32[]{:S(2)}) async-start(f32[64,8,128]{2,1,0:T(8,128)} %far.1), calls=%async_computation.4 | async-start | bytes 524288 | tf_op jit(solution)/shard_map/all_to_all | solution.py:29
Sparse Core Ops, SparseCore 0:
  106.3 32.1 all-gather.1

commit v3 on v2

v3 whole, which is shorter than its diff:
```python
import jax
import jax.numpy as jnp
from jax import lax
from jax.experimental import pallas as pl
from jax.experimental.pallas import tpu as pltpu
from jax.sharding import Mesh, PartitionSpec as P

AXES = ("x", "zh", "zl", "y", "core")
SIZES = (4, 16, 2, 4, 2)
SLOTS = 2
X, ZH, ZL, Y, CORE = SIZES
DEV = ("y", "core")
SIDE = ("x", "zl")
NEAR = ("x", "zl", "y", "core")
FAR = "zh"
TILE = 128
NT = 8
CHUNKS = 64

F32 = jnp.float32
BF16 = jnp.bfloat16
SMEM = pl.BlockSpec(memory_space=pltpu.SMEM)
ANY = pl.BlockSpec(memory_space=pl.ANY)
VMEM = pl.BlockSpec(memory_space=pltpu.VMEM)


def swap(x, axes):
    return lax.all_to_all(x, axes, split_axis=0, concat_axis=0, tiled=True)


def shift(x, axis, step, size):
    return lax.ppermute(x, axis, [(i, (i + step) % size) for i in range(size)])


def dot(a, b, da=1, db=0):
    return lax.dot_general(a, b, (((da,), (db,)), ((), ())), preferred_element_type=F32)


def halves(x):
    high = x.astype(BF16)
    return high, (x - high.astype(F32)).astype(BF16)


def call(kernel, out_shape, in_specs, name, scratch=()):
    out_specs = (VMEM,) * len(out_shape) if isinstance(out_shape, tuple) else VMEM
    return pl.pallas_call(
        kernel, out_shape=out_shape, in_specs=in_specs, out_specs=out_specs,
        scratch_shapes=scratch, name=name,
        compiler_params=pltpu.CompilerParams(vmem_limit_bytes=24 * 1024 * 1024),
    )


def digits(count, dim, sizes):
    left = lax.broadcasted_iota(jnp.int32, (count, count), dim)
    found = []
    for size in reversed(sizes):
        found.append(lax.rem(left, size))
        left = lax.div(left, size)
    return found[::-1]


def boundary_row(x, zh, zl, s):
    return ((x * ZH + zh) * ZL + zl) * SLOTS + s


def permutation(match):
    return match.astype(F32).astype(BF16)


def picks(rows, rows_ref, count_ref):
    groups = count_ref.shape[1]
    places = lax.broadcasted_iota(jnp.int32, (rows, groups), 0)
    found = []
    for slot in range(SLOTS):
        live = count_ref[...] > slot
        wanted = jnp.where(live, rows_ref[slot:slot + 1, :], -1)
        found.append(permutation(places == wanted))
    count = groups * SLOTS
    zh, x, zl, s = digits(count, 1, (ZH, X, ZL, SLOTS))
    order = permutation(s * groups + (x * ZH + zh) * ZL + zl == lax.broadcasted_iota(jnp.int32, (count, count), 0))
    return dot(jnp.concatenate(found, axis=1), order).astype(BF16)


def pick_kernel(rows_ref, count_ref, features_ref, out_ref):
    wanted = picks(features_ref.shape[0], rows_ref, count_ref)
    out_ref[...] = dot(wanted, features_ref[...], 0, 0).astype(BF16).reshape(out_ref.shape)


def terms_kernel(place_ref, count_ref, src_ref, dst_ref, tiles_ref, cot_ref, mine_ref, other_ref, acc_ref):
    live = count_ref[0]
    core = place_ref[1]
    mine_ref[...] = jnp.zeros(mine_ref.shape, BF16)
    other_ref[...] = jnp.zeros(other_ref.shape, BF16)
    for k in range(NT):
        @pl.when(k < live)
        def _():
            acc_ref[src_ref[k]] = jnp.zeros(acc_ref.shape[1:], F32)
    for k in range(NT):
        @pl.when(k < live)
        def _():
            acc_ref[src_ref[k]] += dot(tiles_ref[k], cot_ref[dst_ref[k]], 0, 0)
    for k in range(NT):
        block = src_ref[k]
        member = lax.div(lax.rem(block, 16), 2)
        y = lax.div(member, 2)
        part = lax.rem(block, 2) + 2 * lax.div(block, 16)
        same = lax.rem(member, 2) == core

        @pl.when((k < live) & same)
        def _():
            mine_ref[y, part] = acc_ref[block].astype(BF16)

        @pl.when((k < live) & jnp.logical_not(same))
        def _():
            other_ref[y, part] = acc_ref[block].astype(BF16)


def pair_kernel(place_ref, mine_ref, came_ref, keep_ref, *out_refs):
    y = place_ref[0]
    keep_ref[...] = mine_ref[y].astype(F32) + came_ref[y].astype(F32)
    for step, out_ref in enumerate(out_refs, 1):
        to = lax.rem(y + step, Y)
        out_ref[...] = (mine_ref[to].astype(F32) + came_ref[to].astype(F32)).astype(BF16)


def side_kernel(keep_ref, came1_ref, came2_ref, came3_ref, far_ref, done_ref, own_ref, high_ref, low_ref, out_ref):
    del done_ref
    terms = keep_ref[...]
    for came_ref in (came1_ref, came2_ref, came3_ref):
        terms += came_ref[...].astype(F32)
    own_ref[...] = terms[:2].reshape(2 * TILE, -1)
    bound = terms[2:].reshape(2 * TILE, -1)
    rows, width = bound.shape
    column = lax.broadcasted_iota(jnp.int32, (rows, rows), 1)
    x, zl, zh, s = digits(rows, 0, (X, ZL, ZH, SLOTS))
    lines = rows // (X * ZL)
    order = permutation(((zh * X + x) * ZL + zl) * SLOTS + s == column)
    rows_out = dot(order, far_ref[...].reshape(rows, width)).astype(BF16)
    out_ref[:, :lines, :] = rows_out.reshape(X * ZL, lines, width)
    order = permutation(boundary_row(x, zh, zl, s) == column)
    high, low = halves(bound)
    high = dot(order, high).astype(BF16)
    high_ref[...] = high
    low_ref[...] = dot(order, low).astype(BF16)
    out_ref[:, lines:, :] = high.reshape(X * ZL, lines, width)


def mid_kernel(own_ref, high_ref, low_ref, side_ref, features_ref, gw_ref, arrived_ref):
    rows, width = own_ref.shape
    own_high, own_low = halves(own_ref[...])
    features = features_ref[...]
    arrived = side_ref[:, :rows // (X * ZL), :].reshape(rows, width)
    gw = (dot(features, own_high, 0, 0) + dot(features, own_low, 0, 0)
          + dot(arrived, high_ref[...], 0, 0) + dot(arrived, low_ref[...], 0, 0))
    for c in range(CHUNKS):
        row, col = c // 2 * 8, c % 2 * 128
        gw_ref[c] = gw[row:row + 8, col:col + 128]
    x, zl, zh, s = digits(rows, 1, (X, ZL, ZH, SLOTS))
    order = permutation(boundary_row(x, zh, zl, s) == lax.broadcasted_iota(jnp.int32, (rows, rows), 0))
    arrived_ref[...] = dot(order, arrived).astype(BF16)


def pack_kernel(side_ref, near_ref, out_ref):
    lines = out_ref.shape[1] - 8
    rows = ZH * lines
    width = out_ref.shape[2]
    zh, x, zl, s = digits(rows, 0, (ZH, X, ZL, SLOTS))
    order = permutation(((x * ZL + zl) * ZH + zh) * SLOTS + s == lax.broadcasted_iota(jnp.int32, (rows, rows), 1))
    side = side_ref[:, rows // (X * ZL):, :].reshape(rows, width)
    out_ref[:, :lines, :] = dot(order, side).astype(BF16).reshape(ZH, lines, width)
    high, low = halves(jnp.sum(near_ref[...], axis=0))
    both = jnp.concatenate([high, low], axis=1)
    for z in range(ZH):
        out_ref[z, lines:, :] = both


def far_kernel(far_ref, done_ref, out_ref):
    del done_ref
    lines = far_ref.shape[1] - 8
    both = jnp.sum(far_ref[:, lines:, :].astype(F32), axis=0)
    out_ref[...] = jnp.broadcast_to((both[:, :128] + both[:, 128:])[None], out_ref.shape)


def back_kernel(rows_ref, count_ref, own_ref, far_ref, weight_ref, out_ref):
    rows, width = own_ref.shape
    back = far_ref[:, :far_ref.shape[1] - 8, :].reshape(-1, width)
    total = own_ref[...] + dot(picks(rows, rows_ref, count_ref), back)
    high, low = halves(total)
    weight = weight_ref[...]
    out_ref[...] = dot(high, weight, 1, 1) + dot(low, weight, 1, 1)


def forward_kernel(count_ref, src_ref, dst_ref, tiles_ref, own_ref, bound_ref, weight_ref, out_ref, acc_ref):
    live = count_ref[0]
    acc_ref[...] = jnp.zeros(acc_ref.shape, F32)
    for k in range(NT):
        block = src_ref[k]

        @pl.when((k < live) & (block < 16))
        def _():
            acc_ref[dst_ref[k]] += dot(tiles_ref[k], own_ref[block])

        @pl.when((k < live) & (block >= 16))
        def _():
            acc_ref[dst_ref[k]] += dot(tiles_ref[k], bound_ref[block - 16])
    for t in range(2):
        out_ref[t] = dot(acc_ref[t].astype(BF16), weight_ref[...]).astype(BF16)


def per_device(
    features, tiles, tile_dst, tile_src, tile_count, send_rows, send_count, weight, cotangent
):
    rows, width = features.shape
    groups, slots = send_rows.shape[1:]
    lines = groups * slots // ZH
    shape = jax.ShapeDtypeStruct
    place = jnp.stack([lax.axis_index("y"), lax.axis_index("core")])
    send_rows = send_rows.transpose(0, 2, 1).reshape(slots, groups)
    blocked = (16, TILE, width)

    outgoing = call(pick_kernel, shape((ZH, lines, width), BF16), [VMEM] * 3, "pick")(send_rows, send_count, features)
    landed = swap(outgoing, FAR)
    all_own = lax.all_gather(features, DEV, axis=0, tiled=True)

    part = shape((4, TILE, width), BF16)
    half = shape((Y, 4, TILE, width), BF16)
    mine, other = call(
        terms_kernel, (half, half), [SMEM] * 4 + [VMEM] * 2, "terms", [pltpu.VMEM((32, TILE, width), F32)],
    )(place, tile_count, tile_src, tile_dst, tiles, cotangent.reshape(2, TILE, width))
    came = shift(other, "core", 1, CORE)
    keep, *sent = call(
        pair_kernel, (shape((4, TILE, width), F32), part, part, part), [SMEM] + [VMEM] * 2, "pair",
    )(place, mine, came)
    came = [shift(block, "y", step, Y) for step, block in enumerate(sent, 1)]

    square = shape((rows, width), BF16)
    own, high, low, side = call(
        side_kernel,
        (shape((rows, width), F32), square, square, shape((X * ZL, 2 * rows // (X * ZL), width), BF16)),
        [VMEM] * 5 + [ANY], "side",
    )(keep, *came, landed, all_own)
    side = swap(side, SIDE)
    gw, arrived = call(
        mid_kernel, (shape((CHUNKS, 8, 128), F32), square), [VMEM] * 5, "mid",
    )(own, high, low, side, features)
    near = swap(gw, NEAR)
    packed = call(pack_kernel, shape((ZH, lines + 8, width), BF16), [VMEM] * 2, "pack")(side, near)
    far = swap(packed, FAR)

    all_bound = lax.all_gather(arrived, DEV, axis=0, tiled=True)
    output = call(
        forward_kernel, shape((2, TILE, width), BF16), [SMEM] * 3 + [VMEM] * 4, "forward",
        [pltpu.VMEM((2, TILE, width), F32)],
    )(tile_count, tile_src, tile_dst, tiles, all_own.reshape(blocked), all_bound.reshape(blocked), weight)

    spread = call(far_kernel, shape((CHUNKS, 8, 128), F32), [VMEM, ANY], "far")(far, output)
    grad_weight = swap(spread, NEAR).reshape(width // 8, 2, 8, 128).transpose(0, 2, 1, 3).reshape(width, width)
    grad_features = call(back_kernel, shape((rows, width), F32), [VMEM] * 5, "back")(
        send_rows, send_count, own, far, weight)
    return output.reshape(rows, width), grad_features, grad_weight


def solution(mesh):
    fine = Mesh(mesh.devices.reshape(SIZES), AXES)
    split = [P(AXES)] * 7
    return jax.shard_map(
        per_device,
        mesh=fine,
        in_specs=(*split, P(), P(AXES)),
        out_specs=(P(AXES), P(AXES), P()),
        check_vma=False,
    )
```

time: 179 us -> 179 us (level)
  starting transfers between devices: 89.7 us -> 76.6 us
  blocking collectives: 9.32 us -> 16.5 us
  waiting for transfers between devices: 45.2 us -> 50.2 us
  Pallas kernels: 9.83 us -> 13.1 us
  local copies, waits for them, and re-layouts: 8.45 us -> 5.69 us
    all_gather x1 -> x2, waiting for transfers between devices: 0.01 us -> 14.3 us  [the longest x1 14.3 us: per_device(): all_bound = lax.all_gather(arrived, DEV, axis=0, tiled=True)]
    ppermute x8 -> x4, starting transfers between devices: 39.4 us -> 25.8 us  [shift(): return lax.ppermute(x, axis, [(i, (i + step) % size) for i in range(size)])]
    ppermute x8 -> x4, waiting for transfers between devices: 7.24 us -> 0.01 us  [shift(): return lax.ppermute(x, axis, [(i, (i + step) % size) for i in range(size)])]
    all_to_all x1, blocking collectives: 9.32 us -> 16.5 us  [swap(): return lax.all_to_all(x, axes, split_axis=0, concat_axis=0, tiled=True)]
    all_to_all x4, waiting for transfers between devices: 37.2 us -> 34.4 us  [swap(): return lax.all_to_all(x, axes, split_axis=0, concat_axis=0, tiled=True)]
    pallas_call x5 -> x6, Pallas kernels: 5.36 us -> 7.42 us  [the longest x1 2.61 us: per_device(): call(forward_kernel, shape((2, TILE, width), BF16), [SMEM] * 3 + [VMEM] *...]
  transfers between devices with their start and end apart: 13 -> 10, of which waited for: 8 -> 5; matrix products, arithmetic and copies ran while one was open for 2% -> 0% of each run, Pallas kernels for 3% -> 6%
where the time goes in v3:
time: 179 us; the launch traced here: 177 us
  starting transfers between devices  76.6 us (43%)
  waiting for transfers between devices  50.2 us (28%)
  blocking collectives  16.5 us (9%)
  between operations  14.8 us (8%)
  Pallas kernels  13.1 us (7%)
  local copies, waits for them, and re-layouts  5.69 us (3%)
    all_to_all x4, starting transfers between devices, swap(): return lax.all_to_all(x, axes, split_axis=0, concat_axis=0, tiled=True)  50.7 us
    all_to_all x4, waiting for transfers between devices, swap(): return lax.all_to_all(x, axes, split_axis=0, concat_axis=0, tiled=True)  34.4 us
    ppermute x4, starting transfers between devices, shift(): return lax.ppermute(x, axis, [(i, (i + step) % size) for i in range(size)])  25.8 us
    all_to_all x1, blocking collectives, swap(): return lax.all_to_all(x, axes, split_axis=0, concat_axis=0, tiled=True)  16.5 us
    all_gather x1, waiting for transfers between devices, per_device(): all_bound = lax.all_gather(arrived, DEV, axis=0, tiled=True)  14.3 us
    unnamed x27, local copies, waits for them, and re-layouts  5.69 us
  transfers between devices with their start and end apart: 10, of which 5 were waited for; matrix products, arithmetic and copies ran while one was open for 0% of the time, Pallas kernels for 6%

profile of v3, /device:TPU:1, one launch (start us, length us, event | category | flops | bytes accessed | tf_op | source)
XLA Modules:
  0.0 177.0 jit_solution(10426449970029030328)
XLA Ops:
  9.3 0.9 copy-done.4
  10.3 3.6 %terms.1 = (bf16[4,4,128,256]{3,2,1,0:T(8,128)(2,1)S(1)}, bf16[4,4,128,256]{3,2,1,0:T(8,128)(2,1)}) custom-call(s32[2]{0:T(128)S(1)} %pad_add_fusion.place_ref, s32[1]{0:T(128)S(6)} %copy.13.count_ref, s32[8]{0:T(128)S(1)} %copy-done.11, s32[8]{0:T(128)S(1)} %copy-done.12, bf16[8,128,128]{2,1,0:T(8,128)(2,1)S(1)} %copy-done.4, bf16[2,128,256]{2,1,0:T(8,128)(2,1)S(1)} %bitcast.17), custom_call_target="tpu_custom_call" | custom-call | tf_op jit(solution)/shard_map/terms/pallas_call | solution.py:227
  13.8 14.9 %collective-permute-start = (bf16[4,4,128,256]{3,2,1,0:T(8,128)(2,1)}, bf16[4,4,128,256]{3,2,1,0:T(8,128)(2,1)S(1)}, u32[]{:S(2)}, u32[]{:S(2)}) collective-permute-start(bf16[4,4,128,256]{3,2,1,0:T(8,128)(2,1)} %get-tuple-element.16), channel_id=1, source_target_pairs={{0,1},{1,0},{2,3},{3,2},{4,5},{5,4},{6,7},{7,6},{8,9},{9,8},{10,11... | collective-permute-start | bytes 3145736 | tf_op jit(solution)/shard_map/ppermute | solution.py:32
  28.8 1.1 pick.1
  29.9 15.5 %all-to-all-start = ((bf16[16,16,256]{2,1,0:T(8,128)(2,1)}), bf16[16,16,256]{2,1,0:T(8,128)(2,1)S(1)}, u32[]{:S(2)}, u32[]{:S(2)}) async-start(bf16[16,16,256]{2,1,0:T(8,128)(2,1)} %pick.1), calls=%async_computation | async-start | bytes 262144 | tf_op jit(solution)/shard_map/all_to_all | solution.py:28
  45.5 1.4 pair.1
  46.9 4.4 %collective-permute-start.1 = (bf16[4,128,256]{2,1,0:T(8,128)(2,1)}, bf16[4,128,256]{2,1,0:T(8,128)(2,1)S(1)}, u32[]{:S(2)}, u32[]{:S(2)}) collective-permute-start(bf16[4,128,256]{2,1,0:T(8,128)(2,1)} %get-tuple-element.18), channel_id=1, source_target_pairs={{0,2},{2,4},{4,6},{6,0},{1,3},{3,5},{5,7},{7,1},{8,10},{10,12},{12... | collective-permute-start | bytes 786440 | tf_op jit(solution)/shard_map/ppermute | solution.py:32
  51.3 4.5 %collective-permute-start.2 = (bf16[4,128,256]{2,1,0:T(8,128)(2,1)S(1)}, bf16[4,128,256]{2,1,0:T(8,128)(2,1)S(1)}, u32[]{:S(2)}, u32[]{:S(2)}) collective-permute-start(bf16[4,128,256]{2,1,0:T(8,128)(2,1)S(1)} %get-tuple-element.19), channel_id=1, source_target_pairs={{0,4},{2,6},{4,0},{6,2},{1,5},{3,7},{5,1},{7,3},{8,12},{10,14},{12... | collective-permute-start | bytes 786440 | tf_op jit(solution)/shard_map/ppermute | solution.py:32
  55.8 1.9 %collective-permute-start.3 = (bf16[4,128,256]{2,1,0:T(8,128)(2,1)S(1)}, bf16[4,128,256]{2,1,0:T(8,128)(2,1)S(1)}, u32[]{:S(2)}, u32[]{:S(2)}) collective-permute-start(bf16[4,128,256]{2,1,0:T(8,128)(2,1)S(1)} %get-tuple-element.20), channel_id=1, source_target_pairs={{0,6},{2,0},{4,2},{6,4},{1,7},{3,1},{5,3},{7,5},{8,14},{10,8},{12,... | collective-permute-start | bytes 786440 | tf_op jit(solution)/shard_map/ppermute | solution.py:32
  57.8 10.5 %all-to-all-done.far_ref = bf16[16,16,256]{2,1,0:T(8,128)(2,1)S(1)} async-done(((bf16[16,16,256]{2,1,0:T(8,128)(2,1)}), bf16[16,16,256]{2,1,0:T(8,128)(2,1)S(1)}, u32[]{:S(2)}, u32[]{:S(2)}) %all-to-all-start) | async-done | bytes 131104 | tf_op jit(solution)/shard_map/all_to_all | solution.py:28
  68.4 1.2 copy-done
  70.0 16.5 %all_to_all.25.side_ref = bf16[8,64,256]{2,1,0:T(8,128)(2,1)S(1)} all-to-all(bf16[8,64,256]{2,1,0:T(8,128)(2,1)S(1)} %get-tuple-element.24), channel_id=1, replica_groups=mesh['x'=4,'zh'=16,'zl'=2,'y'=4,'core'=2] {'x','zl'}, dimensions={0} | all-to-all | bytes 524288 | tf_op jit(solution)/shard_map/all_to_all | solution.py:28
  86.5 1.1 mid.1
  87.6 6.6 %all-to-all-start.2 = ((f32[64,8,128]{2,1,0:T(8,128)}), f32[64,8,128]{2,1,0:T(8,128)S(1)}, u32[]{:S(2)}, u32[]{:S(2)}) async-start(f32[64,8,128]{2,1,0:T(8,128)} %get-tuple-element.26), calls=%async_computation.2 | async-start | bytes 524288 | tf_op jit(solution)/shard_map/all_to_all | solution.py:28
  95.0 9.2 %all-to-all-done.2.near_ref = f32[64,8,128]{2,1,0:T(8,128)S(1)} async-done(((f32[64,8,128]{2,1,0:T(8,128)}), f32[64,8,128]{2,1,0:T(8,128)S(1)}, u32[]{:S(2)}, u32[]{:S(2)}) %all-to-all-start.2) | async-done | bytes 262176 | tf_op jit(solution)/shard_map/all_to_all | solution.py:28
  104.2 0.9 pack.1
  105.1 16.6 %all-to-all-start.3 = ((bf16[16,24,256]{2,1,0:T(8,128)(2,1)}), bf16[16,24,256]{2,1,0:T(8,128)(2,1)S(1)}, u32[]{:S(2)}, u32[]{:S(2)}) async-start(bf16[16,24,256]{2,1,0:T(8,128)(2,1)} %pack.1), calls=%async_computation.3 | async-start | bytes 393216 | tf_op jit(solution)/shard_map/all_to_all | solution.py:28
  121.7 14.3 %all-gather.5.cloned.1.call-done = bf16[2048,256]{1,0:T(8,128)(2,1)} async-done(((bf16[256,256]{1,0:T(8,128)(2,1)}), bf16[2048,256]{1,0:T(8,128)(2,1)}) %all-gather.5.cloned.1.call-update) | async-done | bytes 1048592 | tf_op jit(solution)/shard_map/all_gather | solution.py:250
  136.1 1.2 copy-done.3
  137.3 2.6 %forward.1.done_ref = bf16[2,128,256]{2,1,0:T(8,128)(2,1)} custom-call(s32[1]{0:T(128)S(6)} %copy.13.count_ref, s32[8]{0:T(128)S(1)} %copy-done.11, s32[8]{0:T(128)S(1)} %copy-done.12, bf16[8,128,128]{2,1,0:T(8,128)(2,1)S(1)} %copy-done.5, bf16[16,128,256]{2,1,0:T(8,128)(2,1)S(1)} %bitcast.14, bf16[16,128,256]{2,1,0:T(8,128)(2,1)S(1)} %bitcast.15, ...), custom_call_target="tpu_custom_call" | custom-call | tf_op jit(solution)/shard_map/forward/pallas_call | solution.py:251
  139.9 6.1 %all-to-all-done.3.far_ref = bf16[16,24,256]{2,1,0:T(8,128)(2,1)S(1)} async-done(((bf16[16,24,256]{2,1,0:T(8,128)(2,1)}), bf16[16,24,256]{2,1,0:T(8,128)(2,1)S(1)}, u32[]{:S(2)}, u32[]{:S(2)}) %all-to-all-start.3) | async-done | bytes 196640 | tf_op jit(solution)/shard_map/all_to_all | solution.py:28
  147.6 12.0 %all-to-all-start.4 = ((f32[64,8,128]{2,1,0:T(8,128)}), f32[64,8,128]{2,1,0:T(8,128)S(1)}, u32[]{:S(2)}, u32[]{:S(2)}) async-start(f32[64,8,128]{2,1,0:T(8,128)} %far.1), calls=%async_computation.4 | async-start | bytes 524288 | tf_op jit(solution)/shard_map/all_to_all | solution.py:28
  159.6 1.2 back.1
  160.8 8.6 %all-to-all-done.4 = f32[64,8,128]{2,1,0:T(8,128)S(1)} async-done(((f32[64,8,128]{2,1,0:T(8,128)}), f32[64,8,128]{2,1,0:T(8,128)S(1)}, u32[]{:S(2)}, u32[]{:S(2)}) %all-to-all-start.4) | async-done | bytes 262176 | tf_op jit(solution)/shard_map/all_to_all | solution.py:28
  (36 shorter events, 5.1 us)
Async XLA Ops:
  7.2 1.5 copy-start.8
  7.2 61.2 %all-gather.3.cloned.1.call-start = ((), (), s32[]{:S(2)}) async-start(), calls=%async_computation.5 | async-start | bytes 1179648 | tf_op jit(solution)/shard_map/all_gather | solution.py:223
  8.6 0.7 copy-start.11
  8.6 0.7 copy-start.12
  9.3 0.9 copy-start.4
  10.3 18.5 %copy-start.2 = (bf16[256,256]{1,0:T(8,128)(2,1)S(1)}, bf16[256,256]{1,0:T(8,128)(2,1)}, u32[]{:S(2)}) copy-start(bf16[256,256]{1,0:T(8,128)(2,1)} %features_ref.3) | copy-start | bytes 393220
  13.8 15.0 %copy-start.9 = (s32[1,128,2]{1,2,0:T(2,128)S(1)}, s32[1,128,2]{1,2,0:T(2,128)}, u32[]{:S(2)}) copy-start(s32[1,128,2]{1,2,0:T(2,128)} %param.14) | copy-start | bytes 3076
  13.8 15.0 %copy-start.10 = (s32[1,128]{1,0:T(1,128)S(1)}, s32[1,128]{1,0:T(1,128)}, u32[]{:S(2)}) copy-start(s32[1,128]{1,0:T(1,128)} %count_ref.5) | copy-start | bytes 1540
  13.8 31.6 %collective-permute-start = (bf16[4,4,128,256]{3,2,1,0:T(8,128)(2,1)}, bf16[4,4,128,256]{3,2,1,0:T(8,128)(2,1)S(1)}, u32[]{:S(2)}, u32[]{:S(2)}) collective-permute-start(bf16[4,4,128,256]{3,2,1,0:T(8,128)(2,1)} %get-tuple-element.16), channel_id=1, source_target_pairs={{0,1},{1,0},{2,3},{3,2},{4,5},{5,4},{6,7},{7,6},{8,9},{9,8},{10,11... | collective-permute-start | bytes 3145736 | tf_op jit(solution)/shard_map/ppermute | solution.py:32
  29.9 38.4 %all-to-all-start = ((bf16[16,16,256]{2,1,0:T(8,128)(2,1)}), bf16[16,16,256]{2,1,0:T(8,128)(2,1)S(1)}, u32[]{:S(2)}, u32[]{:S(2)}) async-start(bf16[16,16,256]{2,1,0:T(8,128)(2,1)} %pick.1), calls=%async_computation | async-start | bytes 262144 | tf_op jit(solution)/shard_map/all_to_all | solution.py:28
  46.9 21.5 %collective-permute-start.1 = (bf16[4,128,256]{2,1,0:T(8,128)(2,1)}, bf16[4,128,256]{2,1,0:T(8,128)(2,1)S(1)}, u32[]{:S(2)}, u32[]{:S(2)}) collective-permute-start(bf16[4,128,256]{2,1,0:T(8,128)(2,1)} %get-tuple-element.18), channel_id=1, source_target_pairs={{0,2},{2,4},{4,6},{6,0},{1,3},{3,5},{5,7},{7,1},{8,10},{10,12},{12... | collective-permute-start | bytes 786440 | tf_op jit(solution)/shard_map/ppermute | solution.py:32
  51.3 17.0 %collective-permute-start.2 = (bf16[4,128,256]{2,1,0:T(8,128)(2,1)S(1)}, bf16[4,128,256]{2,1,0:T(8,128)(2,1)S(1)}, u32[]{:S(2)}, u32[]{:S(2)}) collective-permute-start(bf16[4,128,256]{2,1,0:T(8,128)(2,1)S(1)} %get-tuple-element.19), channel_id=1, source_target_pairs={{0,4},{2,6},{4,0},{6,2},{1,5},{3,7},{5,1},{7,3},{8,12},{10,14},{12... | collective-permute-start | bytes 786440 | tf_op jit(solution)/shard_map/ppermute | solution.py:32
  55.8 12.5 %collective-permute-start.3 = (bf16[4,128,256]{2,1,0:T(8,128)(2,1)S(1)}, bf16[4,128,256]{2,1,0:T(8,128)(2,1)S(1)}, u32[]{:S(2)}, u32[]{:S(2)}) collective-permute-start(bf16[4,128,256]{2,1,0:T(8,128)(2,1)S(1)} %get-tuple-element.20), channel_id=1, source_target_pairs={{0,6},{2,0},{4,2},{6,4},{1,7},{3,1},{5,3},{7,5},{8,14},{10,8},{12,... | collective-permute-start | bytes 786440 | tf_op jit(solution)/shard_map/ppermute | solution.py:32
  68.4 1.2 copy-start
  87.6 48.4 %copy-start.1 = (bf16[2048,256]{1,0:T(8,128)(2,1)S(1)}, bf16[2048,256]{1,0:T(8,128)(2,1)}, u32[]{:S(2)}) copy-start(bf16[2048,256]{1,0:T(8,128)(2,1)} %all-gather.3.cloned.1.call-done.done_ref) | copy-start | bytes 3145732
  87.6 16.5 %all-to-all-start.2 = ((f32[64,8,128]{2,1,0:T(8,128)}), f32[64,8,128]{2,1,0:T(8,128)S(1)}, u32[]{:S(2)}, u32[]{:S(2)}) async-start(f32[64,8,128]{2,1,0:T(8,128)} %get-tuple-element.26), calls=%async_computation.2 | async-start | bytes 524288 | tf_op jit(solution)/shard_map/all_to_all | solution.py:28
  94.3 41.8 %all-gather.5.cloned.1.call-start = ((), (), s32[]{:S(2)}) async-start(), calls=%async_computation.6 | async-start | bytes 1179648 | tf_op jit(solution)/shard_map/all_gather | solution.py:250
  105.1 31.0 %copy-start.5 = (bf16[8,128,128]{2,1,0:T(8,128)(2,1)S(1)}, bf16[8,128,128]{2,1,0:T(8,128)(2,1)}, u32[]{:S(2)}) copy-start(bf16[8,128,128]{2,1,0:T(8,128)(2,1)} %tiles_ref.3) | copy-start | bytes 786436
  105.1 31.0 %copy-start.6 = (bf16[256,256]{1,0:T(8,128)(2,1)S(1)}, bf16[256,256]{1,0:T(8,128)(2,1)}, u32[]{:S(2)}) copy-start(bf16[256,256]{1,0:T(8,128)(2,1)} %weight_ref.3) | copy-start | bytes 393220
  105.1 40.9 %all-to-all-start.3 = ((bf16[16,24,256]{2,1,0:T(8,128)(2,1)}), bf16[16,24,256]{2,1,0:T(8,128)(2,1)S(1)}, u32[]{:S(2)}, u32[]{:S(2)}) async-start(bf16[16,24,256]{2,1,0:T(8,128)(2,1)} %pack.1), calls=%async_computation.3 | async-start | bytes 393216 | tf_op jit(solution)/shard_map/all_to_all | solution.py:28
  136.0 1.2 copy-start.3
  146.0 0.9 copy-start.7
  147.6 21.8 %all-to-all-start.4 = ((f32[64,8,128]{2,1,0:T(8,128)}), f32[64,8,128]{2,1,0:T(8,128)S(1)}, u32[]{:S(2)}, u32[]{:S(2)}) async-start(f32[64,8,128]{2,1,0:T(8,128)} %far.1), calls=%async_computation.4 | async-start | bytes 524288 | tf_op jit(solution)/shard_map/all_to_all | solution.py:28
Sparse Core Ops, SparseCore 0:
  10.7 51.2 all-gather.2
  98.4 37.5 all-gather.4

commit v4 on v3

v4 whole, which is shorter than its diff:
```python
import jax
import jax.numpy as jnp
from jax import lax
from jax.experimental import pallas as pl
from jax.experimental.pallas import tpu as pltpu
from jax.sharding import Mesh, PartitionSpec as P

AXES = ("x", "zh", "zl", "y", "core")
SIZES = (4, 16, 2, 4, 2)
SLOTS = 2
X, ZH, ZL, Y, CORE = SIZES
DEV = ("y", "core")
SIDE = ("x", "zl")
NEAR = ("x", "zl", "y", "core")
FAR = "zh"
TILE = 128
NT = 8
CHUNKS = 64
SRC = 3
DST = SRC + NT

F32 = jnp.float32
BF16 = jnp.bfloat16
SMEM = pl.BlockSpec(memory_space=pltpu.SMEM)
VMEM = pl.BlockSpec(memory_space=pltpu.VMEM)


def swap(x, axes):
    return lax.all_to_all(x, axes, split_axis=0, concat_axis=0, tiled=True)


def shift(x, axis, step, size):
    return lax.ppermute(x, axis, [(i, (i + step) % size) for i in range(size)])


def dot(a, b, da=1, db=0):
    return lax.dot_general(a, b, (((da,), (db,)), ((), ())), preferred_element_type=F32)


def halves(x):
    high = x.astype(BF16)
    return high, (x - high.astype(F32)).astype(BF16)


def call(kernel, out_shape, in_specs, name, scratch=(), mebibytes=24):
    out_specs = (VMEM,) * len(out_shape) if isinstance(out_shape, tuple) else VMEM
    return pl.pallas_call(
        kernel, out_shape=out_shape, in_specs=in_specs, out_specs=out_specs,
        scratch_shapes=scratch, name=name,
        compiler_params=pltpu.CompilerParams(vmem_limit_bytes=mebibytes * 1024 * 1024),
    )


def digits(count, dim, sizes):
    left = lax.broadcasted_iota(jnp.int32, (count, count), dim)
    found = []
    for size in reversed(sizes):
        found.append(lax.rem(left, size))
        left = lax.div(left, size)
    return found[::-1]


def boundary_row(x, zh, zl, s):
    return ((x * ZH + zh) * ZL + zl) * SLOTS + s


def permutation(match):
    return match.astype(F32).astype(BF16)


def picks(rows, rows_ref, count_ref):
    groups = count_ref.shape[1]
    places = lax.broadcasted_iota(jnp.int32, (rows, groups), 0)
    found = []
    for slot in range(SLOTS):
        live = count_ref[...] > slot
        wanted = jnp.where(live, rows_ref[slot:slot + 1, :], -1)
        found.append(permutation(places == wanted))
    count = groups * SLOTS
    zh, x, zl, s = digits(count, 1, (ZH, X, ZL, SLOTS))
    order = permutation(s * groups + (x * ZH + zh) * ZL + zl == lax.broadcasted_iota(jnp.int32, (count, count), 0))
    return dot(jnp.concatenate(found, axis=1), order).astype(BF16)


def pick_kernel(rows_ref, count_ref, features_ref, out_ref):
    wanted = picks(features_ref.shape[0], rows_ref, count_ref)
    out_ref[...] = dot(wanted, features_ref[...], 0, 0).astype(BF16).reshape(out_ref.shape)


def terms_kernel(meta_ref, tiles_ref, cot_ref, mine_ref, other_ref, acc_ref):
    live, core = meta_ref[0], meta_ref[2]
    mine_ref[...] = jnp.zeros(mine_ref.shape, BF16)
    other_ref[...] = jnp.zeros(other_ref.shape, BF16)
    for k in range(NT):
        @pl.when(k < live)
        def _():
            acc_ref[meta_ref[SRC + k]] = jnp.zeros(acc_ref.shape[1:], F32)
    for k in range(NT):
        @pl.when(k < live)
        def _():
            acc_ref[meta_ref[SRC + k]] += dot(tiles_ref[k], cot_ref[meta_ref[DST + k]], 0, 0)
    for k in range(NT):
        block = meta_ref[SRC + k]
        member = lax.div(lax.rem(block, 16), 2)
        y = lax.div(member, 2)
        part = lax.rem(block, 2) + 2 * lax.div(block, 16)
        same = lax.rem(member, 2) == core

        @pl.when((k < live) & same)
        def _():
            mine_ref[y, part] = acc_ref[block].astype(BF16)

        @pl.when((k < live) & jnp.logical_not(same))
        def _():
            other_ref[y, part] = acc_ref[block].astype(BF16)


def pair_kernel(meta_ref, mine_ref, came_ref, keep_ref, *out_refs):
    y = meta_ref[1]
    keep_ref[...] = mine_ref[y].astype(F32) + came_ref[y].astype(F32)
    for step, out_ref in enumerate(out_refs, 1):
        to = lax.rem(y + step, Y)
        out_ref[...] = (mine_ref[to].astype(F32) + came_ref[to].astype(F32)).astype(BF16)


def side_kernel(keep_ref, came1_ref, came2_ref, came3_ref, far_ref, own_ref, high_ref, low_ref, out_ref):
    terms = keep_ref[...]
    for came_ref in (came1_ref, came2_ref, came3_ref):
        terms += came_ref[...].astype(F32)
    own_ref[...] = terms[:2].reshape(2 * TILE, -1)
    bound = terms[2:].reshape(2 * TILE, -1)
    rows, width = bound.shape
    column = lax.broadcasted_iota(jnp.int32, (rows, rows), 1)
    x, zl, zh, s = digits(rows, 0, (X, ZL, ZH, SLOTS))
    lines = rows // (X * ZL)
    order = permutation(((zh * X + x) * ZL + zl) * SLOTS + s == column)
    rows_out = dot(order, far_ref[...].reshape(rows, width)).astype(BF16)
    out_ref[:, :lines, :] = rows_out.reshape(X * ZL, lines, width)
    order = permutation(boundary_row(x, zh, zl, s) == column)
    high, low = halves(bound)
    high = dot(order, high).astype(BF16)
    high_ref[...] = high
    low_ref[...] = dot(order, low).astype(BF16)
    out_ref[:, lines:, :] = high.reshape(X * ZL, lines, width)


def mid_kernel(own_ref, high_ref, low_ref, side_ref, features_ref, gw_ref, both_ref):
    rows, width = own_ref.shape
    features = features_ref[...]
    arrived = side_ref[:, :rows // (X * ZL), :].reshape(rows, width)
    own_high, own_low = halves(own_ref[...])
    gw = (dot(features, own_high, 0, 0) + dot(features, own_low, 0, 0)
          + dot(arrived, high_ref[...], 0, 0) + dot(arrived, low_ref[...], 0, 0))
    for c in range(CHUNKS):
        row, col = c // 2 * 8, c % 2 * 128
        gw_ref[c] = gw[row:row + 8, col:col + 128]
    x, zl, zh, s = digits(rows, 1, (X, ZL, ZH, SLOTS))
    order = permutation(boundary_row(x, zh, zl, s) == lax.broadcasted_iota(jnp.int32, (rows, rows), 0))
    both_ref[:rows, :] = features
    both_ref[rows:, :] = dot(order, arrived).astype(BF16)


def pack_kernel(side_ref, near_ref, out_ref):
    lines = out_ref.shape[1] // 2 - 4
    rows = ZH * lines
    zh, x, zl, s = digits(rows, 0, (ZH, X, ZL, SLOTS))
    order = permutation(((x * ZL + zl) * ZH + zh) * SLOTS + s == lax.broadcasted_iota(jnp.int32, (rows, rows), 1))
    side = dot(order, side_ref[:, rows // (X * ZL):, :].reshape(rows, -1)).astype(BF16)
    out_ref[:, :lines, :] = side[:, :128].reshape(ZH, lines, 128)
    out_ref[:, lines:2 * lines, :] = side[:, 128:].reshape(ZH, lines, 128)
    near = jnp.sum(near_ref[...], axis=0).astype(BF16)
    for z in range(ZH):
        out_ref[z, 2 * lines:, :] = near


def far_kernel(far_ref, token_ref, out_ref):
    del token_ref
    total = jnp.sum(far_ref[:, far_ref.shape[1] - 8:, :].astype(F32), axis=0)
    out_ref[...] = jnp.broadcast_to(total[None], out_ref.shape)


def back_kernel(rows_ref, count_ref, own_ref, far_ref, weight_ref, out_ref):
    rows = own_ref.shape[0]
    lines = far_ref.shape[1] // 2 - 4
    left = far_ref[:, :lines, :].reshape(ZH * lines, 128)
    right = far_ref[:, lines:2 * lines, :].reshape(ZH * lines, 128)
    total = own_ref[...] + dot(picks(rows, rows_ref, count_ref), jnp.concatenate([left, right], axis=1))
    high, low = halves(total)
    weight = weight_ref[...]
    out_ref[...] = dot(high, weight, 1, 1) + dot(low, weight, 1, 1)


def forward_kernel(meta_ref, tiles_ref, source_ref, weight_ref, out_ref, token_ref, acc_ref):
    live = meta_ref[0]
    token_ref[...] = jnp.zeros(token_ref.shape, F32)
    acc_ref[...] = jnp.zeros(acc_ref.shape, F32)
    for k in range(NT):
        @pl.when(k < live)
        def _():
            block = meta_ref[SRC + k]
            member = lax.div(lax.rem(block, 16), 2)
            part = lax.rem(block, 2) + 2 * lax.div(block, 16)
            acc_ref[meta_ref[DST + k]] += dot(tiles_ref[k], source_ref[member, part])
    for t in range(2):
        out_ref[t] = dot(acc_ref[t].astype(BF16), weight_ref[...]).astype(BF16)


def per_device(
    features, tiles, tile_dst, tile_src, tile_count, send_rows, send_count, weight, cotangent
):
    rows, width = features.shape
    groups, slots = send_rows.shape[1:]
    lines = groups * slots // ZH
    shape = jax.ShapeDtypeStruct
    places = jnp.stack([lax.axis_index("y"), lax.axis_index("core")])
    meta = jnp.concatenate([tile_count, places, tile_src, tile_dst])
    send_rows = send_rows.transpose(0, 2, 1).reshape(slots, groups)

    part = shape((4, TILE, width), BF16)
    half = shape((Y, 4, TILE, width), BF16)
    mine, other = call(
        terms_kernel, (half, half), [SMEM] + [VMEM] * 2, "terms", [pltpu.VMEM((32, TILE, width), F32)], 60,
    )(meta, tiles, cotangent.reshape(2, TILE, width))
    came = shift(other, "core", 1, CORE)
    outgoing = call(pick_kernel, shape((ZH, lines, width), BF16), [VMEM] * 3, "pick", (), 60)(
        send_rows, send_count, features)
    landed = swap(outgoing, FAR)
    keep, *sent = call(
        pair_kernel, (shape((4, TILE, width), F32), part, part, part), [SMEM] + [VMEM] * 2, "pair", (), 60,
    )(meta, mine, came)
    came = [shift(block, "y", step, Y) for step, block in enumerate(sent, 1)]

    square = shape((rows, width), BF16)
    own, high, low, side = call(
        side_kernel,
        (shape((rows, width), F32), square, square, shape((X * ZL, 2 * rows // (X * ZL), width), BF16)),
        [VMEM] * 5, "side",
    )(keep, *came, landed)
    side = swap(side, SIDE)
    gw, both = call(
        mid_kernel, (shape((CHUNKS, 8, 128), F32), shape((2 * rows, width), BF16)), [VMEM] * 5, "mid",
    )(own, high, low, side, features)
    near = swap(gw, NEAR)
    packed = call(pack_kernel, shape((ZH, 2 * lines + 8, 128), BF16), [VMEM] * 2, "pack")(side, near)
    far = swap(packed, FAR)

    source = lax.all_gather(both, DEV, axis=0, tiled=True).reshape(Y * CORE, 4, TILE, width)
    output, token = call(
        forward_kernel, (shape((2, TILE, width), BF16), shape((8, 128), F32)), [SMEM] + [VMEM] * 3, "forward",
        [pltpu.VMEM((2, TILE, width), F32)],
    )(meta, tiles, source, weight)

    spread = call(far_kernel, shape((CHUNKS, 8, 128), F32), [VMEM] * 2, "far")(far, token)
    grad_weight = swap(spread, NEAR).reshape(width // 8, 2, 8, 128).transpose(0, 2, 1, 3).reshape(width, width)
    grad_features = call(back_kernel, shape((rows, width), F32), [VMEM] * 5, "back")(
        send_rows, send_count, own, far, weight)
    return output.reshape(rows, width), grad_features, grad_weight


def solution(mesh):
    fine = Mesh(mesh.devices.reshape(SIZES), AXES)
    split = [P(AXES)] * 7
    return jax.shard_map(
        per_device,
        mesh=fine,
        in_specs=(*split, P(), P(AXES)),
        out_specs=(P(AXES), P(AXES), P()),
        check_vma=False,
    )
```

time: 179 us -> 175 us (0.978); the launches traced: 177 us -> 175 us
  blocking collectives: 16.5 us -> 34.4 us
  waiting for transfers between devices: 50.2 us -> 35.8 us
  starting transfers between devices: 76.6 us -> 70.1 us
    all_to_all x1 -> x2, blocking collectives: 16.5 us -> 34.4 us  [swap(): return lax.all_to_all(x, axes, split_axis=0, concat_axis=0, tiled=True)]
    all_gather x2 -> x1, waiting for transfers between devices: 14.3 us -> 3.96 us  [per_device(): lax.all_gather(both, DEV, axis=0, tiled=True)]
    all_to_all x4 -> x3, starting transfers between devices: 50.7 us -> 44.3 us  [swap(): return lax.all_to_all(x, axes, split_axis=0, concat_axis=0, tiled=True)]
    all_to_all x4 -> x3, waiting for transfers between devices: 34.4 us -> 31.4 us  [swap(): return lax.all_to_all(x, axes, split_axis=0, concat_axis=0, tiled=True)]
    unnamed x27 -> x19, local copies, waits for them, and re-layouts: 5.69 us -> 4.32 us
  transfers between devices with their start and end apart: 10 -> 8, of which waited for: 5 -> 5; matrix products, arithmetic and copies ran while one was open for 0% -> 0% of each run, Pallas kernels for 6% -> 5%
where the time goes in v4:
time: 175 us
  starting transfers between devices  70.1 us (40%)
  waiting for transfers between devices  35.8 us (20%)
  blocking collectives  34.4 us (20%)
  between operations  14.8 us (8%)
  Pallas kernels  14 us (8%)
  local copies, waits for them, and re-layouts  5.57 us (3%)
    all_to_all x3, starting transfers between devices, swap(): return lax.all_to_all(x, axes, split_axis=0, concat_axis=0, tiled=True)  44.3 us
    all_to_all x2, blocking collectives, swap(): return lax.all_to_all(x, axes, split_axis=0, concat_axis=0, tiled=True)  34.4 us
    all_to_all x3, waiting for transfers between devices, swap(): return lax.all_to_all(x, axes, split_axis=0, concat_axis=0, tiled=True)  31.4 us
    ppermute x4, starting transfers between devices, shift(): return lax.ppermute(x, axis, [(i, (i + step) % size) for i in range(size)])  25.7 us
    unnamed x19, local copies, waits for them, and re-layouts  4.32 us
    all_gather x1, waiting for transfers between devices, per_device(): lax.all_gather(both, DEV, axis=0, tiled=True)  3.96 us
  transfers between devices with their start and end apart: 8, of which 5 were waited for; matrix products, arithmetic and copies ran while one was open for 0% of the time, Pallas kernels for 5%

profile of v4, /device:TPU:1, one launch (start us, length us, event | category | flops | bytes accessed | tf_op | source)
XLA Modules:
  0.0 174.8 jit_solution(7254817366017529348)
XLA Ops:
  7.8 1.3 concatenate.3.meta_ref
  9.1 3.1 %terms.1 = (bf16[4,4,128,256]{3,2,1,0:T(8,128)(2,1)}, bf16[4,4,128,256]{3,2,1,0:T(8,128)(2,1)}) custom-call(s32[19]{0:T(128)} %concatenate.3.meta_ref, bf16[8,128,128]{2,1,0:T(8,128)(2,1)} %tiles_ref.3, bf16[2,128,256]{2,1,0:T(8,128)(2,1)} %bitcast.17), custom_call_target="tpu_custom_call" | custom-call | tf_op jit(solution)/shard_map/terms/pallas_call | solution.py:221
  12.2 15.8 %collective-permute-start = (bf16[4,4,128,256]{3,2,1,0:T(8,128)(2,1)}, bf16[4,4,128,256]{3,2,1,0:T(8,128)(2,1)S(1)}, u32[]{:S(2)}, u32[]{:S(2)}) collective-permute-start(bf16[4,4,128,256]{3,2,1,0:T(8,128)(2,1)} %get-tuple-element.18), channel_id=1, source_target_pairs={{0,1},{1,0},{2,3},{3,2},{4,5},{5,4},{6,7},{7,6},{8,9},{9,8},{10,11... | collective-permute-start | bytes 3145736 | tf_op jit(solution)/shard_map/ppermute | solution.py:33
  28.0 2.1 %pick.1 = bf16[16,16,256]{2,1,0:T(8,128)(2,1)} custom-call(s32[2,128]{1,0:T(2,128)} %bitcast.14, s32[1,128]{1,0:T(1,128)} %count_ref.3, bf16[256,256]{1,0:T(8,128)(2,1)} %features_ref.3), custom_call_target="tpu_custom_call" | custom-call | tf_op jit(solution)/shard_map/pick/pallas_call | solution.py:225
  30.1 16.3 %all-to-all-start = ((bf16[16,16,256]{2,1,0:T(8,128)(2,1)}), bf16[16,16,256]{2,1,0:T(8,128)(2,1)S(1)}, u32[]{:S(2)}, u32[]{:S(2)}) async-start(bf16[16,16,256]{2,1,0:T(8,128)(2,1)} %pick.1), calls=%async_computation | async-start | bytes 262144 | tf_op jit(solution)/shard_map/all_to_all | solution.py:29
  46.5 1.0 copy-done.8
  47.5 2.8 %pair.1 = (f32[4,128,256]{2,1,0:T(8,128)}, bf16[4,128,256]{2,1,0:T(8,128)(2,1)}, bf16[4,128,256]{2,1,0:T(8,128)(2,1)}, bf16[4,128,256]{2,1,0:T(8,128)(2,1)}) custom-call(s32[19]{0:T(128)} %concatenate.3.meta_ref, bf16[4,4,128,256]{3,2,1,0:T(8,128)(2,1)} %get-tuple-element.17.mine_ref, bf16[4,4,128,256]{3,2,1,0:T(8,128)(2,1)} %copy-done.8), custom_call_target="tpu_custom_call" | custom-call | tf_op jit(solution)/shard_map/pair/pallas_call | solution.py:228
  50.2 3.0 %collective-permute-start.1 = (bf16[4,128,256]{2,1,0:T(8,128)(2,1)}, bf16[4,128,256]{2,1,0:T(8,128)(2,1)S(1)}, u32[]{:S(2)}, u32[]{:S(2)}) collective-permute-start(bf16[4,128,256]{2,1,0:T(8,128)(2,1)} %get-tuple-element.20), channel_id=1, source_target_pairs={{0,2},{2,4},{4,6},{6,0},{1,3},{3,5},{5,7},{7,1},{8,10},{10,12},{12... | collective-permute-start | bytes 786440 | tf_op jit(solution)/shard_map/ppermute | solution.py:33
  53.2 4.5 %collective-permute-start.2 = (bf16[4,128,256]{2,1,0:T(8,128)(2,1)}, bf16[4,128,256]{2,1,0:T(8,128)(2,1)S(1)}, u32[]{:S(2)}, u32[]{:S(2)}) collective-permute-start(bf16[4,128,256]{2,1,0:T(8,128)(2,1)} %get-tuple-element.21), channel_id=1, source_target_pairs={{0,4},{2,6},{4,0},{6,2},{1,5},{3,7},{5,1},{7,3},{8,12},{10,14},{12... | collective-permute-start | bytes 786440 | tf_op jit(solution)/shard_map/ppermute | solution.py:33
  57.8 2.4 %collective-permute-start.3 = (bf16[4,128,256]{2,1,0:T(8,128)(2,1)}, bf16[4,128,256]{2,1,0:T(8,128)(2,1)S(1)}, u32[]{:S(2)}, u32[]{:S(2)}) collective-permute-start(bf16[4,128,256]{2,1,0:T(8,128)(2,1)} %get-tuple-element.22), channel_id=1, source_target_pairs={{0,6},{2,0},{4,2},{6,4},{1,7},{3,1},{5,3},{7,5},{8,14},{10,8},{12,... | collective-permute-start | bytes 786440 | tf_op jit(solution)/shard_map/ppermute | solution.py:33
  60.1 8.2 %all-to-all-done.far_ref = bf16[16,16,256]{2,1,0:T(8,128)(2,1)S(1)} async-done(((bf16[16,16,256]{2,1,0:T(8,128)(2,1)}), bf16[16,16,256]{2,1,0:T(8,128)(2,1)S(1)}, u32[]{:S(2)}, u32[]{:S(2)}) %all-to-all-start) | async-done | bytes 131104 | tf_op jit(solution)/shard_map/all_to_all | solution.py:29
  68.8 1.0 copy-done.3
  70.4 11.5 %all_to_all.25.side_ref = bf16[8,64,256]{2,1,0:T(8,128)(2,1)S(1)} all-to-all(bf16[8,64,256]{2,1,0:T(8,128)(2,1)S(1)} %get-tuple-element.26), channel_id=1, replica_groups=mesh['x'=4,'zh'=16,'zl'=2,'y'=4,'core'=2] {'x','zl'}, dimensions={0} | all-to-all | bytes 524288 | tf_op jit(solution)/shard_map/all_to_all | solution.py:29
  81.8 1.1 mid.1
  82.9 22.9 %all_to_all.26.near_ref = f32[64,8,128]{2,1,0:T(8,128)S(1)} all-to-all(f32[64,8,128]{2,1,0:T(8,128)S(1)} %get-tuple-element.29), channel_id=1, replica_groups=mesh['x'=4,'zh'=16,'zl'=2,'y'=4,'core'=2] {'x','zl','y','core'}, dimensions={0} | all-to-all | bytes 524288 | tf_op jit(solution)/shard_map/all_to_all | solution.py:29
  105.9 0.9 pack.1
  106.8 15.7 %all-to-all-start.3 = ((bf16[16,40,128]{2,1,0:T(8,128)(2,1)}), bf16[16,40,128]{2,1,0:T(8,128)(2,1)S(1)}, u32[]{:S(2)}, u32[]{:S(2)}) async-start(bf16[16,40,128]{2,1,0:T(8,128)(2,1)} %pack.1), calls=%async_computation.3 | async-start | bytes 327680 | tf_op jit(solution)/shard_map/all_to_all | solution.py:29
  122.5 4.0 %all-gather.2.cloned.1.call-done = bf16[4096,256]{1,0:T(8,128)(2,1)} async-done(((bf16[512,256]{1,0:T(8,128)(2,1)}), bf16[4096,256]{1,0:T(8,128)(2,1)}) %all-gather.2.cloned.1.call-update) | async-done | bytes 2097168 | tf_op jit(solution)/shard_map/all_gather | solution.py:247
  126.4 1.6 copy-done
  128.0 1.7 forward.1
  129.8 14.6 %all-to-all-done.3.far_ref = bf16[16,40,128]{2,1,0:T(8,128)(2,1)S(1)} async-done(((bf16[16,40,128]{2,1,0:T(8,128)(2,1)}), bf16[16,40,128]{2,1,0:T(8,128)(2,1)S(1)}, u32[]{:S(2)}, u32[]{:S(2)}) %all-to-all-start.3) | async-done | bytes 163872 | tf_op jit(solution)/shard_map/all_to_all | solution.py:29
  145.1 12.3 %all-to-all-start.4 = ((f32[64,8,128]{2,1,0:T(8,128)}), f32[64,8,128]{2,1,0:T(8,128)S(1)}, u32[]{:S(2)}, u32[]{:S(2)}) async-start(f32[64,8,128]{2,1,0:T(8,128)} %far.1), calls=%async_computation.4 | async-start | bytes 524288 | tf_op jit(solution)/shard_map/all_to_all | solution.py:29
  157.4 1.2 back.1
  158.6 8.6 %all-to-all-done.4 = f32[64,8,128]{2,1,0:T(8,128)S(1)} async-done(((f32[64,8,128]{2,1,0:T(8,128)}), f32[64,8,128]{2,1,0:T(8,128)S(1)}, u32[]{:S(2)}, u32[]{:S(2)}) %all-to-all-start.4) | async-done | bytes 262176 | tf_op jit(solution)/shard_map/all_to_all | solution.py:29
  (24 shorter events, 2.5 us)
Async XLA Ops:
  12.2 34.3 %collective-permute-start = (bf16[4,4,128,256]{3,2,1,0:T(8,128)(2,1)}, bf16[4,4,128,256]{3,2,1,0:T(8,128)(2,1)S(1)}, u32[]{:S(2)}, u32[]{:S(2)}) collective-permute-start(bf16[4,4,128,256]{3,2,1,0:T(8,128)(2,1)} %get-tuple-element.18), channel_id=1, source_target_pairs={{0,1},{1,0},{2,3},{3,2},{4,5},{5,4},{6,7},{7,6},{8,9},{9,8},{10,11... | collective-permute-start | bytes 3145736 | tf_op jit(solution)/shard_map/ppermute | solution.py:33
  30.1 38.3 %all-to-all-start = ((bf16[16,16,256]{2,1,0:T(8,128)(2,1)}), bf16[16,16,256]{2,1,0:T(8,128)(2,1)S(1)}, u32[]{:S(2)}, u32[]{:S(2)}) async-start(bf16[16,16,256]{2,1,0:T(8,128)(2,1)} %pick.1), calls=%async_computation | async-start | bytes 262144 | tf_op jit(solution)/shard_map/all_to_all | solution.py:29
  46.4 35.4 %copy-start.2 = (bf16[256,256]{1,0:T(8,128)(2,1)S(1)}, bf16[256,256]{1,0:T(8,128)(2,1)}, u32[]{:S(2)}) copy-start(bf16[256,256]{1,0:T(8,128)(2,1)} %features_ref.3) | copy-start | bytes 393220
  46.4 80.0 %all-gather.2.cloned.1.call-start = ((), (), s32[]{:S(2)}) async-start(), calls=%async_computation.5 | async-start | bytes 2359296 | tf_op jit(solution)/shard_map/all_gather | solution.py:247
  46.5 1.0 copy-start.8
  50.2 18.1 %collective-permute-start.1 = (bf16[4,128,256]{2,1,0:T(8,128)(2,1)}, bf16[4,128,256]{2,1,0:T(8,128)(2,1)S(1)}, u32[]{:S(2)}, u32[]{:S(2)}) collective-permute-start(bf16[4,128,256]{2,1,0:T(8,128)(2,1)} %get-tuple-element.20), channel_id=1, source_target_pairs={{0,2},{2,4},{4,6},{6,0},{1,3},{3,5},{5,7},{7,1},{8,10},{10,12},{12... | collective-permute-start | bytes 786440 | tf_op jit(solution)/shard_map/ppermute | solution.py:33
  53.2 15.1 %collective-permute-start.2 = (bf16[4,128,256]{2,1,0:T(8,128)(2,1)}, bf16[4,128,256]{2,1,0:T(8,128)(2,1)S(1)}, u32[]{:S(2)}, u32[]{:S(2)}) collective-permute-start(bf16[4,128,256]{2,1,0:T(8,128)(2,1)} %get-tuple-element.21), channel_id=1, source_target_pairs={{0,4},{2,6},{4,0},{6,2},{1,5},{3,7},{5,1},{7,3},{8,12},{10,14},{12... | collective-permute-start | bytes 786440 | tf_op jit(solution)/shard_map/ppermute | solution.py:33
  57.8 11.1 %collective-permute-start.3 = (bf16[4,128,256]{2,1,0:T(8,128)(2,1)}, bf16[4,128,256]{2,1,0:T(8,128)(2,1)S(1)}, u32[]{:S(2)}, u32[]{:S(2)}) collective-permute-start(bf16[4,128,256]{2,1,0:T(8,128)(2,1)} %get-tuple-element.22), channel_id=1, source_target_pairs={{0,6},{2,0},{4,2},{6,4},{1,7},{3,1},{5,3},{7,5},{8,14},{10,8},{12,... | collective-permute-start | bytes 786440 | tf_op jit(solution)/shard_map/ppermute | solution.py:33
  68.8 1.0 copy-start.3
  69.9 56.5 %copy-start.1 = (bf16[8,128,128]{2,1,0:T(8,128)(2,1)S(1)}, bf16[8,128,128]{2,1,0:T(8,128)(2,1)}, u32[]{:S(2)}) copy-start(bf16[8,128,128]{2,1,0:T(8,128)(2,1)} %tiles_ref.3) | copy-start | bytes 786436
  69.9 56.5 %copy-start.4 = (bf16[256,256]{1,0:T(8,128)(2,1)S(1)}, bf16[256,256]{1,0:T(8,128)(2,1)}, u32[]{:S(2)}) copy-start(bf16[256,256]{1,0:T(8,128)(2,1)} %weight_ref.3) | copy-start | bytes 393220
  69.9 56.5 %copy-start.5 = (s32[19]{0:T(128)S(1)}, s32[19]{0:T(128)}, u32[]{:S(2)}) copy-start(s32[19]{0:T(128)} %concatenate.3.meta_ref) | copy-start | bytes 232
  105.9 51.5 %copy-start.6 = (s32[1,128,2]{1,2,0:T(2,128)S(1)}, s32[1,128,2]{1,2,0:T(2,128)}, u32[]{:S(2)}) copy-start(s32[1,128,2]{1,2,0:T(2,128)} %param.14) | copy-start | bytes 3076
  105.9 51.6 %copy-start.7 = (s32[1,128]{1,0:T(1,128)S(1)}, s32[1,128]{1,0:T(1,128)}, u32[]{:S(2)}) copy-start(s32[1,128]{1,0:T(1,128)} %count_ref.3) | copy-start | bytes 1540
  106.8 37.6 %all-to-all-start.3 = ((bf16[16,40,128]{2,1,0:T(8,128)(2,1)}), bf16[16,40,128]{2,1,0:T(8,128)(2,1)S(1)}, u32[]{:S(2)}, u32[]{:S(2)}) async-start(bf16[16,40,128]{2,1,0:T(8,128)(2,1)} %pack.1), calls=%async_computation.3 | async-start | bytes 327680 | tf_op jit(solution)/shard_map/all_to_all | solution.py:29
  126.4 1.6 copy-start
  145.1 22.1 %all-to-all-start.4 = ((f32[64,8,128]{2,1,0:T(8,128)}), f32[64,8,128]{2,1,0:T(8,128)S(1)}, u32[]{:S(2)}, u32[]{:S(2)}) async-start(f32[64,8,128]{2,1,0:T(8,128)} %far.1), calls=%async_computation.4 | async-start | bytes 524288 | tf_op jit(solution)/shard_map/all_to_all | solution.py:29
Sparse Core Ops, SparseCore 0:
  83.1 43.3 all-gather.1

commit v5 on v4

--- a/solution.py
+++ b/solution.py
@@ -1,3 +1,5 @@
+import functools
+
 import jax
 import jax.numpy as jnp
 from jax import lax
@@ -15,6 +17,7 @@
 FAR = "zh"
 TILE = 128
 NT = 8
+PAIR = 24
 CHUNKS = 64
 SRC = 3
 DST = SRC + NT
@@ -22,6 +25,7 @@
 F32 = jnp.float32
 BF16 = jnp.bfloat16
 SMEM = pl.BlockSpec(memory_space=pltpu.SMEM)
+ANY = pl.BlockSpec(memory_space=pl.ANY)
 VMEM = pl.BlockSpec(memory_space=pltpu.VMEM)
 
 
@@ -103,19 +107,26 @@
         block = meta_ref[SRC + k]
         member = lax.div(lax.rem(block, 16), 2)
         y = lax.div(member, 2)
-        part = lax.rem(block, 2) + 2 * lax.div(block, 16)
+        kind, part = lax.div(block, 16), lax.rem(block, 2)
         same = lax.rem(member, 2) == core
 
         @pl.when((k < live) & same)
         def _():
-            mine_ref[y, part] = acc_ref[block].astype(BF16)
+            mine_ref[kind, y, part] = acc_ref[block].astype(BF16)
 
         @pl.when((k < live) & jnp.logical_not(same))
         def _():
-            other_ref[y, part] = acc_ref[block].astype(BF16)
-
-
-def pair_kernel(meta_ref, mine_ref, came_ref, keep_ref, *out_refs):
+            other_ref[kind, y, part] = acc_ref[block].astype(BF16)
+
+
+def pair_kernel(kind, meta_ref, mine_in, came_in, *rest):
+    keep_ref, *out_refs, mine_ref, came_ref, sems = rest[-7:]
+    copies = [pltpu.make_async_copy(mine_in.at[kind], mine_ref, sems.at[0]),
+              pltpu.make_async_copy(came_in.at[kind], came_ref, sems.at[1])]
+    for copy in copies:
+        copy.start()
+    for copy in copies:
+        copy.wait()
     y = meta_ref[1]
     keep_ref[...] = mine_ref[y].astype(F32) + came_ref[y].astype(F32)
     for step, out_ref in enumerate(out_refs, 1):
@@ -123,12 +134,33 @@
         out_ref[...] = (mine_ref[to].astype(F32) + came_ref[to].astype(F32)).astype(BF16)
 
 
-def side_kernel(keep_ref, came1_ref, came2_ref, came3_ref, far_ref, own_ref, high_ref, low_ref, out_ref):
+def sum_kernel(keep_ref, came1_ref, came2_ref, came3_ref, token_ref, out_ref, out_token_ref):
+    out_token_ref[...] = token_ref[...]
     terms = keep_ref[...]
     for came_ref in (came1_ref, came2_ref, came3_ref):
         terms += came_ref[...].astype(F32)
-    own_ref[...] = terms[:2].reshape(2 * TILE, -1)
-    bound = terms[2:].reshape(2 * TILE, -1)
+    out_ref[...] = terms.reshape(out_ref.shape)
+
+
+def own_kernel(meta_ref, tiles_ref, cot_ref, source_ref, out_ref):
+    live = meta_ref[0]
+    out_ref[...] = jnp.zeros(out_ref.shape, F32)
+    for k in range(NT):
+        block = meta_ref[SRC + k]
+
+        @pl.when((k < live) & (block < 16))
+        def _():
+            high, low = halves(dot(tiles_ref[k], cot_ref[meta_ref[DST + k]], 0, 0))
+            source = source_ref[block]
+            out_ref[...] += dot(source, high, 0, 0) + dot(source, low, 0, 0)
+
+
+def side_kernel(keep_ref, came1_ref, came2_ref, came3_ref, far_ref, own_ref, high_ref, low_ref, out_ref):
+    del own_ref
+    terms = keep_ref[...]
+    for came_ref in (came1_ref, came2_ref, came3_ref):
+        terms += came_ref[...].astype(F32)
+    bound = terms.reshape(2 * TILE, -1)
     rows, width = bound.shape
     column = lax.broadcasted_iota(jnp.int32, (rows, rows), 1)
     x, zl, zh, s = digits(rows, 0, (X, ZL, ZH, SLOTS))
@@ -144,23 +176,20 @@
     out_ref[:, lines:, :] = high.reshape(X * ZL, lines, width)
 
 
-def mid_kernel(own_ref, high_ref, low_ref, side_ref, features_ref, gw_ref, both_ref):
-    rows, width = own_ref.shape
-    features = features_ref[...]
+def mid_kernel(own_ref, high_ref, low_ref, side_ref, gw_ref, arrived_ref):
+    rows, width = high_ref.shape
     arrived = side_ref[:, :rows // (X * ZL), :].reshape(rows, width)
-    own_high, own_low = halves(own_ref[...])
-    gw = (dot(features, own_high, 0, 0) + dot(features, own_low, 0, 0)
-          + dot(arrived, high_ref[...], 0, 0) + dot(arrived, low_ref[...], 0, 0))
+    gw = own_ref[...] + dot(arrived, high_ref[...], 0, 0) + dot(arrived, low_ref[...], 0, 0)
     for c in range(CHUNKS):
         row, col = c // 2 * 8, c % 2 * 128
         gw_ref[c] = gw[row:row + 8, col:col + 128]
     x, zl, zh, s = digits(rows, 1, (X, ZL, ZH, SLOTS))
     order = permutation(boundary_row(x, zh, zl, s) == lax.broadcasted_iota(jnp.int32, (rows, rows), 0))
-    both_ref[:rows, :] = features
-    both_ref[rows:, :] = dot(order, arrived).astype(BF16)
-
-
-def pack_kernel(side_ref, near_ref, out_ref):
+    arrived_ref[...] = dot(order, arrived).astype(BF16)
+
+
+def pack_kernel(side_ref, near_ref, out_ref, token_ref):
+    token_ref[...] = jnp.zeros(token_ref.shape, F32)
     lines = out_ref.shape[1] // 2 - 4
     rows = ZH * lines
     zh, x, zl, s = digits(rows, 0, (ZH, X, ZL, SLOTS))
@@ -190,17 +219,20 @@
     out_ref[...] = dot(high, weight, 1, 1) + dot(low, weight, 1, 1)
 
 
-def forward_kernel(meta_ref, tiles_ref, source_ref, weight_ref, out_ref, token_ref, acc_ref):
+def forward_kernel(meta_ref, tiles_ref, own_ref, bound_ref, weight_ref, out_ref, token_ref, acc_ref):
     live = meta_ref[0]
     token_ref[...] = jnp.zeros(token_ref.shape, F32)
     acc_ref[...] = jnp.zeros(acc_ref.shape, F32)
     for k in range(NT):
-        @pl.when(k < live)
-        def _():
-            block = meta_ref[SRC + k]
-            member = lax.div(lax.rem(block, 16), 2)
-            part = lax.rem(block, 2) + 2 * lax.div(block, 16)
-            acc_ref[meta_ref[DST + k]] += dot(tiles_ref[k], source_ref[member, part])
+        block = meta_ref[SRC + k]
+
+        @pl.when((k < live) & (block < 16))
+        def _():
+            acc_ref[meta_ref[DST + k]] += dot(tiles_ref[k], own_ref[block])
+
+        @pl.when((k < live) & (block >= 16))
+        def _():
+            acc_ref[meta_ref[DST + k]] += dot(tiles_ref[k], bound_ref[block - 16])
     for t in range(2):
         out_ref[t] = dot(acc_ref[t].astype(BF16), weight_ref[...]).astype(BF16)
 
@@ -216,41 +248,56 @@
     meta = jnp.concatenate([tile_count, places, tile_src, tile_dst])
     send_rows = send_rows.transpose(0, 2, 1).reshape(slots, groups)
 
-    part = shape((4, TILE, width), BF16)
-    half = shape((Y, 4, TILE, width), BF16)
+    cotangent = cotangent.reshape(2, TILE, width)
+    blocked = (16, TILE, width)
+    square = shape((rows, width), BF16)
+    token = shape((8, 128), F32)
+
+    all_own = lax.all_gather(features, DEV, axis=0, tiled=True).reshape(blocked)
+
+    half = shape((2, Y, 2, TILE, width), BF16)
     mine, other = call(
         terms_kernel, (half, half), [SMEM] + [VMEM] * 2, "terms", [pltpu.VMEM((32, TILE, width), F32)], 60,
-    )(meta, tiles, cotangent.reshape(2, TILE, width))
+    )(meta, tiles, cotangent)
     came = shift(other, "core", 1, CORE)
     outgoing = call(pick_kernel, shape((ZH, lines, width), BF16), [VMEM] * 3, "pick", (), 60)(
         send_rows, send_count, features)
     landed = swap(outgoing, FAR)
-    keep, *sent = call(
-        pair_kernel, (shape((4, TILE, width), F32), part, part, part), [SMEM] + [VMEM] * 2, "pair", (), 60,
-    )(meta, mine, came)
-    came = [shift(block, "y", step, Y) for step, block in enumerate(sent, 1)]
-
-    square = shape((rows, width), BF16)
-    own, high, low, side = call(
-        side_kernel,
-        (shape((rows, width), F32), square, square, shape((X * ZL, 2 * rows // (X * ZL), width), BF16)),
-        [VMEM] * 5, "side",
-    )(keep, *came, landed)
+
+    def exchange(kind, name, after):
+        held = pltpu.VMEM((Y, 2, TILE, width), BF16)
+        part = shape((2, TILE, width), BF16)
+        keep, *sent = call(
+            functools.partial(pair_kernel, kind), (shape(part.shape, F32), part, part, part), [SMEM, ANY, ANY] + [VMEM] * len(after),
+            name, [held, held, pltpu.SemaphoreType.DMA((2,))], PAIR,
+        )(meta, mine, came, *after)
+        return keep, [shift(block, "y", step, Y) for step, block in enumerate(sent, 1)]
+
+    keep, sums = exchange(1, "pair_bound", ())
+    gw_own = call(own_kernel, shape((width, width), F32), [SMEM] + [VMEM] * 3, "own")(meta, tiles, cotangent, all_own)
+    high, low, side = call(
+        side_kernel, (square, square, shape((X * ZL, 2 * rows // (X * ZL), width), BF16)), [VMEM] * 5 + [ANY], "side",
+    )(keep, *sums, landed, gw_own)
     side = swap(side, SIDE)
-    gw, both = call(
-        mid_kernel, (shape((CHUNKS, 8, 128), F32), shape((2 * rows, width), BF16)), [VMEM] * 5, "mid",
-    )(own, high, low, side, features)
+    gw, arrived = call(
+        mid_kernel, (shape((CHUNKS, 8, 128), F32), square), [VMEM] * 4, "mid",
+    )(gw_own, high, low, side)
     near = swap(gw, NEAR)
-    packed = call(pack_kernel, shape((ZH, 2 * lines + 8, 128), BF16), [VMEM] * 2, "pack")(side, near)
+    packed, packed_token = call(
+        pack_kernel, (shape((ZH, 2 * lines + 8, 128), BF16), token), [VMEM] * 2, "pack",
+    )(side, near)
     far = swap(packed, FAR)
 
-    source = lax.all_gather(both, DEV, axis=0, tiled=True).reshape(Y * CORE, 4, TILE, width)
-    output, token = call(
-        forward_kernel, (shape((2, TILE, width), BF16), shape((8, 128), F32)), [SMEM] + [VMEM] * 3, "forward",
+    all_bound = lax.all_gather(arrived, DEV, axis=0, tiled=True).reshape(blocked)
+    output, forward_token = call(
+        forward_kernel, (shape((2, TILE, width), BF16), token), [SMEM] + [VMEM] * 4, "forward",
         [pltpu.VMEM((2, TILE, width), F32)],
-    )(meta, tiles, source, weight)
-
-    spread = call(far_kernel, shape((CHUNKS, 8, 128), F32), [VMEM] * 2, "far")(far, token)
+    )(meta, tiles, all_own, all_bound, weight)
+    keep, sums = exchange(0, "pair_own", (packed_token,))
+    own, last_token = call(sum_kernel, (shape((rows, width), F32), token), [VMEM] * 5, "sum")(
+        keep, *sums, forward_token)
+
+    spread = call(far_kernel, shape((CHUNKS, 8, 128), F32), [VMEM] * 2, "far")(far, last_token)
     grad_weight = swap(spread, NEAR).reshape(width // 8, 2, 8, 128).transpose(0, 2, 1, 3).reshape(width, width)
     grad_features = call(back_kernel, shape((rows, width), F32), [VMEM] * 5, "back")(
         send_rows, send_count, own, far, weight)

time: 175 us -> 171 us (0.977)
  blocking collectives: 34.4 us -> 9.72 us
  starting transfers between devices: 70.1 us -> 87.9 us
  Pallas kernels: 14 us -> 16.3 us
  local copies, waits for them, and re-layouts: 5.57 us -> 7.67 us
  waiting for transfers between devices: 35.8 us -> 33.7 us
    all_to_all x2 -> x1, blocking collectives: 34.4 us -> 9.72 us  [swap(): return lax.all_to_all(x, axes, split_axis=0, concat_axis=0, tiled=True)]
    ppermute x4 -> x7, starting transfers between devices: 25.7 us -> 36.2 us  [shift(): return lax.ppermute(x, axis, [(i, (i + step) % size) for i in range(size)])]
    all_to_all x3 -> x4, waiting for transfers between devices: 31.4 us -> 23.7 us  [swap(): return lax.all_to_all(x, axes, split_axis=0, concat_axis=0, tiled=True)]
    all_to_all x3 -> x4, starting transfers between devices: 44.3 us -> 51.7 us  [swap(): return lax.all_to_all(x, axes, split_axis=0, concat_axis=0, tiled=True)]
    all_gather x1 -> x2, waiting for transfers between devices: 3.96 us -> 8.55 us  [the longest x1 6.65 us: per_device(): lax.all_gather(arrived, DEV, axis=0, tiled=True).reshape(blocked)]
    unnamed x19 -> x31, local copies, waits for them, and re-layouts: 4.32 us -> 7.07 us
    pallas_call x5 -> x8, Pallas kernels: 6.92 us -> 7.4 us  [the longest x2 2.19 us: exchange(): call(functools.partial(pair_kernel, kind), (shape(part.shape, F32), part,...]
  transfers between devices with their start and end apart: 8 -> 13, of which waited for: 5 -> 6; matrix products, arithmetic and copies ran while one was open for 0% -> 0% of each run, Pallas kernels for 5% -> 8%
where the time goes in v5:
time: 171 us; the launch traced here: 170 us
  starting transfers between devices  87.9 us (51%)
  waiting for transfers between devices  33.7 us (20%)
  Pallas kernels  16.3 us (10%)
  between operations  14.9 us (9%)
  blocking collectives  9.72 us (6%)
  local copies, waits for them, and re-layouts  7.67 us (4%)
    all_to_all x4, starting transfers between devices, swap(): return lax.all_to_all(x, axes, split_axis=0, concat_axis=0, tiled=True)  51.7 us
    ppermute x7, starting transfers between devices, shift(): return lax.ppermute(x, axis, [(i, (i + step) % size) for i in range(size)])  36.2 us
    all_to_all x4, waiting for transfers between devices, swap(): return lax.all_to_all(x, axes, split_axis=0, concat_axis=0, tiled=True)  23.7 us
    all_to_all x1, blocking collectives, swap(): return lax.all_to_all(x, axes, split_axis=0, concat_axis=0, tiled=True)  9.72 us
    unnamed x31, local copies, waits for them, and re-layouts  7.07 us
    all_gather x1, waiting for transfers between devices, per_device(): lax.all_gather(arrived, DEV, axis=0, tiled=True).reshape(blocked)  6.65 us
  transfers between devices with their start and end apart: 13, of which 6 were waited for; matrix products, arithmetic and copies ran while one was open for 0% of the time, Pallas kernels for 8%

profile of v5, /device:TPU:1, one launch (start us, length us, event | category | flops | bytes accessed | tf_op | source)
XLA Modules:
  0.0 170.2 jit_solution(7658971564525981666)
XLA Ops:
  9.8 3.1 %terms.1 = (bf16[2,4,2,128,256]{4,3,2,1,0:T(8,128)(2,1)}, bf16[2,4,2,128,256]{4,3,2,1,0:T(8,128)(2,1)}) custom-call(s32[19]{0:T(128)} %concatenate.3.meta_ref, bf16[8,128,128]{2,1,0:T(8,128)(2,1)} %tiles_ref.5, bf16[2,128,256]{2,1,0:T(8,128)(2,1)} %bitcast.17), custom_call_target="tpu_custom_call" | custom-call | tf_op jit(solution)/shard_map/terms/pallas_call | solution.py:259
  12.9 16.5 %collective-permute-start = (bf16[2,4,2,128,256]{4,3,2,1,0:T(8,128)(2,1)}, bf16[2,4,2,128,256]{4,3,2,1,0:T(8,128)(2,1)S(1)}, u32[]{:S(2)}, u32[]{:S(2)}) collective-permute-start(bf16[2,4,2,128,256]{4,3,2,1,0:T(8,128)(2,1)} %get-tuple-element.25), channel_id=1, source_target_pairs={{0,1},{1,0},{2,3},{3,2},{4,5},{5,4},{6,7},{7,6},{8,9},{9,8},{10,11... | collective-permute-start | bytes 3145736 | tf_op jit(solution)/shard_map/ppermute | solution.py:37
  29.4 2.1 %pick.1 = bf16[16,16,256]{2,1,0:T(8,128)(2,1)} custom-call(s32[2,128]{1,0:T(2,128)} %bitcast.19, s32[1,128]{1,0:T(1,128)} %count_ref.3, bf16[256,256]{1,0:T(8,128)(2,1)} %features_ref.1), custom_call_target="tpu_custom_call" | custom-call | tf_op jit(solution)/shard_map/pick/pallas_call | solution.py:263
  31.4 14.9 %all-to-all-start = ((bf16[16,16,256]{2,1,0:T(8,128)(2,1)}), bf16[16,16,256]{2,1,0:T(8,128)(2,1)S(1)}, u32[]{:S(2)}, u32[]{:S(2)}) async-start(bf16[16,16,256]{2,1,0:T(8,128)(2,1)} %pick.1), calls=%async_computation | async-start | bytes 262144 | tf_op jit(solution)/shard_map/all_to_all | solution.py:33
  49.0 4.0 %collective-permute-start.1 = (bf16[2,128,256]{2,1,0:T(8,128)(2,1)S(1)}, bf16[2,128,256]{2,1,0:T(8,128)(2,1)S(1)}, u32[]{:S(2)}, u32[]{:S(2)}) collective-permute-start(bf16[2,128,256]{2,1,0:T(8,128)(2,1)S(1)} %get-tuple-element.27), channel_id=1, source_target_pairs={{0,2},{2,4},{4,6},{6,0},{1,3},{3,5},{5,7},{7,1},{8,10},{10,12},{12... | collective-permute-start | bytes 393224 | tf_op jit(solution)/shard_map/ppermute | solution.py:37
  53.0 4.4 %collective-permute-start.2 = (bf16[2,128,256]{2,1,0:T(8,128)(2,1)S(1)}, bf16[2,128,256]{2,1,0:T(8,128)(2,1)S(1)}, u32[]{:S(2)}, u32[]{:S(2)}) collective-permute-start(bf16[2,128,256]{2,1,0:T(8,128)(2,1)S(1)} %get-tuple-element.28), channel_id=1, source_target_pairs={{0,4},{2,6},{4,0},{6,2},{1,5},{3,7},{5,1},{7,3},{8,12},{10,14},{12... | collective-permute-start | bytes 393224 | tf_op jit(solution)/shard_map/ppermute | solution.py:37
  57.3 2.9 %collective-permute-start.3 = (bf16[2,128,256]{2,1,0:T(8,128)(2,1)S(1)}, bf16[2,128,256]{2,1,0:T(8,128)(2,1)S(1)}, u32[]{:S(2)}, u32[]{:S(2)}) collective-permute-start(bf16[2,128,256]{2,1,0:T(8,128)(2,1)S(1)} %get-tuple-element.29), channel_id=1, source_target_pairs={{0,6},{2,0},{4,2},{6,4},{1,7},{3,1},{5,3},{7,5},{8,14},{10,8},{12,... | collective-permute-start | bytes 393224 | tf_op jit(solution)/shard_map/ppermute | solution.py:37
  60.3 1.9 %all-gather.3.cloned.1.call-done = bf16[2048,256]{1,0:T(8,128)(2,1)} async-done(((bf16[256,256]{1,0:T(8,128)(2,1)}), bf16[2048,256]{1,0:T(8,128)(2,1)}) %all-gather.3.cloned.1.call-update) | async-done | bytes 1048592 | tf_op jit(solution)/shard_map/all_gather | solution.py:256
  64.5 5.8 %all-to-all-done.far_ref = bf16[16,16,256]{2,1,0:T(8,128)(2,1)S(1)} async-done(((bf16[16,16,256]{2,1,0:T(8,128)(2,1)}), bf16[16,16,256]{2,1,0:T(8,128)(2,1)S(1)}, u32[]{:S(2)}, u32[]{:S(2)}) %all-to-all-start) | async-done | bytes 131104 | tf_op jit(solution)/shard_map/all_to_all | solution.py:33
  70.7 9.7 %all_to_all.25.side_ref = bf16[8,64,256]{2,1,0:T(8,128)(2,1)S(1)} all-to-all(bf16[8,64,256]{2,1,0:T(8,128)(2,1)S(1)} %get-tuple-element.32), channel_id=1, replica_groups=mesh['x'=4,'zh'=16,'zl'=2,'y'=4,'core'=2] {'x','zl'}, dimensions={0} | all-to-all | bytes 524288 | tf_op jit(solution)/shard_map/all_to_all | solution.py:33
  81.5 14.3 %all-to-all-start.2 = ((f32[64,8,128]{2,1,0:T(8,128)}), f32[64,8,128]{2,1,0:T(8,128)S(1)}, u32[]{:S(2)}, u32[]{:S(2)}) async-start(f32[64,8,128]{2,1,0:T(8,128)} %get-tuple-element.35), calls=%async_computation.2 | async-start | bytes 524288 | tf_op jit(solution)/shard_map/all_to_all | solution.py:33
  96.6 9.1 %all-to-all-done.2.near_ref = f32[64,8,128]{2,1,0:T(8,128)S(1)} async-done(((f32[64,8,128]{2,1,0:T(8,128)}), f32[64,8,128]{2,1,0:T(8,128)S(1)}, u32[]{:S(2)}, u32[]{:S(2)}) %all-to-all-start.2) | async-done | bytes 262176 | tf_op jit(solution)/shard_map/all_to_all | solution.py:33
  106.5 10.4 %all-to-all-start.3 = ((bf16[16,40,128]{2,1,0:T(8,128)(2,1)}), bf16[16,40,128]{2,1,0:T(8,128)(2,1)}, u32[]{:S(2)}, u32[]{:S(2)}) async-start(bf16[16,40,128]{2,1,0:T(8,128)(2,1)} %get-tuple-element.43), calls=%async_computation.3 | async-start | bytes 327680 | tf_op jit(solution)/shard_map/all_to_all | solution.py:33
  116.9 1.4 pair_own.1
  119.1 2.2 %collective-permute-start.4 = (bf16[2,128,256]{2,1,0:T(8,128)(2,1)}, bf16[2,128,256]{2,1,0:T(8,128)(2,1)S(1)}, u32[]{:S(2)}, u32[]{:S(2)}) collective-permute-start(bf16[2,128,256]{2,1,0:T(8,128)(2,1)} %get-tuple-element.38), channel_id=1, source_target_pairs={{0,2},{2,4},{4,6},{6,0},{1,3},{3,5},{5,7},{7,1},{8,10},{10,12},{12... | collective-permute-start | bytes 393224 | tf_op jit(solution)/shard_map/ppermute | solution.py:37
  121.2 3.7 %collective-permute-start.5 = (bf16[2,128,256]{2,1,0:T(8,128)(2,1)}, bf16[2,128,256]{2,1,0:T(8,128)(2,1)S(1)}, u32[]{:S(2)}, u32[]{:S(2)}) collective-permute-start(bf16[2,128,256]{2,1,0:T(8,128)(2,1)} %get-tuple-element.39), channel_id=1, source_target_pairs={{0,4},{2,6},{4,0},{6,2},{1,5},{3,7},{5,1},{7,3},{8,12},{10,14},{12... | collective-permute-start | bytes 393224 | tf_op jit(solution)/shard_map/ppermute | solution.py:37
  125.0 2.5 %collective-permute-start.6 = (bf16[2,128,256]{2,1,0:T(8,128)(2,1)}, bf16[2,128,256]{2,1,0:T(8,128)(2,1)S(1)}, u32[]{:S(2)}, u32[]{:S(2)}) collective-permute-start(bf16[2,128,256]{2,1,0:T(8,128)(2,1)} %get-tuple-element.40), channel_id=1, source_target_pairs={{0,6},{2,0},{4,2},{6,4},{1,7},{3,1},{5,3},{7,5},{8,14},{10,8},{12,... | collective-permute-start | bytes 393224 | tf_op jit(solution)/shard_map/ppermute | solution.py:37
  127.5 6.7 %all-gather.5.cloned.1.call-done = bf16[2048,256]{1,0:T(8,128)(2,1)} async-done(((bf16[256,256]{1,0:T(8,128)(2,1)}), bf16[2048,256]{1,0:T(8,128)(2,1)}) %all-gather.5.cloned.1.call-update) | async-done | bytes 1048592 | tf_op jit(solution)/shard_map/all_gather | solution.py:291
  135.4 1.8 %forward.1 = (bf16[2,128,256]{2,1,0:T(8,128)(2,1)}, f32[8,128]{1,0:T(8,128)S(1)}) custom-call(s32[19]{0:T(128)S(1)} %copy-done.10, bf16[8,128,128]{2,1,0:T(8,128)(2,1)S(1)} %copy-done.4, bf16[16,128,256]{2,1,0:T(8,128)(2,1)S(1)} %bitcast.15, bf16[16,128,256]{2,1,0:T(8,128)(2,1)S(1)} %bitcast.16, bf16[256,256]{1,0:T(8,128)(2,1)S(1)} %copy-done.7), custom_call_target="tpu_custom_call" | custom-call | tf_op jit(solution)/shard_map/forward/pallas_call | solution.py:292
  137.2 1.8 %all-to-all-done.3.far_ref = bf16[16,40,128]{2,1,0:T(8,128)(2,1)} async-done(((bf16[16,40,128]{2,1,0:T(8,128)(2,1)}), bf16[16,40,128]{2,1,0:T(8,128)(2,1)}, u32[]{:S(2)}, u32[]{:S(2)}) %all-to-all-start.3) | async-done | bytes 163872 | tf_op jit(solution)/shard_map/all_to_all | solution.py:33
  139.0 1.7 far.1
  140.7 12.1 %all-to-all-start.4 = ((f32[64,8,128]{2,1,0:T(8,128)}), f32[64,8,128]{2,1,0:T(8,128)S(1)}, u32[]{:S(2)}, u32[]{:S(2)}) async-start(f32[64,8,128]{2,1,0:T(8,128)} %far.1), calls=%async_computation.4 | async-start | bytes 524288 | tf_op jit(solution)/shard_map/all_to_all | solution.py:33
  153.5 2.1 %back.1 = f32[256,256]{1,0:T(8,128)} custom-call(s32[2,128]{1,0:T(2,128)S(1)} %bitcast.20, s32[1,128]{1,0:T(1,128)S(1)} %copy-done.12, f32[256,256]{1,0:T(8,128)S(1)} %get-tuple-element.42.own_ref, bf16[16,40,128]{2,1,0:T(8,128)(2,1)} %all-to-all-done.3.far_ref, bf16[256,256]{1,0:T(8,128)(2,1)S(1)} %copy-done.7), custom_call_target="tpu_custom_call" | custom-call | tf_op jit(solution)/shard_map/back/pallas_call | solution.py:302
  155.6 7.0 %all-to-all-done.4 = f32[64,8,128]{2,1,0:T(8,128)S(1)} async-done(((f32[64,8,128]{2,1,0:T(8,128)}), f32[64,8,128]{2,1,0:T(8,128)S(1)}, u32[]{:S(2)}, u32[]{:S(2)}) %all-to-all-start.4) | async-done | bytes 262176 | tf_op jit(solution)/shard_map/all_to_all | solution.py:33
  (49 shorter events, 13.3 us)
Async XLA Ops:
  7.2 55.0 %all-gather.3.cloned.1.call-start = ((), (), s32[]{:S(2)}) async-start(), calls=%async_computation.5 | async-start | bytes 1179648 | tf_op jit(solution)/shard_map/all_gather | solution.py:256
  12.9 33.4 %collective-permute-start = (bf16[2,4,2,128,256]{4,3,2,1,0:T(8,128)(2,1)}, bf16[2,4,2,128,256]{4,3,2,1,0:T(8,128)(2,1)S(1)}, u32[]{:S(2)}, u32[]{:S(2)}) collective-permute-start(bf16[2,4,2,128,256]{4,3,2,1,0:T(8,128)(2,1)} %get-tuple-element.25), channel_id=1, source_target_pairs={{0,1},{1,0},{2,3},{3,2},{4,5},{5,4},{6,7},{7,6},{8,9},{9,8},{10,11... | collective-permute-start | bytes 3145736 | tf_op jit(solution)/shard_map/ppermute | solution.py:37
  31.4 38.9 %all-to-all-start = ((bf16[16,16,256]{2,1,0:T(8,128)(2,1)}), bf16[16,16,256]{2,1,0:T(8,128)(2,1)S(1)}, u32[]{:S(2)}, u32[]{:S(2)}) async-start(bf16[16,16,256]{2,1,0:T(8,128)(2,1)} %pick.1), calls=%async_computation | async-start | bytes 262144 | tf_op jit(solution)/shard_map/all_to_all | solution.py:33
  47.0 1.2 copy-start
  48.2 14.0 %copy-start.4 = (bf16[8,128,128]{2,1,0:T(8,128)(2,1)S(1)}, bf16[8,128,128]{2,1,0:T(8,128)(2,1)}, u32[]{:S(2)}) copy-start(bf16[8,128,128]{2,1,0:T(8,128)(2,1)} %tiles_ref.5) | copy-start | bytes 786436
  48.2 14.0 %copy-start.6 = (bf16[256,256]{1,0:T(8,128)(2,1)S(1)}, bf16[256,256]{1,0:T(8,128)(2,1)}, u32[]{:S(2)}) copy-start(bf16[256,256]{1,0:T(8,128)(2,1)} %param.17) | copy-start | bytes 393220
  49.0 21.3 %collective-permute-start.1 = (bf16[2,128,256]{2,1,0:T(8,128)(2,1)S(1)}, bf16[2,128,256]{2,1,0:T(8,128)(2,1)S(1)}, u32[]{:S(2)}, u32[]{:S(2)}) collective-permute-start(bf16[2,128,256]{2,1,0:T(8,128)(2,1)S(1)} %get-tuple-element.27), channel_id=1, source_target_pairs={{0,2},{2,4},{4,6},{6,0},{1,3},{3,5},{5,7},{7,1},{8,10},{10,12},{12... | collective-permute-start | bytes 393224 | tf_op jit(solution)/shard_map/ppermute | solution.py:37
  53.0 17.3 %collective-permute-start.2 = (bf16[2,128,256]{2,1,0:T(8,128)(2,1)S(1)}, bf16[2,128,256]{2,1,0:T(8,128)(2,1)S(1)}, u32[]{:S(2)}, u32[]{:S(2)}) collective-permute-start(bf16[2,128,256]{2,1,0:T(8,128)(2,1)S(1)} %get-tuple-element.28), channel_id=1, source_target_pairs={{0,4},{2,6},{4,0},{6,2},{1,5},{3,7},{5,1},{7,3},{8,12},{10,14},{12... | collective-permute-start | bytes 393224 | tf_op jit(solution)/shard_map/ppermute | solution.py:37
  57.3 13.0 %collective-permute-start.3 = (bf16[2,128,256]{2,1,0:T(8,128)(2,1)S(1)}, bf16[2,128,256]{2,1,0:T(8,128)(2,1)S(1)}, u32[]{:S(2)}, u32[]{:S(2)}) collective-permute-start(bf16[2,128,256]{2,1,0:T(8,128)(2,1)S(1)} %get-tuple-element.29), channel_id=1, source_target_pairs={{0,6},{2,0},{4,2},{6,4},{1,7},{3,1},{5,3},{7,5},{8,14},{10,8},{12,... | collective-permute-start | bytes 393224 | tf_op jit(solution)/shard_map/ppermute | solution.py:37
  62.2 1.2 copy-start.2
  80.4 36.5 %copy-start.1 = (bf16[2,4,2,128,256]{4,3,2,1,0:T(8,128)(2,1)S(1)}, bf16[2,4,2,128,256]{4,3,2,1,0:T(8,128)(2,1)}, u32[]{:S(2)}) copy-start(bf16[2,4,2,128,256]{4,3,2,1,0:T(8,128)(2,1)} %get-tuple-element.24.mine_in) | copy-start | bytes 3145732
  81.5 24.1 %all-to-all-start.2 = ((f32[64,8,128]{2,1,0:T(8,128)}), f32[64,8,128]{2,1,0:T(8,128)S(1)}, u32[]{:S(2)}, u32[]{:S(2)}) async-start(f32[64,8,128]{2,1,0:T(8,128)} %get-tuple-element.35), calls=%async_computation.2 | async-start | bytes 524288 | tf_op jit(solution)/shard_map/all_to_all | solution.py:33
  95.8 38.3 %all-gather.5.cloned.1.call-start = ((), (), s32[]{:S(2)}) async-start(), calls=%async_computation.6 | async-start | bytes 1179648 | tf_op jit(solution)/shard_map/all_gather | solution.py:291
  106.5 32.5 %all-to-all-start.3 = ((bf16[16,40,128]{2,1,0:T(8,128)(2,1)}), bf16[16,40,128]{2,1,0:T(8,128)(2,1)}, u32[]{:S(2)}, u32[]{:S(2)}) async-start(bf16[16,40,128]{2,1,0:T(8,128)(2,1)} %get-tuple-element.43), calls=%async_computation.3 | async-start | bytes 327680 | tf_op jit(solution)/shard_map/all_to_all | solution.py:33
  116.9 17.3 %copy-start.3 = (bf16[2048,256]{1,0:T(8,128)(2,1)S(1)}, bf16[2048,256]{1,0:T(8,128)(2,1)}, u32[]{:S(2)}) copy-start(bf16[2048,256]{1,0:T(8,128)(2,1)} %all-gather.3.cloned.1.call-done) | copy-start | bytes 3145732
  116.9 17.2 %copy-start.7 = (bf16[256,256]{1,0:T(8,128)(2,1)S(1)}, bf16[256,256]{1,0:T(8,128)(2,1)}, u32[]{:S(2)}) copy-start(bf16[256,256]{1,0:T(8,128)(2,1)} %weight_ref.3) | copy-start | bytes 393220
  118.4 0.7 copy-start.8
  119.1 18.1 %collective-permute-start.4 = (bf16[2,128,256]{2,1,0:T(8,128)(2,1)}, bf16[2,128,256]{2,1,0:T(8,128)(2,1)S(1)}, u32[]{:S(2)}, u32[]{:S(2)}) collective-permute-start(bf16[2,128,256]{2,1,0:T(8,128)(2,1)} %get-tuple-element.38), channel_id=1, source_target_pairs={{0,2},{2,4},{4,6},{6,0},{1,3},{3,5},{5,7},{7,1},{8,10},{10,12},{12... | collective-permute-start | bytes 393224 | tf_op jit(solution)/shard_map/ppermute | solution.py:37
  121.2 15.9 %collective-permute-start.5 = (bf16[2,128,256]{2,1,0:T(8,128)(2,1)}, bf16[2,128,256]{2,1,0:T(8,128)(2,1)S(1)}, u32[]{:S(2)}, u32[]{:S(2)}) collective-permute-start(bf16[2,128,256]{2,1,0:T(8,128)(2,1)} %get-tuple-element.39), channel_id=1, source_target_pairs={{0,4},{2,6},{4,0},{6,2},{1,5},{3,7},{5,1},{7,3},{8,12},{10,14},{12... | collective-permute-start | bytes 393224 | tf_op jit(solution)/shard_map/ppermute | solution.py:37
  125.0 12.2 %collective-permute-start.6 = (bf16[2,128,256]{2,1,0:T(8,128)(2,1)}, bf16[2,128,256]{2,1,0:T(8,128)(2,1)S(1)}, u32[]{:S(2)}, u32[]{:S(2)}) collective-permute-start(bf16[2,128,256]{2,1,0:T(8,128)(2,1)} %get-tuple-element.40), channel_id=1, source_target_pairs={{0,6},{2,0},{4,2},{6,4},{1,7},{3,1},{5,3},{7,5},{8,14},{10,8},{12,... | collective-permute-start | bytes 393224 | tf_op jit(solution)/shard_map/ppermute | solution.py:37
  134.2 1.2 copy-start.5
  135.4 1.8 %copy-start.9 = (f32[2,128,256]{2,1,0:T(8,128)S(1)}, f32[2,128,256]{2,1,0:T(8,128)}, u32[]{:S(2)}) copy-start(f32[2,128,256]{2,1,0:T(8,128)} %copy-done.8) | copy-start | bytes 786436
  140.7 21.9 %all-to-all-start.4 = ((f32[64,8,128]{2,1,0:T(8,128)}), f32[64,8,128]{2,1,0:T(8,128)S(1)}, u32[]{:S(2)}, u32[]{:S(2)}) async-start(f32[64,8,128]{2,1,0:T(8,128)} %far.1), calls=%async_computation.4 | async-start | bytes 524288 | tf_op jit(solution)/shard_map/all_to_all | solution.py:33
  152.8 0.7 copy-start.11
  (4 other events, 2.7 us)
Sparse Core Ops, SparseCore 0:
  10.7 51.4 all-gather.2
  100.0 34.1 all-gather.4

commit v6 on v5

--- a/solution.py
+++ b/solution.py
@@ -17,7 +17,6 @@
 FAR = "zh"
 TILE = 128
 NT = 8
-PAIR = 24
 CHUNKS = 64
 SRC = 3
 DST = SRC + NT
@@ -91,42 +90,40 @@
     out_ref[...] = dot(wanted, features_ref[...], 0, 0).astype(BF16).reshape(out_ref.shape)
 
 
-def terms_kernel(meta_ref, tiles_ref, cot_ref, mine_ref, other_ref, acc_ref):
+def terms_kernel(kind, meta_ref, tiles_ref, cot_ref, token_ref, mine_ref, other_ref, acc_ref):
+    del token_ref
     live, core = meta_ref[0], meta_ref[2]
     mine_ref[...] = jnp.zeros(mine_ref.shape, BF16)
     other_ref[...] = jnp.zeros(other_ref.shape, BF16)
-    for k in range(NT):
-        @pl.when(k < live)
-        def _():
-            acc_ref[meta_ref[SRC + k]] = jnp.zeros(acc_ref.shape[1:], F32)
-    for k in range(NT):
-        @pl.when(k < live)
-        def _():
-            acc_ref[meta_ref[SRC + k]] += dot(tiles_ref[k], cot_ref[meta_ref[DST + k]], 0, 0)
-    for k in range(NT):
+
+    def each(k, act):
         block = meta_ref[SRC + k]
-        member = lax.div(lax.rem(block, 16), 2)
-        y = lax.div(member, 2)
-        kind, part = lax.div(block, 16), lax.rem(block, 2)
-        same = lax.rem(member, 2) == core
-
-        @pl.when((k < live) & same)
-        def _():
-            mine_ref[kind, y, part] = acc_ref[block].astype(BF16)
-
-        @pl.when((k < live) & jnp.logical_not(same))
-        def _():
-            other_ref[kind, y, part] = acc_ref[block].astype(BF16)
-
-
-def pair_kernel(kind, meta_ref, mine_in, came_in, *rest):
-    keep_ref, *out_refs, mine_ref, came_ref, sems = rest[-7:]
-    copies = [pltpu.make_async_copy(mine_in.at[kind], mine_ref, sems.at[0]),
-              pltpu.make_async_copy(came_in.at[kind], came_ref, sems.at[1])]
-    for copy in copies:
-        copy.start()
-    for copy in copies:
-        copy.wait()
+        pl.when((k < live) & (lax.div(block, 16) == kind))(lambda: act(lax.rem(block, 16)))
+
+    for k in range(NT):
+        @functools.partial(each, k)
+        def _(block):
+            acc_ref[block] = jnp.zeros(acc_ref.shape[1:], F32)
+    for k in range(NT):
+        @functools.partial(each, k)
+        def _(block):
+            acc_ref[block] += dot(tiles_ref[k], cot_ref[meta_ref[DST + k]], 0, 0)
+    for k in range(NT):
+        @functools.partial(each, k)
+        def _(block):
+            member, part = lax.div(block, 2), lax.rem(block, 2)
+            y, same = lax.div(member, 2), lax.rem(member, 2) == core
+
+            @pl.when(same)
+            def _():
+                mine_ref[y, part] = acc_ref[block].astype(BF16)
+
+            @pl.when(jnp.logical_not(same))
+            def _():
+                other_ref[y, part] = acc_ref[block].astype(BF16)
+
+
+def pair_kernel(meta_ref, mine_ref, came_ref, keep_ref, *out_refs):
     y = meta_ref[1]
     keep_ref[...] = mine_ref[y].astype(F32) + came_ref[y].astype(F32)
     for step, out_ref in enumerate(out_refs, 1):
@@ -176,7 +173,8 @@
     out_ref[:, lines:, :] = high.reshape(X * ZL, lines, width)
 
 
-def mid_kernel(own_ref, high_ref, low_ref, side_ref, gw_ref, arrived_ref):
+def mid_kernel(own_ref, high_ref, low_ref, side_ref, gw_ref, arrived_ref, token_ref):
+    token_ref[...] = jnp.zeros(token_ref.shape, F32)
     rows, width = high_ref.shape
     arrived = side_ref[:, :rows // (X * ZL), :].reshape(rows, width)
     gw = own_ref[...] + dot(arrived, high_ref[...], 0, 0) + dot(arrived, low_ref[...], 0, 0)
@@ -188,8 +186,7 @@
     arrived_ref[...] = dot(order, arrived).astype(BF16)
 
 
-def pack_kernel(side_ref, near_ref, out_ref, token_ref):
-    token_ref[...] = jnp.zeros(token_ref.shape, F32)
+def pack_kernel(side_ref, near_ref, out_ref):
     lines = out_ref.shape[1] // 2 - 4
     rows = ZH * lines
     zh, x, zl, s = digits(rows, 0, (ZH, X, ZL, SLOTS))
@@ -255,37 +252,34 @@
 
     all_own = lax.all_gather(features, DEV, axis=0, tiled=True).reshape(blocked)
 
-    half = shape((2, Y, 2, TILE, width), BF16)
-    mine, other = call(
-        terms_kernel, (half, half), [SMEM] + [VMEM] * 2, "terms", [pltpu.VMEM((32, TILE, width), F32)], 60,
-    )(meta, tiles, cotangent)
-    came = shift(other, "core", 1, CORE)
     outgoing = call(pick_kernel, shape((ZH, lines, width), BF16), [VMEM] * 3, "pick", (), 60)(
         send_rows, send_count, features)
     landed = swap(outgoing, FAR)
 
     def exchange(kind, name, after):
-        held = pltpu.VMEM((Y, 2, TILE, width), BF16)
+        half = shape((Y, 2, TILE, width), BF16)
         part = shape((2, TILE, width), BF16)
+        mine, other = call(
+            functools.partial(terms_kernel, kind), (half, half), [SMEM, VMEM, VMEM, ANY], "terms_" + name,
+            [pltpu.VMEM((16, TILE, width), F32)],
+        )(meta, tiles, cotangent, after)
+        came = shift(other, "core", 1, CORE)
         keep, *sent = call(
-            functools.partial(pair_kernel, kind), (shape(part.shape, F32), part, part, part), [SMEM, ANY, ANY] + [VMEM] * len(after),
-            name, [held, held, pltpu.SemaphoreType.DMA((2,))], PAIR,
-        )(meta, mine, came, *after)
+            pair_kernel, (shape(part.shape, F32), part, part, part), [SMEM] + [VMEM] * 2, "pair_" + name,
+        )(meta, mine, came)
         return keep, [shift(block, "y", step, Y) for step, block in enumerate(sent, 1)]
 
-    keep, sums = exchange(1, "pair_bound", ())
+    keep, sums = exchange(1, "bound", outgoing)
     gw_own = call(own_kernel, shape((width, width), F32), [SMEM] + [VMEM] * 3, "own")(meta, tiles, cotangent, all_own)
     high, low, side = call(
         side_kernel, (square, square, shape((X * ZL, 2 * rows // (X * ZL), width), BF16)), [VMEM] * 5 + [ANY], "side",
     )(keep, *sums, landed, gw_own)
     side = swap(side, SIDE)
-    gw, arrived = call(
-        mid_kernel, (shape((CHUNKS, 8, 128), F32), square), [VMEM] * 4, "mid",
+    gw, arrived, mid_token = call(
+        mid_kernel, (shape((CHUNKS, 8, 128), F32), square, token), [VMEM] * 4, "mid",
     )(gw_own, high, low, side)
     near = swap(gw, NEAR)
-    packed, packed_token = call(
-        pack_kernel, (shape((ZH, 2 * lines + 8, 128), BF16), token), [VMEM] * 2, "pack",
-    )(side, near)
+    packed = call(pack_kernel, shape((ZH, 2 * lines + 8, 128), BF16), [VMEM] * 2, "pack")(side, near)
     far = swap(packed, FAR)
 
     all_bound = lax.all_gather(arrived, DEV, axis=0, tiled=True).reshape(blocked)
@@ -293,7 +287,7 @@
         forward_kernel, (shape((2, TILE, width), BF16), token), [SMEM] + [VMEM] * 4, "forward",
         [pltpu.VMEM((2, TILE, width), F32)],
     )(meta, tiles, all_own, all_bound, weight)
-    keep, sums = exchange(0, "pair_own", (packed_token,))
+    keep, sums = exchange(0, "own", mid_token)
     own, last_token = call(sum_kernel, (shape((rows, width), F32), token), [VMEM] * 5, "sum")(
         keep, *sums, forward_token)
 

time: 171 us -> 171 us (level)
  starting transfers between devices: 87.9 us -> 96.6 us
  waiting for transfers between devices: 33.7 us -> 30.1 us
  Pallas kernels: 16.3 us -> 12.8 us
  local copies, waits for them, and re-layouts: 7.67 us -> 4.57 us
    all_to_all x4, starting transfers between devices: 51.7 us -> 71.6 us  [swap(): return lax.all_to_all(x, axes, split_axis=0, concat_axis=0, tiled=True)]
    ppermute x7 -> x8, starting transfers between devices: 36.2 us -> 24.9 us  [shift(): return lax.ppermute(x, axis, [(i, (i + step) % size) for i in range(size)])]
    all_gather x1, waiting for transfers between devices: 6.65 us -> 0.08 us  [per_device(): lax.all_gather(arrived, DEV, axis=0, tiled=True).reshape(blocked)]
    ppermute x7 -> x8, waiting for transfers between devices: 0.02 us -> 3.29 us  [shift(): return lax.ppermute(x, axis, [(i, (i + step) % size) for i in range(size)])]
    all_to_all x4, waiting for transfers between devices: 23.7 us -> 20.6 us  [swap(): return lax.all_to_all(x, axes, split_axis=0, concat_axis=0, tiled=True)]
    all_gather x1, waiting for transfers between devices: 1.9 us -> 4.71 us  [per_device(): all_own = lax.all_gather(features, DEV, axis=0, tiled=True).reshape(blocked)]
    unnamed x31 -> x23, local copies, waits for them, and re-layouts: 7.07 us -> 4.5 us
    pallas_call x5 -> x6, Pallas kernels: 7.22 us -> 5.49 us  [the longest x2 2.17 us: exchange(): call(functools.partial(terms_kernel, kind), (half, half), [SMEM, VMEM, VM...]
  transfers between devices with their start and end apart: 13 -> 14, of which waited for: 6 -> 8; matrix products, arithmetic and copies ran while one was open for 0% -> 0% of each run, Pallas kernels for 8% -> 6%
where the time goes in v6:
time: 171 us; the launch traced here: 170 us
  starting transfers between devices  96.6 us (56%)
  waiting for transfers between devices  30.1 us (18%)
  between operations  14.9 us (9%)
  Pallas kernels  12.8 us (7%)
  blocking collectives  11.4 us (7%)
  local copies, waits for them, and re-layouts  4.57 us (3%)
    all_to_all x4, starting transfers between devices, swap(): return lax.all_to_all(x, axes, split_axis=0, concat_axis=0, tiled=True)  71.6 us
    ppermute x8, starting transfers between devices, shift(): return lax.ppermute(x, axis, [(i, (i + step) % size) for i in range(size)])  24.9 us
    all_to_all x4, waiting for transfers between devices, swap(): return lax.all_to_all(x, axes, split_axis=0, concat_axis=0, tiled=True)  20.6 us
    all_to_all x1, blocking collectives, swap(): return lax.all_to_all(x, axes, split_axis=0, concat_axis=0, tiled=True)  11.4 us
    all_gather x1, waiting for transfers between devices, per_device(): all_own = lax.all_gather(features, DEV, axis=0, tiled=True).reshape(blocked)  4.71 us
    unnamed x23, local copies, waits for them, and re-layouts  4.5 us
  transfers between devices with their start and end apart: 14, of which 8 were waited for; matrix products, arithmetic and copies ran while one was open for 0% of the time, Pallas kernels for 6%

profile of v6, /device:TPU:1, one launch (start us, length us, event | category | flops | bytes accessed | tf_op | source)
XLA Modules:
  0.0 170.3 jit_solution(1380107655668418078)
XLA Ops:
  7.9 2.1 %pick.1.token_ref = bf16[16,16,256]{2,1,0:T(8,128)(2,1)} custom-call(s32[2,128]{1,0:T(2,128)} %bitcast.20, s32[1,128]{1,0:T(1,128)} %count_ref.3, bf16[256,256]{1,0:T(8,128)(2,1)} %features_ref.1), custom_call_target="tpu_custom_call" | custom-call | tf_op jit(solution)/shard_map/pick/pallas_call | solution.py:255
  10.0 29.1 %all-to-all-start = ((bf16[16,16,256]{2,1,0:T(8,128)(2,1)}), bf16[16,16,256]{2,1,0:T(8,128)(2,1)S(1)}, u32[]{:S(2)}, u32[]{:S(2)}) async-start(bf16[16,16,256]{2,1,0:T(8,128)(2,1)} %pick.1.token_ref), calls=%async_computation | async-start | bytes 262144 | tf_op jit(solution)/shard_map/all_to_all | solution.py:32
  41.7 3.1 %collective-permute-start = (bf16[4,2,128,256]{3,2,1,0:T(8,128)(2,1)S(1)}, bf16[4,2,128,256]{3,2,1,0:T(8,128)(2,1)S(1)}, u32[]{:S(2)}, u32[]{:S(2)}) collective-permute-start(bf16[4,2,128,256]{3,2,1,0:T(8,128)(2,1)S(1)} %get-tuple-element.26), channel_id=1, source_target_pairs={{0,1},{1,0},{2,3},{3,2},{4,5},{5,4},{6,7},{7,6},{8,9},{9,8},{10,11... | collective-permute-start | bytes 1572872 | tf_op jit(solution)/shard_map/ppermute | solution.py:36
  44.8 1.5 collective-permute-done.came_ref
  46.9 3.2 %collective-permute-start.1 = (bf16[2,128,256]{2,1,0:T(8,128)(2,1)S(1)}, bf16[2,128,256]{2,1,0:T(8,128)(2,1)S(1)}, u32[]{:S(2)}, u32[]{:S(2)}) collective-permute-start(bf16[2,128,256]{2,1,0:T(8,128)(2,1)S(1)} %get-tuple-element.28), channel_id=1, source_target_pairs={{0,2},{2,4},{4,6},{6,0},{1,3},{3,5},{5,7},{7,1},{8,10},{10,12},{12... | collective-permute-start | bytes 393224 | tf_op jit(solution)/shard_map/ppermute | solution.py:36
  50.2 5.2 %collective-permute-start.2 = (bf16[2,128,256]{2,1,0:T(8,128)(2,1)S(1)}, bf16[2,128,256]{2,1,0:T(8,128)(2,1)S(1)}, u32[]{:S(2)}, u32[]{:S(2)}) collective-permute-start(bf16[2,128,256]{2,1,0:T(8,128)(2,1)S(1)} %get-tuple-element.29), channel_id=1, source_target_pairs={{0,4},{2,6},{4,0},{6,2},{1,5},{3,7},{5,1},{7,3},{8,12},{10,14},{12... | collective-permute-start | bytes 393224 | tf_op jit(solution)/shard_map/ppermute | solution.py:36
  55.3 1.9 %collective-permute-start.3 = (bf16[2,128,256]{2,1,0:T(8,128)(2,1)S(1)}, bf16[2,128,256]{2,1,0:T(8,128)(2,1)S(1)}, u32[]{:S(2)}, u32[]{:S(2)}) collective-permute-start(bf16[2,128,256]{2,1,0:T(8,128)(2,1)S(1)} %get-tuple-element.30), channel_id=1, source_target_pairs={{0,6},{2,0},{4,2},{6,4},{1,7},{3,1},{5,3},{7,5},{8,14},{10,8},{12,... | collective-permute-start | bytes 393224 | tf_op jit(solution)/shard_map/ppermute | solution.py:36
  57.3 4.7 %all-gather.3.cloned.1.call-done = bf16[2048,256]{1,0:T(8,128)(2,1)} async-done(((bf16[256,256]{1,0:T(8,128)(2,1)}), bf16[2048,256]{1,0:T(8,128)(2,1)}) %all-gather.3.cloned.1.call-update) | async-done | bytes 1048592 | tf_op jit(solution)/shard_map/all_gather | solution.py:253
  62.0 1.2 copy-done
  64.7 11.4 %all_to_all.25.side_ref = bf16[8,64,256]{2,1,0:T(8,128)(2,1)S(1)} all-to-all(bf16[8,64,256]{2,1,0:T(8,128)(2,1)S(1)} %get-tuple-element.33), channel_id=1, replica_groups=mesh['x'=4,'zh'=16,'zl'=2,'y'=4,'core'=2] {'x','zl'}, dimensions={0} | all-to-all | bytes 524288 | tf_op jit(solution)/shard_map/all_to_all | solution.py:32
  77.1 7.8 %all-to-all-start.2 = ((f32[64,8,128]{2,1,0:T(8,128)}), f32[64,8,128]{2,1,0:T(8,128)S(1)}, u32[]{:S(2)}, u32[]{:S(2)}) async-start(f32[64,8,128]{2,1,0:T(8,128)} %get-tuple-element.45), calls=%async_computation.2 | async-start | bytes 524288 | tf_op jit(solution)/shard_map/all_to_all | solution.py:32
  85.6 9.1 %all-to-all-done.2.near_ref = f32[64,8,128]{2,1,0:T(8,128)S(1)} async-done(((f32[64,8,128]{2,1,0:T(8,128)}), f32[64,8,128]{2,1,0:T(8,128)S(1)}, u32[]{:S(2)}, u32[]{:S(2)}) %all-to-all-start.2) | async-done | bytes 262176 | tf_op jit(solution)/shard_map/all_to_all | solution.py:32
  95.6 22.5 %all-to-all-start.3 = ((bf16[16,40,128]{2,1,0:T(8,128)(2,1)}), bf16[16,40,128]{2,1,0:T(8,128)(2,1)S(1)}, u32[]{:S(2)}, u32[]{:S(2)}) async-start(bf16[16,40,128]{2,1,0:T(8,128)(2,1)} %pack.1), calls=%async_computation.3 | async-start | bytes 327680 | tf_op jit(solution)/shard_map/all_to_all | solution.py:32
  119.1 2.4 %collective-permute-start.4 = (bf16[4,2,128,256]{3,2,1,0:T(8,128)(2,1)S(1)}, bf16[4,2,128,256]{3,2,1,0:T(8,128)(2,1)S(1)}, u32[]{:S(2)}, u32[]{:S(2)}) collective-permute-start(bf16[4,2,128,256]{3,2,1,0:T(8,128)(2,1)S(1)} %get-tuple-element.38), channel_id=1, source_target_pairs={{0,1},{1,0},{2,3},{3,2},{4,5},{5,4},{6,7},{7,6},{8,9},{9,8},{10,11... | collective-permute-start | bytes 1572872 | tf_op jit(solution)/shard_map/ppermute | solution.py:36
  121.5 1.5 collective-permute-done.4.came_ref
  123.7 2.9 %collective-permute-start.5 = (bf16[2,128,256]{2,1,0:T(8,128)(2,1)S(1)}, bf16[2,128,256]{2,1,0:T(8,128)(2,1)S(1)}, u32[]{:S(2)}, u32[]{:S(2)}) collective-permute-start(bf16[2,128,256]{2,1,0:T(8,128)(2,1)S(1)} %get-tuple-element.40), channel_id=1, source_target_pairs={{0,2},{2,4},{4,6},{6,0},{1,3},{3,5},{5,7},{7,1},{8,10},{10,12},{12... | collective-permute-start | bytes 393224 | tf_op jit(solution)/shard_map/ppermute | solution.py:36
  126.7 3.6 %collective-permute-start.6 = (bf16[2,128,256]{2,1,0:T(8,128)(2,1)S(1)}, bf16[2,128,256]{2,1,0:T(8,128)(2,1)S(1)}, u32[]{:S(2)}, u32[]{:S(2)}) collective-permute-start(bf16[2,128,256]{2,1,0:T(8,128)(2,1)S(1)} %get-tuple-element.41), channel_id=1, source_target_pairs={{0,4},{2,6},{4,0},{6,2},{1,5},{3,7},{5,1},{7,3},{8,12},{10,14},{12... | collective-permute-start | bytes 393224 | tf_op jit(solution)/shard_map/ppermute | solution.py:36
  130.2 2.6 %collective-permute-start.7 = (bf16[2,128,256]{2,1,0:T(8,128)(2,1)S(1)}, bf16[2,128,256]{2,1,0:T(8,128)(2,1)S(1)}, u32[]{:S(2)}, u32[]{:S(2)}) collective-permute-start(bf16[2,128,256]{2,1,0:T(8,128)(2,1)S(1)} %get-tuple-element.42), channel_id=1, source_target_pairs={{0,6},{2,0},{4,2},{6,4},{1,7},{3,1},{5,3},{7,5},{8,14},{10,8},{12,... | collective-permute-start | bytes 393224 | tf_op jit(solution)/shard_map/ppermute | solution.py:36
  133.0 1.2 copy-done.5
  134.2 1.8 %forward.1 = (bf16[2,128,256]{2,1,0:T(8,128)(2,1)}, f32[8,128]{1,0:T(8,128)S(1)}) custom-call(s32[19]{0:T(128)S(1)} %concatenate.3.meta_ref, bf16[8,128,128]{2,1,0:T(8,128)(2,1)S(1)} %copy-done.2, bf16[16,128,256]{2,1,0:T(8,128)(2,1)S(1)} %bitcast.15, bf16[16,128,256]{2,1,0:T(8,128)(2,1)S(1)} %bitcast.19, bf16[256,256]{1,0:T(8,128)(2,1)S(1)} %copy-done.6), custom_call_target="tpu_custom_call" | custom-call | tf_op jit(solution)/shard_map/forward/pallas_call | solution.py:286
  136.3 3.6 %all-to-all-done.3.far_ref = bf16[16,40,128]{2,1,0:T(8,128)(2,1)S(1)} async-done(((bf16[16,40,128]{2,1,0:T(8,128)(2,1)}), bf16[16,40,128]{2,1,0:T(8,128)(2,1)S(1)}, u32[]{:S(2)}, u32[]{:S(2)}) %all-to-all-start.3) | async-done | bytes 163872 | tf_op jit(solution)/shard_map/all_to_all | solution.py:32
  140.7 12.3 %all-to-all-start.4 = ((f32[64,8,128]{2,1,0:T(8,128)}), f32[64,8,128]{2,1,0:T(8,128)S(1)}, u32[]{:S(2)}, u32[]{:S(2)}) async-start(f32[64,8,128]{2,1,0:T(8,128)} %far.1), calls=%async_computation.4 | async-start | bytes 524288 | tf_op jit(solution)/shard_map/all_to_all | solution.py:32
  153.7 1.2 back.1
  154.9 7.9 %all-to-all-done.4 = f32[64,8,128]{2,1,0:T(8,128)S(1)} async-done(((f32[64,8,128]{2,1,0:T(8,128)}), f32[64,8,128]{2,1,0:T(8,128)S(1)}, u32[]{:S(2)}, u32[]{:S(2)}) %all-to-all-start.4) | async-done | bytes 262176 | tf_op jit(solution)/shard_map/all_to_all | solution.py:32
  (44 shorter events, 11.6 us)
Async XLA Ops:
  7.2 54.8 %all-gather.3.cloned.1.call-start = ((), (), s32[]{:S(2)}) async-start(), calls=%async_computation.5 | async-start | bytes 1179648 | tf_op jit(solution)/shard_map/all_gather | solution.py:253
  7.9 32.7 %copy-start.2 = (bf16[8,128,128]{2,1,0:T(8,128)(2,1)S(1)}, bf16[8,128,128]{2,1,0:T(8,128)(2,1)}, u32[]{:S(2)}) copy-start(bf16[8,128,128]{2,1,0:T(8,128)(2,1)} %tiles_ref.7) | copy-start | bytes 786436
  10.0 30.5 %copy-start.3 = (bf16[256,256]{1,0:T(8,128)(2,1)S(1)}, bf16[256,256]{1,0:T(8,128)(2,1)}, u32[]{:S(2)}) copy-start(bf16[256,256]{1,0:T(8,128)(2,1)} %param.17) | copy-start | bytes 393220
  10.0 30.5 %copy-start.4 = (bf16[16,16,256]{2,1,0:T(8,128)(2,1)S(1)}, bf16[16,16,256]{2,1,0:T(8,128)(2,1)}, u32[]{:S(2)}) copy-start(bf16[16,16,256]{2,1,0:T(8,128)(2,1)} %pick.1.token_ref) | copy-start | bytes 393220
  10.0 54.2 %all-to-all-start = ((bf16[16,16,256]{2,1,0:T(8,128)(2,1)}), bf16[16,16,256]{2,1,0:T(8,128)(2,1)S(1)}, u32[]{:S(2)}, u32[]{:S(2)}) async-start(bf16[16,16,256]{2,1,0:T(8,128)(2,1)} %pick.1.token_ref), calls=%async_computation | async-start | bytes 262144 | tf_op jit(solution)/shard_map/all_to_all | solution.py:32
  39.8 0.7 copy-start.10
  41.7 4.6 %collective-permute-start = (bf16[4,2,128,256]{3,2,1,0:T(8,128)(2,1)S(1)}, bf16[4,2,128,256]{3,2,1,0:T(8,128)(2,1)S(1)}, u32[]{:S(2)}, u32[]{:S(2)}) collective-permute-start(bf16[4,2,128,256]{3,2,1,0:T(8,128)(2,1)S(1)} %get-tuple-element.26), channel_id=1, source_target_pairs={{0,1},{1,0},{2,3},{3,2},{4,5},{5,4},{6,7},{7,6},{8,9},{9,8},{10,11... | collective-permute-start | bytes 1572872 | tf_op jit(solution)/shard_map/ppermute | solution.py:36
  46.9 17.3 %collective-permute-start.1 = (bf16[2,128,256]{2,1,0:T(8,128)(2,1)S(1)}, bf16[2,128,256]{2,1,0:T(8,128)(2,1)S(1)}, u32[]{:S(2)}, u32[]{:S(2)}) collective-permute-start(bf16[2,128,256]{2,1,0:T(8,128)(2,1)S(1)} %get-tuple-element.28), channel_id=1, source_target_pairs={{0,2},{2,4},{4,6},{6,0},{1,3},{3,5},{5,7},{7,1},{8,10},{10,12},{12... | collective-permute-start | bytes 393224 | tf_op jit(solution)/shard_map/ppermute | solution.py:36
  50.2 14.1 %collective-permute-start.2 = (bf16[2,128,256]{2,1,0:T(8,128)(2,1)S(1)}, bf16[2,128,256]{2,1,0:T(8,128)(2,1)S(1)}, u32[]{:S(2)}, u32[]{:S(2)}) collective-permute-start(bf16[2,128,256]{2,1,0:T(8,128)(2,1)S(1)} %get-tuple-element.29), channel_id=1, source_target_pairs={{0,4},{2,6},{4,0},{6,2},{1,5},{3,7},{5,1},{7,3},{8,12},{10,14},{12... | collective-permute-start | bytes 393224 | tf_op jit(solution)/shard_map/ppermute | solution.py:36
  55.3 8.9 %collective-permute-start.3 = (bf16[2,128,256]{2,1,0:T(8,128)(2,1)S(1)}, bf16[2,128,256]{2,1,0:T(8,128)(2,1)S(1)}, u32[]{:S(2)}, u32[]{:S(2)}) collective-permute-start(bf16[2,128,256]{2,1,0:T(8,128)(2,1)S(1)} %get-tuple-element.30), channel_id=1, source_target_pairs={{0,6},{2,0},{4,2},{6,4},{1,7},{3,1},{5,3},{7,5},{8,14},{10,8},{12,... | collective-permute-start | bytes 393224 | tf_op jit(solution)/shard_map/ppermute | solution.py:36
  62.0 1.2 copy-start
  77.1 17.6 %all-to-all-start.2 = ((f32[64,8,128]{2,1,0:T(8,128)}), f32[64,8,128]{2,1,0:T(8,128)S(1)}, u32[]{:S(2)}, u32[]{:S(2)}) async-start(f32[64,8,128]{2,1,0:T(8,128)} %get-tuple-element.45), calls=%async_computation.2 | async-start | bytes 524288 | tf_op jit(solution)/shard_map/all_to_all | solution.py:32
  84.9 48.1 %all-gather.5.cloned.1.call-start = ((), (), s32[]{:S(2)}) async-start(), calls=%async_computation.6 | async-start | bytes 1179648 | tf_op jit(solution)/shard_map/all_gather | solution.py:285
  95.6 37.4 %copy-start.1 = (bf16[2048,256]{1,0:T(8,128)(2,1)S(1)}, bf16[2048,256]{1,0:T(8,128)(2,1)}, u32[]{:S(2)}) copy-start(bf16[2048,256]{1,0:T(8,128)(2,1)} %all-gather.3.cloned.1.call-done) | copy-start | bytes 3145732
  95.6 44.3 %all-to-all-start.3 = ((bf16[16,40,128]{2,1,0:T(8,128)(2,1)}), bf16[16,40,128]{2,1,0:T(8,128)(2,1)S(1)}, u32[]{:S(2)}, u32[]{:S(2)}) async-start(bf16[16,40,128]{2,1,0:T(8,128)(2,1)} %pack.1), calls=%async_computation.3 | async-start | bytes 327680 | tf_op jit(solution)/shard_map/all_to_all | solution.py:32
  119.1 3.9 %collective-permute-start.4 = (bf16[4,2,128,256]{3,2,1,0:T(8,128)(2,1)S(1)}, bf16[4,2,128,256]{3,2,1,0:T(8,128)(2,1)S(1)}, u32[]{:S(2)}, u32[]{:S(2)}) collective-permute-start(bf16[4,2,128,256]{3,2,1,0:T(8,128)(2,1)S(1)} %get-tuple-element.38), channel_id=1, source_target_pairs={{0,1},{1,0},{2,3},{3,2},{4,5},{5,4},{6,7},{7,6},{8,9},{9,8},{10,11... | collective-permute-start | bytes 1572872 | tf_op jit(solution)/shard_map/ppermute | solution.py:36
  123.0 9.9 %copy-start.6 = (bf16[256,256]{1,0:T(8,128)(2,1)S(1)}, bf16[256,256]{1,0:T(8,128)(2,1)}, u32[]{:S(2)}) copy-start(bf16[256,256]{1,0:T(8,128)(2,1)} %weight_ref.3) | copy-start | bytes 393220
  123.7 12.3 %collective-permute-start.5 = (bf16[2,128,256]{2,1,0:T(8,128)(2,1)S(1)}, bf16[2,128,256]{2,1,0:T(8,128)(2,1)S(1)}, u32[]{:S(2)}, u32[]{:S(2)}) collective-permute-start(bf16[2,128,256]{2,1,0:T(8,128)(2,1)S(1)} %get-tuple-element.40), channel_id=1, source_target_pairs={{0,2},{2,4},{4,6},{6,0},{1,3},{3,5},{5,7},{7,1},{8,10},{10,12},{12... | collective-permute-start | bytes 393224 | tf_op jit(solution)/shard_map/ppermute | solution.py:36
  126.7 9.3 %collective-permute-start.6 = (bf16[2,128,256]{2,1,0:T(8,128)(2,1)S(1)}, bf16[2,128,256]{2,1,0:T(8,128)(2,1)S(1)}, u32[]{:S(2)}, u32[]{:S(2)}) collective-permute-start(bf16[2,128,256]{2,1,0:T(8,128)(2,1)S(1)} %get-tuple-element.41), channel_id=1, source_target_pairs={{0,4},{2,6},{4,0},{6,2},{1,5},{3,7},{5,1},{7,3},{8,12},{10,14},{12... | collective-permute-start | bytes 393224 | tf_op jit(solution)/shard_map/ppermute | solution.py:36
  130.2 6.0 %collective-permute-start.7 = (bf16[2,128,256]{2,1,0:T(8,128)(2,1)S(1)}, bf16[2,128,256]{2,1,0:T(8,128)(2,1)S(1)}, u32[]{:S(2)}, u32[]{:S(2)}) collective-permute-start(bf16[2,128,256]{2,1,0:T(8,128)(2,1)S(1)} %get-tuple-element.42), channel_id=1, source_target_pairs={{0,6},{2,0},{4,2},{6,4},{1,7},{3,1},{5,3},{7,5},{8,14},{10,8},{12,... | collective-permute-start | bytes 393224 | tf_op jit(solution)/shard_map/ppermute | solution.py:36
  133.0 1.2 copy-start.5
  140.7 22.1 %all-to-all-start.4 = ((f32[64,8,128]{2,1,0:T(8,128)}), f32[64,8,128]{2,1,0:T(8,128)S(1)}, u32[]{:S(2)}, u32[]{:S(2)}) async-start(f32[64,8,128]{2,1,0:T(8,128)} %far.1), calls=%async_computation.4 | async-start | bytes 524288 | tf_op jit(solution)/shard_map/all_to_all | solution.py:32
  153.0 0.7 copy-start.7
  153.0 0.7 copy-start.8
  (1 other events, 0.7 us)
Sparse Core Ops, SparseCore 0:
  10.7 51.1 all-gather.2
  89.0 43.9 all-gather.4

commit v7 on v6

--- a/solution.py
+++ b/solution.py
@@ -152,8 +152,8 @@
             out_ref[...] += dot(source, high, 0, 0) + dot(source, low, 0, 0)
 
 
-def side_kernel(keep_ref, came1_ref, came2_ref, came3_ref, far_ref, own_ref, high_ref, low_ref, out_ref):
-    del own_ref
+def side_kernel(keep_ref, came1_ref, came2_ref, came3_ref, far_ref, token_ref, high_ref, low_ref, out_ref):
+    del token_ref
     terms = keep_ref[...]
     for came_ref in (came1_ref, came2_ref, came3_ref):
         terms += came_ref[...].astype(F32)
@@ -180,7 +180,7 @@
     gw = own_ref[...] + dot(arrived, high_ref[...], 0, 0) + dot(arrived, low_ref[...], 0, 0)
     for c in range(CHUNKS):
         row, col = c // 2 * 8, c % 2 * 128
-        gw_ref[c] = gw[row:row + 8, col:col + 128]
+        gw_ref[c] = gw[row:row + 8, col:col + 128].astype(BF16)
     x, zl, zh, s = digits(rows, 1, (X, ZL, ZH, SLOTS))
     order = permutation(boundary_row(x, zh, zl, s) == lax.broadcasted_iota(jnp.int32, (rows, rows), 0))
     arrived_ref[...] = dot(order, arrived).astype(BF16)
@@ -194,7 +194,7 @@
     side = dot(order, side_ref[:, rows // (X * ZL):, :].reshape(rows, -1)).astype(BF16)
     out_ref[:, :lines, :] = side[:, :128].reshape(ZH, lines, 128)
     out_ref[:, lines:2 * lines, :] = side[:, 128:].reshape(ZH, lines, 128)
-    near = jnp.sum(near_ref[...], axis=0).astype(BF16)
+    near = jnp.sum(near_ref[...].astype(F32), axis=0).astype(BF16)
     for z in range(ZH):
         out_ref[z, 2 * lines:, :] = near
 
@@ -272,11 +272,11 @@
     keep, sums = exchange(1, "bound", outgoing)
     gw_own = call(own_kernel, shape((width, width), F32), [SMEM] + [VMEM] * 3, "own")(meta, tiles, cotangent, all_own)
     high, low, side = call(
-        side_kernel, (square, square, shape((X * ZL, 2 * rows // (X * ZL), width), BF16)), [VMEM] * 5 + [ANY], "side",
-    )(keep, *sums, landed, gw_own)
+        side_kernel, (square, square, shape((X * ZL, 2 * rows // (X * ZL), width), BF16)), [VMEM] * 6, "side",
+    )(keep, *sums, landed, all_own[0, :8, :128])
     side = swap(side, SIDE)
     gw, arrived, mid_token = call(
-        mid_kernel, (shape((CHUNKS, 8, 128), F32), square, token), [VMEM] * 4, "mid",
+        mid_kernel, (shape((CHUNKS, 8, 128), BF16), square, token), [VMEM] * 4, "mid",
     )(gw_own, high, low, side)
     near = swap(gw, NEAR)
     packed = call(pack_kernel, shape((ZH, 2 * lines + 8, 128), BF16), [VMEM] * 2, "pack")(side, near)

time: 171 us -> 167 us (0.977)
  blocking collectives: 11.4 us -> 0 us
  starting transfers between devices: 96.6 us -> 99.7 us
  waiting for transfers between devices: 30.1 us -> 32.4 us
  Pallas kernels: 12.8 us -> 14.6 us
    all_to_all x1 -> x0, blocking collectives: 11.4 us -> none  [swap(): return lax.all_to_all(x, axes, split_axis=0, concat_axis=0, tiled=True)]
    all_to_all x4 -> x5, starting transfers between devices: 71.6 us -> 73.8 us  [swap(): return lax.all_to_all(x, axes, split_axis=0, concat_axis=0, tiled=True)]
    all_to_all x4 -> x5, waiting for transfers between devices: 20.6 us -> 22.3 us  [swap(): return lax.all_to_all(x, axes, split_axis=0, concat_axis=0, tiled=True)]
    unnamed x23 -> x21, local copies, waits for them, and re-layouts: 4.5 us -> 3.27 us
  transfers between devices with their start and end apart: 14 -> 15, of which waited for: 8 -> 8; matrix products, arithmetic and copies ran while one was open for 0% -> 0% of each run, Pallas kernels for 6% -> 7%
where the time goes in v7:
time: 167 us; the launch traced here: 166 us
  starting transfers between devices  99.7 us (60%)
  waiting for transfers between devices  32.4 us (19%)
  between operations  14.9 us (9%)
  Pallas kernels  14.6 us (9%)
  local copies, waits for them, and re-layouts  4.09 us (2%)
    all_to_all x5, starting transfers between devices, swap(): return lax.all_to_all(x, axes, split_axis=0, concat_axis=0, tiled=True)  73.8 us
    ppermute x8, starting transfers between devices, shift(): return lax.ppermute(x, axis, [(i, (i + step) % size) for i in range(size)])  25.8 us
    all_to_all x5, waiting for transfers between devices, swap(): return lax.all_to_all(x, axes, split_axis=0, concat_axis=0, tiled=True)  22.3 us
    all_gather x1, waiting for transfers between devices, per_device(): all_own = lax.all_gather(features, DEV, axis=0, tiled=True).reshape(blocked)  4.59 us
  transfers between devices with their start and end apart: 15, of which 8 were waited for; matrix products, arithmetic and copies ran while one was open for 0% of the time, Pallas kernels for 7%

profile of v7, /device:TPU:1, one launch (start us, length us, event | category | flops | bytes accessed | tf_op | source)
XLA Modules:
  0.0 165.6 jit_solution(8721621348696258949)
XLA Ops:
  7.9 2.1 %pick.1.token_ref = bf16[16,16,256]{2,1,0:T(8,128)(2,1)} custom-call(s32[2,128]{1,0:T(2,128)} %bitcast.23, s32[1,128]{1,0:T(1,128)} %count_ref.3, bf16[256,256]{1,0:T(8,128)(2,1)} %features_ref.1), custom_call_target="tpu_custom_call" | custom-call | tf_op jit(solution)/shard_map/pick/pallas_call | solution.py:255
  10.0 29.1 %all-to-all-start = ((bf16[16,16,256]{2,1,0:T(8,128)(2,1)}), bf16[16,16,256]{2,1,0:T(8,128)(2,1)S(1)}, u32[]{:S(2)}, u32[]{:S(2)}) async-start(bf16[16,16,256]{2,1,0:T(8,128)(2,1)} %pick.1.token_ref), calls=%async_computation | async-start | bytes 262144 | tf_op jit(solution)/shard_map/all_to_all | solution.py:32
  40.6 1.3 terms_bound.1
  41.9 3.3 %collective-permute-start = (bf16[4,2,128,256]{3,2,1,0:T(8,128)(2,1)S(1)}, bf16[4,2,128,256]{3,2,1,0:T(8,128)(2,1)S(1)}, u32[]{:S(2)}, u32[]{:S(2)}) collective-permute-start(bf16[4,2,128,256]{3,2,1,0:T(8,128)(2,1)S(1)} %get-tuple-element.26), channel_id=1, source_target_pairs={{0,1},{1,0},{2,3},{3,2},{4,5},{5,4},{6,7},{7,6},{8,9},{9,8},{10,11... | collective-permute-start | bytes 1572872 | tf_op jit(solution)/shard_map/ppermute | solution.py:36
  45.2 1.5 collective-permute-done.came_ref
  47.4 2.6 %collective-permute-start.1 = (bf16[2,128,256]{2,1,0:T(8,128)(2,1)S(1)}, bf16[2,128,256]{2,1,0:T(8,128)(2,1)S(1)}, u32[]{:S(2)}, u32[]{:S(2)}) collective-permute-start(bf16[2,128,256]{2,1,0:T(8,128)(2,1)S(1)} %get-tuple-element.28), channel_id=1, source_target_pairs={{0,2},{2,4},{4,6},{6,0},{1,3},{3,5},{5,7},{7,1},{8,10},{10,12},{12... | collective-permute-start | bytes 393224 | tf_op jit(solution)/shard_map/ppermute | solution.py:36
  50.0 4.9 %collective-permute-start.2 = (bf16[2,128,256]{2,1,0:T(8,128)(2,1)S(1)}, bf16[2,128,256]{2,1,0:T(8,128)(2,1)S(1)}, u32[]{:S(2)}, u32[]{:S(2)}) collective-permute-start(bf16[2,128,256]{2,1,0:T(8,128)(2,1)S(1)} %get-tuple-element.29), channel_id=1, source_target_pairs={{0,4},{2,6},{4,0},{6,2},{1,5},{3,7},{5,1},{7,3},{8,12},{10,14},{12... | collective-permute-start | bytes 393224 | tf_op jit(solution)/shard_map/ppermute | solution.py:36
  54.9 3.0 %collective-permute-start.3 = (bf16[2,128,256]{2,1,0:T(8,128)(2,1)S(1)}, bf16[2,128,256]{2,1,0:T(8,128)(2,1)S(1)}, u32[]{:S(2)}, u32[]{:S(2)}) collective-permute-start(bf16[2,128,256]{2,1,0:T(8,128)(2,1)S(1)} %get-tuple-element.30), channel_id=1, source_target_pairs={{0,6},{2,0},{4,2},{6,4},{1,7},{3,1},{5,3},{7,5},{8,14},{10,8},{12,... | collective-permute-start | bytes 393224 | tf_op jit(solution)/shard_map/ppermute | solution.py:36
  57.9 4.6 %all-gather.3.cloned.1.call-done = bf16[2048,256]{1,0:T(8,128)(2,1)} async-done(((bf16[256,256]{1,0:T(8,128)(2,1)}), bf16[2048,256]{1,0:T(8,128)(2,1)}) %all-gather.3.cloned.1.call-update) | async-done | bytes 1048592 | tf_op jit(solution)/shard_map/all_gather | solution.py:253
  64.3 4.3 %all-to-all-start.1 = ((bf16[8,64,256]{2,1,0:T(8,128)(2,1)}), bf16[8,64,256]{2,1,0:T(8,128)(2,1)S(1)}, u32[]{:S(2)}, u32[]{:S(2)}) async-start(bf16[8,64,256]{2,1,0:T(8,128)(2,1)} %get-tuple-element.33), calls=%async_computation.1 | async-start | bytes 524288 | tf_op jit(solution)/shard_map/all_to_all | solution.py:32
  68.7 1.4 own.1.own_ref
  70.1 4.7 %all-to-all-done.1.side_ref = bf16[8,64,256]{2,1,0:T(8,128)(2,1)S(1)} async-done(((bf16[8,64,256]{2,1,0:T(8,128)(2,1)}), bf16[8,64,256]{2,1,0:T(8,128)(2,1)S(1)}, u32[]{:S(2)}, u32[]{:S(2)}) %all-to-all-start.1) | async-done | bytes 262176 | tf_op jit(solution)/shard_map/all_to_all | solution.py:32
  75.8 9.9 %all-to-all-start.2 = ((bf16[64,8,128]{2,1,0:T(8,128)(2,1)}), bf16[64,8,128]{2,1,0:T(8,128)(2,1)S(1)}, u32[]{:S(2)}, u32[]{:S(2)}) async-start(bf16[64,8,128]{2,1,0:T(8,128)(2,1)} %get-tuple-element.45), calls=%async_computation.2 | async-start | bytes 262144 | tf_op jit(solution)/shard_map/all_to_all | solution.py:32
  86.5 7.8 %all-to-all-done.2.near_ref = bf16[64,8,128]{2,1,0:T(8,128)(2,1)S(1)} async-done(((bf16[64,8,128]{2,1,0:T(8,128)(2,1)}), bf16[64,8,128]{2,1,0:T(8,128)(2,1)S(1)}, u32[]{:S(2)}, u32[]{:S(2)}) %all-to-all-start.2) | async-done | bytes 131104 | tf_op jit(solution)/shard_map/all_to_all | solution.py:32
  95.1 19.2 %all-to-all-start.3 = ((bf16[16,40,128]{2,1,0:T(8,128)(2,1)}), bf16[16,40,128]{2,1,0:T(8,128)(2,1)S(1)}, u32[]{:S(2)}, u32[]{:S(2)}) async-start(bf16[16,40,128]{2,1,0:T(8,128)(2,1)} %pack.1), calls=%async_computation.3 | async-start | bytes 327680 | tf_op jit(solution)/shard_map/all_to_all | solution.py:32
  115.7 3.0 %collective-permute-start.4 = (bf16[4,2,128,256]{3,2,1,0:T(8,128)(2,1)S(1)}, bf16[4,2,128,256]{3,2,1,0:T(8,128)(2,1)S(1)}, u32[]{:S(2)}, u32[]{:S(2)}) collective-permute-start(bf16[4,2,128,256]{3,2,1,0:T(8,128)(2,1)S(1)} %get-tuple-element.38), channel_id=1, source_target_pairs={{0,1},{1,0},{2,3},{3,2},{4,5},{5,4},{6,7},{7,6},{8,9},{9,8},{10,11... | collective-permute-start | bytes 1572872 | tf_op jit(solution)/shard_map/ppermute | solution.py:36
  118.7 1.5 collective-permute-done.4.came_ref
  120.9 1.9 %collective-permute-start.5 = (bf16[2,128,256]{2,1,0:T(8,128)(2,1)S(1)}, bf16[2,128,256]{2,1,0:T(8,128)(2,1)S(1)}, u32[]{:S(2)}, u32[]{:S(2)}) collective-permute-start(bf16[2,128,256]{2,1,0:T(8,128)(2,1)S(1)} %get-tuple-element.40), channel_id=1, source_target_pairs={{0,2},{2,4},{4,6},{6,0},{1,3},{3,5},{5,7},{7,1},{8,10},{10,12},{12... | collective-permute-start | bytes 393224 | tf_op jit(solution)/shard_map/ppermute | solution.py:36
  122.8 3.5 %collective-permute-start.6 = (bf16[2,128,256]{2,1,0:T(8,128)(2,1)S(1)}, bf16[2,128,256]{2,1,0:T(8,128)(2,1)S(1)}, u32[]{:S(2)}, u32[]{:S(2)}) collective-permute-start(bf16[2,128,256]{2,1,0:T(8,128)(2,1)S(1)} %get-tuple-element.41), channel_id=1, source_target_pairs={{0,4},{2,6},{4,0},{6,2},{1,5},{3,7},{5,1},{7,3},{8,12},{10,14},{12... | collective-permute-start | bytes 393224 | tf_op jit(solution)/shard_map/ppermute | solution.py:36
  126.3 3.7 %collective-permute-start.7 = (bf16[2,128,256]{2,1,0:T(8,128)(2,1)S(1)}, bf16[2,128,256]{2,1,0:T(8,128)(2,1)S(1)}, u32[]{:S(2)}, u32[]{:S(2)}) collective-permute-start(bf16[2,128,256]{2,1,0:T(8,128)(2,1)S(1)} %get-tuple-element.42), channel_id=1, source_target_pairs={{0,6},{2,0},{4,2},{6,4},{1,7},{3,1},{5,3},{7,5},{8,14},{10,8},{12,... | collective-permute-start | bytes 393224 | tf_op jit(solution)/shard_map/ppermute | solution.py:36
  132.3 2.1 %forward.1 = (bf16[2,128,256]{2,1,0:T(8,128)(2,1)}, f32[8,128]{1,0:T(8,128)S(1)}) custom-call(s32[19]{0:T(128)S(1)} %concatenate.3.meta_ref, bf16[8,128,128]{2,1,0:T(8,128)(2,1)S(1)} %copy-done.1, bf16[16,128,256]{2,1,0:T(8,128)(2,1)S(1)} %bitcast.18, bf16[16,128,256]{2,1,0:T(8,128)(2,1)S(1)} %bitcast.22, bf16[256,256]{1,0:T(8,128)(2,1)S(1)} %copy-done.5), custom_call_target="tpu_custom_call" | custom-call | tf_op jit(solution)/shard_map/forward/pallas_call | solution.py:286
  134.4 1.9 %all-to-all-done.3.far_ref = bf16[16,40,128]{2,1,0:T(8,128)(2,1)S(1)} async-done(((bf16[16,40,128]{2,1,0:T(8,128)(2,1)}), bf16[16,40,128]{2,1,0:T(8,128)(2,1)S(1)}, u32[]{:S(2)}, u32[]{:S(2)}) %all-to-all-start.3) | async-done | bytes 163872 | tf_op jit(solution)/shard_map/all_to_all | solution.py:32
  137.1 11.2 %all-to-all-start.4 = ((f32[64,8,128]{2,1,0:T(8,128)}), f32[64,8,128]{2,1,0:T(8,128)S(1)}, u32[]{:S(2)}, u32[]{:S(2)}) async-start(f32[64,8,128]{2,1,0:T(8,128)} %far.1), calls=%async_computation.4 | async-start | bytes 524288 | tf_op jit(solution)/shard_map/all_to_all | solution.py:32
  150.2 7.9 %all-to-all-done.4 = f32[64,8,128]{2,1,0:T(8,128)S(1)} async-done(((f32[64,8,128]{2,1,0:T(8,128)}), f32[64,8,128]{2,1,0:T(8,128)S(1)}, u32[]{:S(2)}, u32[]{:S(2)}) %all-to-all-start.4) | async-done | bytes 262176 | tf_op jit(solution)/shard_map/all_to_all | solution.py:32
  (44 shorter events, 14.3 us)
Async XLA Ops:
  7.2 55.3 %all-gather.3.cloned.1.call-start = ((), (), s32[]{:S(2)}) async-start(), calls=%async_computation.5 | async-start | bytes 1179648 | tf_op jit(solution)/shard_map/all_gather | solution.py:253
  7.9 32.7 %copy-start.1 = (bf16[8,128,128]{2,1,0:T(8,128)(2,1)S(1)}, bf16[8,128,128]{2,1,0:T(8,128)(2,1)}, u32[]{:S(2)}) copy-start(bf16[8,128,128]{2,1,0:T(8,128)(2,1)} %tiles_ref.7) | copy-start | bytes 786436
  10.0 30.5 %copy-start.2 = (bf16[256,256]{1,0:T(8,128)(2,1)S(1)}, bf16[256,256]{1,0:T(8,128)(2,1)}, u32[]{:S(2)}) copy-start(bf16[256,256]{1,0:T(8,128)(2,1)} %param.17) | copy-start | bytes 393220
  10.0 30.5 %copy-start.3 = (bf16[16,16,256]{2,1,0:T(8,128)(2,1)S(1)}, bf16[16,16,256]{2,1,0:T(8,128)(2,1)}, u32[]{:S(2)}) copy-start(bf16[16,16,256]{2,1,0:T(8,128)(2,1)} %pick.1.token_ref) | copy-start | bytes 393220
  10.0 53.2 %all-to-all-start = ((bf16[16,16,256]{2,1,0:T(8,128)(2,1)}), bf16[16,16,256]{2,1,0:T(8,128)(2,1)S(1)}, u32[]{:S(2)}, u32[]{:S(2)}) async-start(bf16[16,16,256]{2,1,0:T(8,128)(2,1)} %pick.1.token_ref), calls=%async_computation | async-start | bytes 262144 | tf_op jit(solution)/shard_map/all_to_all | solution.py:32
  39.8 0.7 copy-start.9
  41.9 4.8 %collective-permute-start = (bf16[4,2,128,256]{3,2,1,0:T(8,128)(2,1)S(1)}, bf16[4,2,128,256]{3,2,1,0:T(8,128)(2,1)S(1)}, u32[]{:S(2)}, u32[]{:S(2)}) collective-permute-start(bf16[4,2,128,256]{3,2,1,0:T(8,128)(2,1)S(1)} %get-tuple-element.26), channel_id=1, source_target_pairs={{0,1},{1,0},{2,3},{3,2},{4,5},{5,4},{6,7},{7,6},{8,9},{9,8},{10,11... | collective-permute-start | bytes 1572872 | tf_op jit(solution)/shard_map/ppermute | solution.py:36
  47.4 15.9 %collective-permute-start.1 = (bf16[2,128,256]{2,1,0:T(8,128)(2,1)S(1)}, bf16[2,128,256]{2,1,0:T(8,128)(2,1)S(1)}, u32[]{:S(2)}, u32[]{:S(2)}) collective-permute-start(bf16[2,128,256]{2,1,0:T(8,128)(2,1)S(1)} %get-tuple-element.28), channel_id=1, source_target_pairs={{0,2},{2,4},{4,6},{6,0},{1,3},{3,5},{5,7},{7,1},{8,10},{10,12},{12... | collective-permute-start | bytes 393224 | tf_op jit(solution)/shard_map/ppermute | solution.py:36
  50.0 13.2 %collective-permute-start.2 = (bf16[2,128,256]{2,1,0:T(8,128)(2,1)S(1)}, bf16[2,128,256]{2,1,0:T(8,128)(2,1)S(1)}, u32[]{:S(2)}, u32[]{:S(2)}) collective-permute-start(bf16[2,128,256]{2,1,0:T(8,128)(2,1)S(1)} %get-tuple-element.29), channel_id=1, source_target_pairs={{0,4},{2,6},{4,0},{6,2},{1,5},{3,7},{5,1},{7,3},{8,12},{10,14},{12... | collective-permute-start | bytes 393224 | tf_op jit(solution)/shard_map/ppermute | solution.py:36
  54.9 8.3 %collective-permute-start.3 = (bf16[2,128,256]{2,1,0:T(8,128)(2,1)S(1)}, bf16[2,128,256]{2,1,0:T(8,128)(2,1)S(1)}, u32[]{:S(2)}, u32[]{:S(2)}) collective-permute-start(bf16[2,128,256]{2,1,0:T(8,128)(2,1)S(1)} %get-tuple-element.30), channel_id=1, source_target_pairs={{0,6},{2,0},{4,2},{6,4},{1,7},{3,1},{5,3},{7,5},{8,14},{10,8},{12,... | collective-permute-start | bytes 393224 | tf_op jit(solution)/shard_map/ppermute | solution.py:36
  62.5 6.2 %copy-start = (bf16[2048,256]{1,0:T(8,128)(2,1)S(1)}, bf16[2048,256]{1,0:T(8,128)(2,1)}, u32[]{:S(2)}) copy-start(bf16[2048,256]{1,0:T(8,128)(2,1)} %all-gather.3.cloned.1.call-done) | copy-start | bytes 3145732
  64.3 10.4 %all-to-all-start.1 = ((bf16[8,64,256]{2,1,0:T(8,128)(2,1)}), bf16[8,64,256]{2,1,0:T(8,128)(2,1)S(1)}, u32[]{:S(2)}, u32[]{:S(2)}) async-start(bf16[8,64,256]{2,1,0:T(8,128)(2,1)} %get-tuple-element.33), calls=%async_computation.1 | async-start | bytes 524288 | tf_op jit(solution)/shard_map/all_to_all | solution.py:32
  75.8 18.4 %all-to-all-start.2 = ((bf16[64,8,128]{2,1,0:T(8,128)(2,1)}), bf16[64,8,128]{2,1,0:T(8,128)(2,1)S(1)}, u32[]{:S(2)}, u32[]{:S(2)}) async-start(bf16[64,8,128]{2,1,0:T(8,128)(2,1)} %get-tuple-element.45), calls=%async_computation.2 | async-start | bytes 262144 | tf_op jit(solution)/shard_map/all_to_all | solution.py:32
  85.7 45.4 %all-gather.5.cloned.1.call-start = ((), (), s32[]{:S(2)}) async-start(), calls=%async_computation.6 | async-start | bytes 1179648 | tf_op jit(solution)/shard_map/all_gather | solution.py:285
  95.1 41.2 %all-to-all-start.3 = ((bf16[16,40,128]{2,1,0:T(8,128)(2,1)}), bf16[16,40,128]{2,1,0:T(8,128)(2,1)S(1)}, u32[]{:S(2)}, u32[]{:S(2)}) async-start(bf16[16,40,128]{2,1,0:T(8,128)(2,1)} %pack.1), calls=%async_computation.3 | async-start | bytes 327680 | tf_op jit(solution)/shard_map/all_to_all | solution.py:32
  115.7 4.5 %collective-permute-start.4 = (bf16[4,2,128,256]{3,2,1,0:T(8,128)(2,1)S(1)}, bf16[4,2,128,256]{3,2,1,0:T(8,128)(2,1)S(1)}, u32[]{:S(2)}, u32[]{:S(2)}) collective-permute-start(bf16[4,2,128,256]{3,2,1,0:T(8,128)(2,1)S(1)} %get-tuple-element.38), channel_id=1, source_target_pairs={{0,1},{1,0},{2,3},{3,2},{4,5},{5,4},{6,7},{7,6},{8,9},{9,8},{10,11... | collective-permute-start | bytes 1572872 | tf_op jit(solution)/shard_map/ppermute | solution.py:36
  120.2 10.9 %copy-start.5 = (bf16[256,256]{1,0:T(8,128)(2,1)S(1)}, bf16[256,256]{1,0:T(8,128)(2,1)}, u32[]{:S(2)}) copy-start(bf16[256,256]{1,0:T(8,128)(2,1)} %weight_ref.3) | copy-start | bytes 393220
  120.9 13.5 %collective-permute-start.5 = (bf16[2,128,256]{2,1,0:T(8,128)(2,1)S(1)}, bf16[2,128,256]{2,1,0:T(8,128)(2,1)S(1)}, u32[]{:S(2)}, u32[]{:S(2)}) collective-permute-start(bf16[2,128,256]{2,1,0:T(8,128)(2,1)S(1)} %get-tuple-element.40), channel_id=1, source_target_pairs={{0,2},{2,4},{4,6},{6,0},{1,3},{3,5},{5,7},{7,1},{8,10},{10,12},{12... | collective-permute-start | bytes 393224 | tf_op jit(solution)/shard_map/ppermute | solution.py:36
  122.8 11.6 %collective-permute-start.6 = (bf16[2,128,256]{2,1,0:T(8,128)(2,1)S(1)}, bf16[2,128,256]{2,1,0:T(8,128)(2,1)S(1)}, u32[]{:S(2)}, u32[]{:S(2)}) collective-permute-start(bf16[2,128,256]{2,1,0:T(8,128)(2,1)S(1)} %get-tuple-element.41), channel_id=1, source_target_pairs={{0,4},{2,6},{4,0},{6,2},{1,5},{3,7},{5,1},{7,3},{8,12},{10,14},{12... | collective-permute-start | bytes 393224 | tf_op jit(solution)/shard_map/ppermute | solution.py:36
  126.3 8.1 %collective-permute-start.7 = (bf16[2,128,256]{2,1,0:T(8,128)(2,1)S(1)}, bf16[2,128,256]{2,1,0:T(8,128)(2,1)S(1)}, u32[]{:S(2)}, u32[]{:S(2)}) collective-permute-start(bf16[2,128,256]{2,1,0:T(8,128)(2,1)S(1)} %get-tuple-element.42), channel_id=1, source_target_pairs={{0,6},{2,0},{4,2},{6,4},{1,7},{3,1},{5,3},{7,5},{8,14},{10,8},{12,... | collective-permute-start | bytes 393224 | tf_op jit(solution)/shard_map/ppermute | solution.py:36
  131.1 1.2 copy-start.4
  137.1 21.0 %all-to-all-start.4 = ((f32[64,8,128]{2,1,0:T(8,128)}), f32[64,8,128]{2,1,0:T(8,128)S(1)}, u32[]{:S(2)}, u32[]{:S(2)}) async-start(f32[64,8,128]{2,1,0:T(8,128)} %far.1), calls=%async_computation.4 | async-start | bytes 524288 | tf_op jit(solution)/shard_map/all_to_all | solution.py:32
  148.3 0.7 copy-start.6
  148.3 0.7 copy-start.7
  (1 other events, 0.7 us)
Sparse Core Ops, SparseCore 0:
  10.7 51.7 all-gather.2
  89.9 41.1 all-gather.4

commit v8 on v7

--- a/solution.py
+++ b/solution.py
@@ -55,11 +55,11 @@
 
 
 def digits(count, dim, sizes):
-    left = lax.broadcasted_iota(jnp.int32, (count, count), dim)
+    left = lax.broadcasted_iota(jnp.int32, (count, 1) if dim == 0 else (1, count), dim)
     found = []
     for size in reversed(sizes):
-        found.append(lax.rem(left, size))
-        left = lax.div(left, size)
+        found.append(left & (size - 1))
+        left = left >> (size.bit_length() - 1)
     return found[::-1]
 
 

time: 167 us -> 167 us (level)
  transfers between devices with their start and end apart: 15 -> 15, of which waited for: 8 -> 8; matrix products, arithmetic and copies ran while one was open for 0% -> 0% of each run, Pallas kernels for 7% -> 6%
where the time goes in v8:
time: 167 us; the launch traced here: 166 us
  starting transfers between devices  100 us (60%)
  waiting for transfers between devices  33.6 us (20%)
  between operations  14.9 us (9%)
  Pallas kernels  13 us (8%)
  local copies, waits for them, and re-layouts  4.09 us (2%)
    all_to_all x5, starting transfers between devices, swap(): return lax.all_to_all(x, axes, split_axis=0, concat_axis=0, tiled=True)  74.1 us
    ppermute x8, starting transfers between devices, shift(): return lax.ppermute(x, axis, [(i, (i + step) % size) for i in range(size)])  26.2 us
    all_to_all x5, waiting for transfers between devices, swap(): return lax.all_to_all(x, axes, split_axis=0, concat_axis=0, tiled=True)  23.7 us
    all_gather x1, waiting for transfers between devices, per_device(): all_own = lax.all_gather(features, DEV, axis=0, tiled=True).reshape(blocked)  4.62 us
  transfers between devices with their start and end apart: 15, of which 8 were waited for; matrix products, arithmetic and copies ran while one was open for 0% of the time, Pallas kernels for 6%

profile of v8, /device:TPU:1, one launch (start us, length us, event | category | flops | bytes accessed | tf_op | source)
XLA Modules:
  0.0 166.0 jit_solution(13072002781334085769)
XLA Ops:
  7.9 2.1 %pick.1.token_ref = bf16[16,16,256]{2,1,0:T(8,128)(2,1)} custom-call(s32[2,128]{1,0:T(2,128)} %bitcast.23, s32[1,128]{1,0:T(1,128)} %count_ref.3, bf16[256,256]{1,0:T(8,128)(2,1)} %features_ref.1), custom_call_target="tpu_custom_call" | custom-call | tf_op jit(solution)/shard_map/pick/pallas_call | solution.py:255
  10.0 29.1 %all-to-all-start = ((bf16[16,16,256]{2,1,0:T(8,128)(2,1)}), bf16[16,16,256]{2,1,0:T(8,128)(2,1)S(1)}, u32[]{:S(2)}, u32[]{:S(2)}) async-start(bf16[16,16,256]{2,1,0:T(8,128)(2,1)} %pick.1.token_ref), calls=%async_computation | async-start | bytes 262144 | tf_op jit(solution)/shard_map/all_to_all | solution.py:32
  40.6 1.3 terms_bound.1
  41.9 2.7 %collective-permute-start = (bf16[4,2,128,256]{3,2,1,0:T(8,128)(2,1)S(1)}, bf16[4,2,128,256]{3,2,1,0:T(8,128)(2,1)S(1)}, u32[]{:S(2)}, u32[]{:S(2)}) collective-permute-start(bf16[4,2,128,256]{3,2,1,0:T(8,128)(2,1)S(1)} %get-tuple-element.26), channel_id=1, source_target_pairs={{0,1},{1,0},{2,3},{3,2},{4,5},{5,4},{6,7},{7,6},{8,9},{9,8},{10,11... | collective-permute-start | bytes 1572872 | tf_op jit(solution)/shard_map/ppermute | solution.py:36
  44.5 1.5 collective-permute-done.came_ref
  46.7 3.0 %collective-permute-start.1 = (bf16[2,128,256]{2,1,0:T(8,128)(2,1)S(1)}, bf16[2,128,256]{2,1,0:T(8,128)(2,1)S(1)}, u32[]{:S(2)}, u32[]{:S(2)}) collective-permute-start(bf16[2,128,256]{2,1,0:T(8,128)(2,1)S(1)} %get-tuple-element.28), channel_id=1, source_target_pairs={{0,2},{2,4},{4,6},{6,0},{1,3},{3,5},{5,7},{7,1},{8,10},{10,12},{12... | collective-permute-start | bytes 393224 | tf_op jit(solution)/shard_map/ppermute | solution.py:36
  49.8 5.1 %collective-permute-start.2 = (bf16[2,128,256]{2,1,0:T(8,128)(2,1)S(1)}, bf16[2,128,256]{2,1,0:T(8,128)(2,1)S(1)}, u32[]{:S(2)}, u32[]{:S(2)}) collective-permute-start(bf16[2,128,256]{2,1,0:T(8,128)(2,1)S(1)} %get-tuple-element.29), channel_id=1, source_target_pairs={{0,4},{2,6},{4,0},{6,2},{1,5},{3,7},{5,1},{7,3},{8,12},{10,14},{12... | collective-permute-start | bytes 393224 | tf_op jit(solution)/shard_map/ppermute | solution.py:36
  54.9 3.0 %collective-permute-start.3 = (bf16[2,128,256]{2,1,0:T(8,128)(2,1)S(1)}, bf16[2,128,256]{2,1,0:T(8,128)(2,1)S(1)}, u32[]{:S(2)}, u32[]{:S(2)}) collective-permute-start(bf16[2,128,256]{2,1,0:T(8,128)(2,1)S(1)} %get-tuple-element.30), channel_id=1, source_target_pairs={{0,6},{2,0},{4,2},{6,4},{1,7},{3,1},{5,3},{7,5},{8,14},{10,8},{12,... | collective-permute-start | bytes 393224 | tf_op jit(solution)/shard_map/ppermute | solution.py:36
  57.9 4.6 %all-gather.3.cloned.1.call-done = bf16[2048,256]{1,0:T(8,128)(2,1)} async-done(((bf16[256,256]{1,0:T(8,128)(2,1)}), bf16[2048,256]{1,0:T(8,128)(2,1)}) %all-gather.3.cloned.1.call-update) | async-done | bytes 1048592 | tf_op jit(solution)/shard_map/all_gather | solution.py:253
  64.3 3.5 %all-to-all-start.1 = ((bf16[8,64,256]{2,1,0:T(8,128)(2,1)}), bf16[8,64,256]{2,1,0:T(8,128)(2,1)S(1)}, u32[]{:S(2)}, u32[]{:S(2)}) async-start(bf16[8,64,256]{2,1,0:T(8,128)(2,1)} %get-tuple-element.33), calls=%async_computation.1 | async-start | bytes 524288 | tf_op jit(solution)/shard_map/all_to_all | solution.py:32
  68.4 5.5 %all-to-all-done.1.side_ref = bf16[8,64,256]{2,1,0:T(8,128)(2,1)S(1)} async-done(((bf16[8,64,256]{2,1,0:T(8,128)(2,1)}), bf16[8,64,256]{2,1,0:T(8,128)(2,1)S(1)}, u32[]{:S(2)}, u32[]{:S(2)}) %all-to-all-start.1) | async-done | bytes 262176 | tf_op jit(solution)/shard_map/all_to_all | solution.py:32
  74.9 10.7 %all-to-all-start.2 = ((bf16[64,8,128]{2,1,0:T(8,128)(2,1)}), bf16[64,8,128]{2,1,0:T(8,128)(2,1)S(1)}, u32[]{:S(2)}, u32[]{:S(2)}) async-start(bf16[64,8,128]{2,1,0:T(8,128)(2,1)} %get-tuple-element.45), calls=%async_computation.2 | async-start | bytes 262144 | tf_op jit(solution)/shard_map/all_to_all | solution.py:32
  86.4 7.8 %all-to-all-done.2.near_ref = bf16[64,8,128]{2,1,0:T(8,128)(2,1)S(1)} async-done(((bf16[64,8,128]{2,1,0:T(8,128)(2,1)}), bf16[64,8,128]{2,1,0:T(8,128)(2,1)S(1)}, u32[]{:S(2)}, u32[]{:S(2)}) %all-to-all-start.2) | async-done | bytes 131104 | tf_op jit(solution)/shard_map/all_to_all | solution.py:32
  95.1 19.6 %all-to-all-start.3 = ((bf16[16,40,128]{2,1,0:T(8,128)(2,1)}), bf16[16,40,128]{2,1,0:T(8,128)(2,1)S(1)}, u32[]{:S(2)}, u32[]{:S(2)}) async-start(bf16[16,40,128]{2,1,0:T(8,128)(2,1)} %pack.1), calls=%async_computation.3 | async-start | bytes 327680 | tf_op jit(solution)/shard_map/all_to_all | solution.py:32
  115.6 2.8 %collective-permute-start.4 = (bf16[4,2,128,256]{3,2,1,0:T(8,128)(2,1)S(1)}, bf16[4,2,128,256]{3,2,1,0:T(8,128)(2,1)S(1)}, u32[]{:S(2)}, u32[]{:S(2)}) collective-permute-start(bf16[4,2,128,256]{3,2,1,0:T(8,128)(2,1)S(1)} %get-tuple-element.38), channel_id=1, source_target_pairs={{0,1},{1,0},{2,3},{3,2},{4,5},{5,4},{6,7},{7,6},{8,9},{9,8},{10,11... | collective-permute-start | bytes 1572872 | tf_op jit(solution)/shard_map/ppermute | solution.py:36
  118.4 1.5 collective-permute-done.4.came_ref
  120.6 2.7 %collective-permute-start.5 = (bf16[2,128,256]{2,1,0:T(8,128)(2,1)S(1)}, bf16[2,128,256]{2,1,0:T(8,128)(2,1)S(1)}, u32[]{:S(2)}, u32[]{:S(2)}) collective-permute-start(bf16[2,128,256]{2,1,0:T(8,128)(2,1)S(1)} %get-tuple-element.40), channel_id=1, source_target_pairs={{0,2},{2,4},{4,6},{6,0},{1,3},{3,5},{5,7},{7,1},{8,10},{10,12},{12... | collective-permute-start | bytes 393224 | tf_op jit(solution)/shard_map/ppermute | solution.py:36
  123.3 4.1 %collective-permute-start.6 = (bf16[2,128,256]{2,1,0:T(8,128)(2,1)S(1)}, bf16[2,128,256]{2,1,0:T(8,128)(2,1)S(1)}, u32[]{:S(2)}, u32[]{:S(2)}) collective-permute-start(bf16[2,128,256]{2,1,0:T(8,128)(2,1)S(1)} %get-tuple-element.41), channel_id=1, source_target_pairs={{0,4},{2,6},{4,0},{6,2},{1,5},{3,7},{5,1},{7,3},{8,12},{10,14},{12... | collective-permute-start | bytes 393224 | tf_op jit(solution)/shard_map/ppermute | solution.py:36
  127.4 2.8 %collective-permute-start.7 = (bf16[2,128,256]{2,1,0:T(8,128)(2,1)S(1)}, bf16[2,128,256]{2,1,0:T(8,128)(2,1)S(1)}, u32[]{:S(2)}, u32[]{:S(2)}) collective-permute-start(bf16[2,128,256]{2,1,0:T(8,128)(2,1)S(1)} %get-tuple-element.42), channel_id=1, source_target_pairs={{0,6},{2,0},{4,2},{6,4},{1,7},{3,1},{5,3},{7,5},{8,14},{10,8},{12,... | collective-permute-start | bytes 393224 | tf_op jit(solution)/shard_map/ppermute | solution.py:36
  131.1 1.2 copy-done.4
  132.3 1.8 %forward.1 = (bf16[2,128,256]{2,1,0:T(8,128)(2,1)}, f32[8,128]{1,0:T(8,128)S(1)}) custom-call(s32[19]{0:T(128)S(1)} %concatenate.3.meta_ref, bf16[8,128,128]{2,1,0:T(8,128)(2,1)S(1)} %copy-done.1, bf16[16,128,256]{2,1,0:T(8,128)(2,1)S(1)} %bitcast.18, bf16[16,128,256]{2,1,0:T(8,128)(2,1)S(1)} %bitcast.22, bf16[256,256]{1,0:T(8,128)(2,1)S(1)} %copy-done.5), custom_call_target="tpu_custom_call" | custom-call | tf_op jit(solution)/shard_map/forward/pallas_call | solution.py:286
  134.2 2.5 %all-to-all-done.3.far_ref = bf16[16,40,128]{2,1,0:T(8,128)(2,1)S(1)} async-done(((bf16[16,40,128]{2,1,0:T(8,128)(2,1)}), bf16[16,40,128]{2,1,0:T(8,128)(2,1)S(1)}, u32[]{:S(2)}, u32[]{:S(2)}) %all-to-all-start.3) | async-done | bytes 163872 | tf_op jit(solution)/shard_map/all_to_all | solution.py:32
  137.4 11.2 %all-to-all-start.4 = ((f32[64,8,128]{2,1,0:T(8,128)}), f32[64,8,128]{2,1,0:T(8,128)S(1)}, u32[]{:S(2)}, u32[]{:S(2)}) async-start(f32[64,8,128]{2,1,0:T(8,128)} %far.1), calls=%async_computation.4 | async-start | bytes 524288 | tf_op jit(solution)/shard_map/all_to_all | solution.py:32
  150.5 7.9 %all-to-all-done.4 = f32[64,8,128]{2,1,0:T(8,128)S(1)} async-done(((f32[64,8,128]{2,1,0:T(8,128)}), f32[64,8,128]{2,1,0:T(8,128)S(1)}, u32[]{:S(2)}, u32[]{:S(2)}) %all-to-all-start.4) | async-done | bytes 262176 | tf_op jit(solution)/shard_map/all_to_all | solution.py:32
  (44 shorter events, 13.0 us)
Async XLA Ops:
  7.2 55.3 %all-gather.3.cloned.1.call-start = ((), (), s32[]{:S(2)}) async-start(), calls=%async_computation.5 | async-start | bytes 1179648 | tf_op jit(solution)/shard_map/all_gather | solution.py:253
  7.9 32.7 %copy-start.1 = (bf16[8,128,128]{2,1,0:T(8,128)(2,1)S(1)}, bf16[8,128,128]{2,1,0:T(8,128)(2,1)}, u32[]{:S(2)}) copy-start(bf16[8,128,128]{2,1,0:T(8,128)(2,1)} %tiles_ref.7) | copy-start | bytes 786436
  10.0 30.5 %copy-start.2 = (bf16[256,256]{1,0:T(8,128)(2,1)S(1)}, bf16[256,256]{1,0:T(8,128)(2,1)}, u32[]{:S(2)}) copy-start(bf16[256,256]{1,0:T(8,128)(2,1)} %param.17) | copy-start | bytes 393220
  10.0 30.5 %copy-start.3 = (bf16[16,16,256]{2,1,0:T(8,128)(2,1)S(1)}, bf16[16,16,256]{2,1,0:T(8,128)(2,1)}, u32[]{:S(2)}) copy-start(bf16[16,16,256]{2,1,0:T(8,128)(2,1)} %pick.1.token_ref) | copy-start | bytes 393220
  10.0 53.3 %all-to-all-start = ((bf16[16,16,256]{2,1,0:T(8,128)(2,1)}), bf16[16,16,256]{2,1,0:T(8,128)(2,1)S(1)}, u32[]{:S(2)}, u32[]{:S(2)}) async-start(bf16[16,16,256]{2,1,0:T(8,128)(2,1)} %pick.1.token_ref), calls=%async_computation | async-start | bytes 262144 | tf_op jit(solution)/shard_map/all_to_all | solution.py:32
  39.8 0.7 copy-start.9
  41.9 4.2 %collective-permute-start = (bf16[4,2,128,256]{3,2,1,0:T(8,128)(2,1)S(1)}, bf16[4,2,128,256]{3,2,1,0:T(8,128)(2,1)S(1)}, u32[]{:S(2)}, u32[]{:S(2)}) collective-permute-start(bf16[4,2,128,256]{3,2,1,0:T(8,128)(2,1)S(1)} %get-tuple-element.26), channel_id=1, source_target_pairs={{0,1},{1,0},{2,3},{3,2},{4,5},{5,4},{6,7},{7,6},{8,9},{9,8},{10,11... | collective-permute-start | bytes 1572872 | tf_op jit(solution)/shard_map/ppermute | solution.py:36
  46.7 16.5 %collective-permute-start.1 = (bf16[2,128,256]{2,1,0:T(8,128)(2,1)S(1)}, bf16[2,128,256]{2,1,0:T(8,128)(2,1)S(1)}, u32[]{:S(2)}, u32[]{:S(2)}) collective-permute-start(bf16[2,128,256]{2,1,0:T(8,128)(2,1)S(1)} %get-tuple-element.28), channel_id=1, source_target_pairs={{0,2},{2,4},{4,6},{6,0},{1,3},{3,5},{5,7},{7,1},{8,10},{10,12},{12... | collective-permute-start | bytes 393224 | tf_op jit(solution)/shard_map/ppermute | solution.py:36
  49.8 13.5 %collective-permute-start.2 = (bf16[2,128,256]{2,1,0:T(8,128)(2,1)S(1)}, bf16[2,128,256]{2,1,0:T(8,128)(2,1)S(1)}, u32[]{:S(2)}, u32[]{:S(2)}) collective-permute-start(bf16[2,128,256]{2,1,0:T(8,128)(2,1)S(1)} %get-tuple-element.29), channel_id=1, source_target_pairs={{0,4},{2,6},{4,0},{6,2},{1,5},{3,7},{5,1},{7,3},{8,12},{10,14},{12... | collective-permute-start | bytes 393224 | tf_op jit(solution)/shard_map/ppermute | solution.py:36
  54.9 8.4 %collective-permute-start.3 = (bf16[2,128,256]{2,1,0:T(8,128)(2,1)S(1)}, bf16[2,128,256]{2,1,0:T(8,128)(2,1)S(1)}, u32[]{:S(2)}, u32[]{:S(2)}) collective-permute-start(bf16[2,128,256]{2,1,0:T(8,128)(2,1)S(1)} %get-tuple-element.30), channel_id=1, source_target_pairs={{0,6},{2,0},{4,2},{6,4},{1,7},{3,1},{5,3},{7,5},{8,14},{10,8},{12,... | collective-permute-start | bytes 393224 | tf_op jit(solution)/shard_map/ppermute | solution.py:36
  62.5 5.3 %copy-start = (bf16[2048,256]{1,0:T(8,128)(2,1)S(1)}, bf16[2048,256]{1,0:T(8,128)(2,1)}, u32[]{:S(2)}) copy-start(bf16[2048,256]{1,0:T(8,128)(2,1)} %all-gather.3.cloned.1.call-done) | copy-start | bytes 3145732
  64.3 9.6 %all-to-all-start.1 = ((bf16[8,64,256]{2,1,0:T(8,128)(2,1)}), bf16[8,64,256]{2,1,0:T(8,128)(2,1)S(1)}, u32[]{:S(2)}, u32[]{:S(2)}) async-start(bf16[8,64,256]{2,1,0:T(8,128)(2,1)} %get-tuple-element.33), calls=%async_computation.1 | async-start | bytes 524288 | tf_op jit(solution)/shard_map/all_to_all | solution.py:32
  74.9 19.3 %all-to-all-start.2 = ((bf16[64,8,128]{2,1,0:T(8,128)(2,1)}), bf16[64,8,128]{2,1,0:T(8,128)(2,1)S(1)}, u32[]{:S(2)}, u32[]{:S(2)}) async-start(bf16[64,8,128]{2,1,0:T(8,128)(2,1)} %get-tuple-element.45), calls=%async_computation.2 | async-start | bytes 262144 | tf_op jit(solution)/shard_map/all_to_all | solution.py:32
  85.7 45.4 %all-gather.5.cloned.1.call-start = ((), (), s32[]{:S(2)}) async-start(), calls=%async_computation.6 | async-start | bytes 1179648 | tf_op jit(solution)/shard_map/all_gather | solution.py:285
  95.1 41.6 %all-to-all-start.3 = ((bf16[16,40,128]{2,1,0:T(8,128)(2,1)}), bf16[16,40,128]{2,1,0:T(8,128)(2,1)S(1)}, u32[]{:S(2)}, u32[]{:S(2)}) async-start(bf16[16,40,128]{2,1,0:T(8,128)(2,1)} %pack.1), calls=%async_computation.3 | async-start | bytes 327680 | tf_op jit(solution)/shard_map/all_to_all | solution.py:32
  115.6 4.3 %collective-permute-start.4 = (bf16[4,2,128,256]{3,2,1,0:T(8,128)(2,1)S(1)}, bf16[4,2,128,256]{3,2,1,0:T(8,128)(2,1)S(1)}, u32[]{:S(2)}, u32[]{:S(2)}) collective-permute-start(bf16[4,2,128,256]{3,2,1,0:T(8,128)(2,1)S(1)} %get-tuple-element.38), channel_id=1, source_target_pairs={{0,1},{1,0},{2,3},{3,2},{4,5},{5,4},{6,7},{7,6},{8,9},{9,8},{10,11... | collective-permute-start | bytes 1572872 | tf_op jit(solution)/shard_map/ppermute | solution.py:36
  119.9 11.2 %copy-start.5 = (bf16[256,256]{1,0:T(8,128)(2,1)S(1)}, bf16[256,256]{1,0:T(8,128)(2,1)}, u32[]{:S(2)}) copy-start(bf16[256,256]{1,0:T(8,128)(2,1)} %weight_ref.3) | copy-start | bytes 393220
  120.6 13.5 %collective-permute-start.5 = (bf16[2,128,256]{2,1,0:T(8,128)(2,1)S(1)}, bf16[2,128,256]{2,1,0:T(8,128)(2,1)S(1)}, u32[]{:S(2)}, u32[]{:S(2)}) collective-permute-start(bf16[2,128,256]{2,1,0:T(8,128)(2,1)S(1)} %get-tuple-element.40), channel_id=1, source_target_pairs={{0,2},{2,4},{4,6},{6,0},{1,3},{3,5},{5,7},{7,1},{8,10},{10,12},{12... | collective-permute-start | bytes 393224 | tf_op jit(solution)/shard_map/ppermute | solution.py:36
  123.3 10.8 %collective-permute-start.6 = (bf16[2,128,256]{2,1,0:T(8,128)(2,1)S(1)}, bf16[2,128,256]{2,1,0:T(8,128)(2,1)S(1)}, u32[]{:S(2)}, u32[]{:S(2)}) collective-permute-start(bf16[2,128,256]{2,1,0:T(8,128)(2,1)S(1)} %get-tuple-element.41), channel_id=1, source_target_pairs={{0,4},{2,6},{4,0},{6,2},{1,5},{3,7},{5,1},{7,3},{8,12},{10,14},{12... | collective-permute-start | bytes 393224 | tf_op jit(solution)/shard_map/ppermute | solution.py:36
  127.4 6.7 %collective-permute-start.7 = (bf16[2,128,256]{2,1,0:T(8,128)(2,1)S(1)}, bf16[2,128,256]{2,1,0:T(8,128)(2,1)S(1)}, u32[]{:S(2)}, u32[]{:S(2)}) collective-permute-start(bf16[2,128,256]{2,1,0:T(8,128)(2,1)S(1)} %get-tuple-element.42), channel_id=1, source_target_pairs={{0,6},{2,0},{4,2},{6,4},{1,7},{3,1},{5,3},{7,5},{8,14},{10,8},{12,... | collective-permute-start | bytes 393224 | tf_op jit(solution)/shard_map/ppermute | solution.py:36
  131.1 1.2 copy-start.4
  137.4 21.0 %all-to-all-start.4 = ((f32[64,8,128]{2,1,0:T(8,128)}), f32[64,8,128]{2,1,0:T(8,128)S(1)}, u32[]{:S(2)}, u32[]{:S(2)}) async-start(f32[64,8,128]{2,1,0:T(8,128)} %far.1), calls=%async_computation.4 | async-start | bytes 524288 | tf_op jit(solution)/shard_map/all_to_all | solution.py:32
  148.6 0.7 copy-start.6
  148.6 0.7 copy-start.7
  (1 other events, 0.7 us)
Sparse Core Ops, SparseCore 0:
  10.7 51.7 all-gather.2
  89.8 41.2 all-gather.4
